TPU v7x, 32 devices: a whole 2x2x4 slice. The times are simulated.
32 devices in a mesh: fsdp: 16 (over z, x, core), seq: 2 (over y).
Axes of the slice: x: 2, y: 2, z: 4, core: 2. Of those that a mesh axis runs over, the one named last changes fastest.
Arguments:
- tokens: bfloat16 [16, 1024, 1024], P('fsdp', 'seq'), may hold values from -6 to 6
- cotangent: bfloat16 [16, 1024, 1024], P('fsdp', 'seq'), may hold values from -6 to 6
- doc_start: int32 [16, 1024], P('fsdp', 'seq'), may hold values from 0 to 1023, as said below
- w_in: bfloat16 [1024, 4096], P('fsdp', 'seq'), may hold values from -0.1875 to 0.1875
- w_dt: bfloat16 [1024, 24], P('fsdp'), may hold values from -0.1875 to 0.1875
- w_out: bfloat16 [2048, 1024], P('fsdp', 'seq'), may hold values from -0.1875 to 0.1875
- w_gate_up: bfloat16 [1024, 4096], P('fsdp', 'seq'), may hold values from -0.1875 to 0.1875
- w_down: bfloat16 [2048, 1024], P('fsdp', 'seq'), may hold values from -0.125 to 0.125
- norm_gains: float32 [2, 1024], replicated, may hold values from 0.5 to 1.5
- conv_params: float32 [5, 1792], replicated, may hold values from -0.5 to 0.5
- ssm_gain: float32 [1536], replicated, may hold values from 0.5 to 1.5
- head_params: float32 [3, 24], replicated, as said below
Outputs:
- out: bfloat16 [16, 1024, 1024], P('fsdp', 'seq')
- d_tokens: float32 [16, 1024, 1024], P('fsdp', 'seq')
- g_w_in: float32 [1024, 4096], P('fsdp', 'seq')
- g_w_dt: float32 [1024, 24], P('fsdp')
- g_w_out: float32 [2048, 1024], P('fsdp', 'seq')
- g_w_gate_up: float32 [1024, 4096], P('fsdp', 'seq')
- g_w_down: float32 [2048, 1024], P('fsdp', 'seq')
- g_norm_gains: float32 [2, 1024], replicated
- g_conv_params: float32 [5, 1792], replicated
- g_ssm_gain: float32 [1536], replicated
- g_head_params: float32 [3, 24], replicated
Inputs may be any that keep to these rules, and one draw needn't show every extreme that they name: `doc_start`: each row of 1024 positions holds documents laid end to end; a position's value is the first position of its document; the first document begins at 0; a middle document begins before position 512 and ends after position 512; in some row the last document is the final position alone. `head_params`: row 0 holds each head's log decay rate, row 1 its step-size bias, row 2 its skip coefficient.
All inputs are finite; a program needn't handle non-finite values.
Results may differ from a plain program's by a relative error of at most 0.017.
Values may be sent and summed in bfloat16 or wider, within the bound.
A program may use at most 256 MiB of HBM per device.

v0:
```python
from functools import partial

import jax
import jax.numpy as jnp
from jax import lax
from jax.sharding import PartitionSpec as P

FF = 2048
HEADS = 8
KV_HEADS = 2
HEAD_DIM = 64
SSM_HEADS = 24
SSM_DIM = 64
STATE = 128
CONV = 4
D_SSM = 1536
XBC = 1792


EPSILON = 1e-05
PRECISE = lax.Precision.HIGHEST


def passed_along(block, axis, distance):
    devices = range(lax.axis_size(axis))
    route = [(i - distance, i) for i in devices if i - distance in devices]
    return lax.ppermute(block, axis, route)


def entering_2(array, axis, combine, identity):
    devices, index = (lax.axis_size(axis), lax.axis_index(axis))
    everything = jax.tree.map(
        lambda part, kind: lax.all_gather(part.astype(kind), axis),
        array,
        (jnp.bfloat16, jnp.bfloat16),
    )
    start = jax.tree.map(
        lambda part, zero: jnp.broadcast_to(jnp.asarray(zero, part.dtype), part.shape),
        array,
        identity,
    )

    def lap(k, before):
        reached = k < index
        new = combine(
            before, jax.tree.map(lambda part, own: part[k].astype(own.dtype), everything, array)
        )
        return jax.tree.map(lambda a, b: jnp.where(reached, a, b), new, before)

    return lax.fori_loop(0, devices, lap, start)


def prefix_2(array, axis, join, neutral):
    count = lax.axis_size(axis)
    place = lax.axis_index(axis)
    ahead = count - 1 - place
    gathered = jax.tree.map(
        lambda a, kind: lax.all_gather(a.astype(kind), axis),
        array,
        jax.tree.map(lambda a: jnp.bfloat16 if a.dtype == jnp.float32 else a.dtype, array),
    )
    state = jax.tree.map(lambda a, e: jnp.zeros_like(a) + jnp.asarray(e, a.dtype), array, neutral)

    def one(lap, state):
        source = count - 1 - lap
        return join(
            state,
            jax.tree.map(
                lambda a, own: lax.dynamic_index_in_dim(a, source, 0, False).astype(own.dtype),
                gathered,
                array,
            ),
        )

    return lax.fori_loop(0, ahead, one, state)


def rms_norm(values, gain):
    return values * lax.rsqrt(jnp.mean(values * values, axis=-1, keepdims=True) + EPSILON) * gain


def swiglu(paired):
    return jax.nn.silu(paired[:, :FF]) * paired[:, FF:]


def times_rows(left, weight):
    return lax.dot_general(
        left, weight, (((1,), (1,)), ((), ())), preferred_element_type=jnp.float32
    )


def outer_total(left, right):
    return lax.dot_general(
        left, right, (((0,), (0,)), ((), ())), preferred_element_type=jnp.float32
    )


def conv_pieces(extended, conv_params, dt_raw, head_params, valid):
    length = dt_raw.shape[1]
    summed = conv_params[CONV] + jnp.zeros((extended.shape[0], length, XBC), jnp.float32)
    for lagged in range(CONV):
        offset = CONV - 1 - lagged
        summed = (
            summed
            + conv_params[lagged]
            * extended[:, offset : offset + length, :]
            * valid[lagged][..., None]
        )
    activated = jax.nn.silu(summed)
    inputs = activated[..., :D_SSM].reshape(activated.shape[0], length, SSM_HEADS, SSM_DIM)
    b_proj = activated[..., D_SSM : D_SSM + STATE]
    c_proj = activated[..., D_SSM + STATE :]
    step_size = jax.nn.softplus(dt_raw + head_params[1])
    cumul = jnp.cumsum(-jnp.exp(head_params[0]) * step_size, axis=1)
    return (inputs, b_proj, c_proj, step_size, cumul)


def block_summary(inputs, b_proj, step_size, cumul, tail_mask, alive):
    final = cumul[:, -1, :]
    decay = jnp.exp(final) * alive[:, None]
    weights = jnp.exp(final[:, None, :] - cumul) * step_size * tail_mask[..., None]
    state = jnp.einsum("sph,sphd,spn->shdn", weights, inputs, b_proj, precision=PRECISE)
    return (decay, state)


def block_output(
    inputs,
    b_proj,
    c_proj,
    step_size,
    cumul,
    head_params,
    entering,
    gate_in,
    ssm_gain,
    inner_mask,
    carry_mask,
):
    gram = jnp.einsum("stn,srn->str", c_proj, b_proj, precision=PRECISE)
    spread = cumul[:, :, None, :] - cumul[:, None, :, :]
    decays = jnp.exp(jnp.where(inner_mask[..., None], spread, -1e30))
    weights = decays * (gram[..., None] * step_size[:, None, :, :])
    within = jnp.einsum("strh,srhd->sthd", weights, inputs, precision=PRECISE)
    entry = jnp.exp(cumul) * carry_mask[..., None]
    incoming = jnp.einsum("sth,shdn,stn->sthd", entry, entering, c_proj, precision=PRECISE)
    output = within + incoming + head_params[2][:, None] * inputs
    output = output.reshape(output.shape[0], output.shape[1], D_SSM) * jax.nn.silu(gate_in)
    return rms_norm(output, ssm_gain)


def join_states(earlier, later):
    return (earlier[0] * later[0], later[0][:, :, None, None] * earlier[1] + later[1])


def join_grads(earlier, later):
    return (later[0] * earlier[0], later[1] + later[0][:, :, None, None] * earlier[1])


def body(
    tokens,
    cotangent,
    doc_start,
    w_in,
    w_dt,
    w_out,
    w_gate_up,
    w_down,
    norm_gains,
    conv_params,
    ssm_gain,
    head_params,
):
    num_seqs, span_len, model_width = tokens.shape
    num_rows = num_seqs * span_len
    block_start = lax.axis_index("seq") * span_len
    q_width = HEADS * HEAD_DIM
    kv_width = KV_HEADS * HEAD_DIM
    head_share = HEADS // KV_HEADS
    att_scale = HEAD_DIM ** (-0.5)
    rim_len = CONV - 1
    base_col = q_width + 2 * kv_width
    dt_rows = w_dt.shape[0]
    cols_in, cols_out, cols_gu, cols_down = (
        lax.all_gather(w_in, "seq", axis=1, tiled=True),
        lax.all_gather(w_out, "seq", axis=1, tiled=True),
        lax.all_gather(w_gate_up, "seq", axis=1, tiled=True),
        lax.all_gather(w_down, "seq", axis=1, tiled=True),
    )
    full_in, full_dt, full_out, full_gu, full_down = (
        lax.all_gather(cols_in, "fsdp", axis=0, tiled=True),
        lax.all_gather(w_dt, "fsdp", axis=0, tiled=True),
        lax.all_gather(cols_out, "fsdp", axis=0, tiled=True),
        lax.all_gather(cols_gu, "fsdp", axis=0, tiled=True),
        lax.all_gather(cols_down, "fsdp", axis=0, tiled=True),
    )
    hidden = tokens.reshape(num_rows, model_width).astype(jnp.float32)
    normed_f, norm1_back = jax.vjp(rms_norm, hidden, norm_gains[0])
    normed = normed_f.astype(jnp.bfloat16)
    projected = jnp.dot(normed, full_in, preferred_element_type=jnp.float32).astype(jnp.bfloat16)
    dt_raw = jnp.dot(normed, full_dt, preferred_element_type=jnp.float32)
    queries = projected[:, :q_width].reshape(num_rows, KV_HEADS, head_share, HEAD_DIM)
    kv_all = lax.all_gather(projected[:, q_width:base_col], "seq", axis=0, tiled=True)
    total_keys = kv_all.shape[0]
    keys_all = kv_all[:, :kv_width].reshape(total_keys, KV_HEADS, HEAD_DIM)
    values_all = kv_all[:, kv_width:].reshape(total_keys, KV_HEADS, HEAD_DIM)
    row_index = jnp.arange(num_rows, dtype=jnp.int32)
    q_seq = row_index // span_len
    q_pos = block_start + row_index % span_len
    row_starts = doc_start.reshape(num_rows)
    key_index = jnp.arange(total_keys, dtype=jnp.int32)
    key_within = key_index % num_rows
    k_seq = key_within // span_len
    k_pos = key_index // num_rows * span_len + key_within % span_len
    allowed = (
        (k_seq[None, :] == q_seq[:, None])
        & (k_pos[None, :] <= q_pos[:, None])
        & (k_pos[None, :] >= row_starts[:, None])
    )
    scores = (
        jnp.einsum("tkgd,ckd->kgtc", queries, keys_all, preferred_element_type=jnp.float32)
        * att_scale
    )
    scores = jnp.where(allowed, scores, -1e30)
    row_max = jnp.max(scores, axis=-1, keepdims=True)
    shifted = jnp.exp(scores - row_max)
    attn_probs = shifted / jnp.sum(shifted, axis=-1, keepdims=True)
    probs_low = attn_probs.astype(jnp.bfloat16)
    attended = (
        jnp.einsum("kgtc,ckd->tkgd", probs_low, values_all, preferred_element_type=jnp.float32)
        .reshape(num_rows, q_width)
        .astype(jnp.bfloat16)
    )
    gate_in = (
        projected[:, base_col : base_col + D_SSM]
        .astype(jnp.float32)
        .reshape(num_seqs, span_len, D_SSM)
    )
    conv_in = projected[:, base_col + D_SSM :].reshape(num_seqs, span_len, XBC)
    before = passed_along(conv_in[:, span_len - rim_len :, :], "seq", 1)
    extended = jnp.concatenate([before, conv_in], axis=1).astype(jnp.float32)
    positions = block_start + jnp.arange(span_len, dtype=jnp.int32)
    valid = jnp.stack([positions[None, :] - lagged >= doc_start for lagged in range(CONV)]).astype(
        jnp.float32
    )
    pieces, pieces_back = jax.vjp(
        partial(conv_pieces, valid=valid),
        extended,
        conv_params,
        dt_raw.reshape(num_seqs, span_len, SSM_HEADS),
        head_params,
    )
    inputs, b_proj, c_proj, step_size, cumul = pieces
    tail_mask = (positions[None, :] >= doc_start[:, -1:]).astype(jnp.float32)
    alive_mask = (doc_start[:, -1] < block_start).astype(jnp.float32)
    summary, summary_back = jax.vjp(
        partial(block_summary, tail_mask=tail_mask, alive=alive_mask),
        inputs,
        b_proj,
        step_size,
        cumul,
    )
    unit_decay = jnp.ones_like(summary[0])
    empty_state = jnp.zeros_like(summary[1])
    prefix = entering_2((summary[0], summary[1]), "seq", join_states, (unit_decay, empty_state))
    entering = prefix[1]
    inner_mask = (positions[None, None, :] <= positions[None, :, None]) & (
        positions[None, None, :] >= doc_start[:, :, None]
    )
    carry_mask = (doc_start < block_start).astype(jnp.float32)
    mamba_f, output_back = jax.vjp(
        partial(block_output, inner_mask=inner_mask, carry_mask=carry_mask),
        inputs,
        b_proj,
        c_proj,
        step_size,
        cumul,
        head_params,
        entering,
        gate_in,
        ssm_gain,
    )
    mamba_low = mamba_f.reshape(num_rows, D_SSM).astype(jnp.bfloat16)
    mixed_in = jnp.concatenate([attended, mamba_low], axis=1)
    second = hidden + jnp.dot(mixed_in, full_out, preferred_element_type=jnp.float32)
    normed2_f, norm2_back = jax.vjp(rms_norm, second, norm_gains[1])
    normed2 = normed2_f.astype(jnp.bfloat16)
    paired = jnp.dot(normed2, full_gu, preferred_element_type=jnp.float32)
    activ_f, activ_back = jax.vjp(swiglu, paired)
    activ = activ_f.astype(jnp.bfloat16)
    result = second + jnp.dot(activ, full_down, preferred_element_type=jnp.float32)
    upstream = cotangent.reshape(num_rows, model_width)
    grad_down = outer_total(activ, upstream)
    d_activ = times_rows(upstream, full_down)
    d_paired = activ_back(d_activ)[0].astype(jnp.bfloat16)
    grad_gu = outer_total(normed2, d_paired)
    d_normed2 = times_rows(d_paired, full_gu)
    d_second, d_gain2 = norm2_back(d_normed2)
    d_second = d_second + upstream.astype(jnp.float32)
    d_mixed = d_second.astype(jnp.bfloat16)
    grad_out = outer_total(mixed_in, d_mixed)
    d_mixed_in = times_rows(d_mixed, full_out)
    d_attended = (
        d_mixed_in[:, :q_width]
        .astype(jnp.bfloat16)
        .reshape(num_rows, KV_HEADS, head_share, HEAD_DIM)
    )
    d_mamba = d_mixed_in[:, q_width:].reshape(num_seqs, span_len, D_SSM)
    d_probs = jnp.einsum(
        "tkgd,ckd->kgtc", d_attended, values_all, preferred_element_type=jnp.float32
    )
    centre = jnp.sum(attn_probs * d_probs, axis=-1, keepdims=True)
    d_scores = (attn_probs * (d_probs - centre)).astype(jnp.bfloat16)
    d_queries = (
        jnp.einsum("kgtc,ckd->tkgd", d_scores, keys_all, preferred_element_type=jnp.float32)
        * att_scale
    ).reshape(num_rows, q_width)
    d_keys = (
        jnp.einsum("kgtc,tkgd->ckd", d_scores, queries, preferred_element_type=jnp.float32)
        * att_scale
    )
    d_values = jnp.einsum(
        "kgtc,tkgd->ckd", probs_low, d_attended, preferred_element_type=jnp.float32
    )
    d_kv = lax.psum_scatter(
        jnp.concatenate(
            [
                d_keys.reshape(num_rows * lax.axis_size("seq"), kv_width),
                d_values.reshape(num_rows * lax.axis_size("seq"), kv_width),
            ],
            axis=1,
        ).astype(jnp.bfloat16),
        "seq",
        scatter_dimension=0,
        tiled=True,
    ).astype(jnp.float32)
    g_inputs, g_bproj, g_cproj, g_step, g_cumul, g_head_out, g_entering, g_gate, g_ssm = (
        output_back(d_mamba)
    )
    ahead = prefix_2((summary[0], g_entering), "seq", join_grads, (unit_decay, empty_state))
    state_grad = ahead[1]
    d_decay = jnp.sum(state_grad * entering, axis=(2, 3))
    s_inputs, s_bproj, s_step, s_cumul = summary_back((d_decay, state_grad))
    d_extended, g_conv, d_dt_raw, g_head_in = pieces_back(
        (g_inputs + s_inputs, g_bproj + s_bproj, g_cproj, g_step + s_step, g_cumul + s_cumul)
    )
    from_next = passed_along(d_extended[:, :rim_len, :], "seq", -1)
    d_conv_in = d_extended[:, rim_len:, :] + jnp.pad(
        from_next, ((0, 0), (span_len - rim_len, 0), (0, 0))
    )
    d_projected = jnp.concatenate(
        [d_queries, d_kv, g_gate.reshape(num_rows, D_SSM), d_conv_in.reshape(num_rows, XBC)], axis=1
    ).astype(jnp.bfloat16)
    d_dt_low = d_dt_raw.reshape(num_rows, SSM_HEADS).astype(jnp.bfloat16)
    grad_in = outer_total(normed, d_projected)
    grad_dt = outer_total(normed, d_dt_low)
    d_normed = times_rows(d_projected, full_in) + times_rows(d_dt_low, full_dt)
    d_hidden, d_gain1 = norm1_back(d_normed)
    d_hidden = d_hidden + d_second
    part_in, part_out, part_gu, part_down = (
        lax.psum_scatter(
            grad_in.astype(jnp.bfloat16), "seq", scatter_dimension=1, tiled=True
        ).astype(jnp.float32),
        lax.psum_scatter(
            grad_out.astype(jnp.bfloat16), "seq", scatter_dimension=1, tiled=True
        ).astype(jnp.float32),
        lax.psum_scatter(
            grad_gu.astype(jnp.bfloat16), "seq", scatter_dimension=1, tiled=True
        ).astype(jnp.float32),
        lax.psum_scatter(
            grad_down.astype(jnp.bfloat16), "seq", scatter_dimension=1, tiled=True
        ).astype(jnp.float32),
    )
    shard_in, shard_out, shard_gu, shard_down = (
        lax.psum_scatter(
            part_in.astype(jnp.bfloat16), "fsdp", scatter_dimension=0, tiled=True
        ).astype(jnp.float32),
        lax.psum_scatter(
            part_out.astype(jnp.bfloat16), "fsdp", scatter_dimension=0, tiled=True
        ).astype(jnp.float32),
        lax.psum_scatter(
            part_gu.astype(jnp.bfloat16), "fsdp", scatter_dimension=0, tiled=True
        ).astype(jnp.float32),
        lax.psum_scatter(
            part_down.astype(jnp.bfloat16), "fsdp", scatter_dimension=0, tiled=True
        ).astype(jnp.float32),
    )
    summed_small = lax.psum(
        (jnp.stack([d_gain1, d_gain2]), g_conv, g_ssm, g_head_out + g_head_in, grad_dt),
        ("fsdp", "seq"),
    )
    shard_dt = lax.dynamic_slice_in_dim(
        summed_small[4], lax.axis_index("fsdp") * dt_rows, dt_rows, 0
    )
    return (
        result.reshape(num_seqs, span_len, model_width).astype(jnp.bfloat16),
        d_hidden.reshape(num_seqs, span_len, model_width),
        shard_in,
        shard_dt,
        shard_out,
        shard_gu,
        shard_down,
        summed_small[0],
        summed_small[1],
        summed_small[2],
        summed_small[3],
    )


def solution(mesh):
    placed = (
        P("fsdp", "seq", None),
        P("fsdp", "seq", None),
        P("fsdp", "seq"),
        P("fsdp", "seq"),
        P("fsdp", None),
        P("fsdp", "seq"),
        P("fsdp", "seq"),
        P("fsdp", "seq"),
        P(),
        P(),
        P(),
        P(),
    )
    return jax.shard_map(
        body,
        mesh=mesh,
        in_specs=placed,
        out_specs=(
            P("fsdp", "seq", None),
            P("fsdp", "seq", None),
            P("fsdp", "seq"),
            P("fsdp", None),
            P("fsdp", "seq"),
            P("fsdp", "seq"),
            P("fsdp", "seq"),
            P(),
            P(),
            P(),
            P(),
        ),
        check_vma=False,
    )
```

profile of v0, /device:TPU:0, one launch (start us, length us, event | category | flops | bytes accessed | tf_op | source)
XLA Modules:
  0.0 1102.0 jit_solution(13682560005312031061)
XLA Ops:
  7.3 12.0 %all_gather.48 = bf16[64,4096]{1,0:T(8,128)(2,1)} all-gather(bf16[64,2048]{1,0:T(8,128)(2,1)} %param.19), channel_id=1, replica_groups=mesh['fsdp'=16,'seq'=2] {'seq'}, dimensions={1}, use_global_device_ids=true | all-gather | bytes 786432 | tf_op jit(solution)/shard_map/all_gather | solution.py:184
  19.4 6.0 all_gather.55
  25.4 9.0 all_gather.57
  34.5 6.0 all_gather.59
  42.0 22.4 %all-gather.2 = bf16[16,64,24]{1,2,0:T(8,128)(2,1)S(1)} all-gather(bf16[1,64,24]{1,2,0:T(8,128)(2,1)S(1)} %bitcast.490), channel_id=1, replica_groups=mesh['fsdp'=16,'seq'=2] {'fsdp'}, dimensions={0}, use_global_device_ids=true | all-gather | bytes 52224 | tf_op jit(solution)/shard_map/all_gather | solution.py:191
  70.0 4.2 all_gather.52
  79.0 15.9 %all-gather.8.cloned.1.call-done = bf16[1024,4096]{1,0:T(8,128)(2,1)} async-done(((bf16[64,4096]{1,0:T(8,128)(2,1)}), bf16[1024,4096]{1,0:T(8,128)(2,1)}) %all-gather.8.cloned.1.call-update) | async-done | bytes 8388624 | tf_op jit(solution)/shard_map/all_gather | solution.py:190
  94.9 8.2 convolution_convert_fusion.2
  106.6 4.0 collective-permute-start
  110.6 9.1 all_gather.50
  123.9 10.5 fusion.207
  134.4 7.5 fusion.83
  144.2 5.2 fusion.37
  153.3 3.7 copy.198
  157.1 4.5 fusion.86
  161.6 10.7 all-gather
  174.8 3.9 fusion.123
  178.8 29.9 %fusion.45 = f32[1,512,24,64]{1,3,2,0:T(8,128)} fusion(f32[1,512,24,64]{1,3,2,0:T(8,128)S(1)} %bitcast.430, f32[512,24,64]{0,2,1:T(8,128)S(1)} %fusion.123, f32[512,24,64]{0,2,1:T(8,128)S(1)} %bitcast.431, f32[512,24]{0,1:T(8,128)S(1)} %copy-done.63, f32[512,512]{1,0:T(8,128)S(1)} %fusion.145, f32[512,24]{0,1:T(8,128)S(1)} %copy-done.61, ...), kind=kOutput, calls=%fused_computation.90 | convolution fusion | flops 4860149760 | bytes 14041184 | tf_op jit(solution)/shard_map/jvp(strh,srhd->sthd)/dot_general | solution.py:143
  208.7 3.9 copy.210
  212.6 3.8 multiply_reduce_fusion.9
  217.8 6.9 multiply_reduce_fusion.12
  224.8 11.8 %fusion.195 = f32[512,4096]{1,0:T(8,128)} fusion(bf16[1024,4096]{1,0:T(8,128)(2,1)} %all-gather.12.cloned.1.call-done, f32[512,1024]{1,0:T(8,128)} %get-tuple-element.356, f32[1024]{0:T(1024)S(1)} %bitcast.484, f32[512]{0:T(512)S(1)} %fusion.182), kind=kOutput, calls=%fused_computation.323 | convolution fusion | flops 4296540160 | bytes 18880512 | tf_op jit(solution)/shard_map/dot_general | solution.py:287
  236.6 35.9 %all-gather.14.cloned.1.call-done = bf16[2048,1024]{1,0:T(8,128)(2,1)} async-done(((bf16[128,1024]{1,0:T(8,128)(2,1)}), bf16[2048,1024]{1,0:T(8,128)(2,1)}) %all-gather.14.cloned.1.call-update) | async-done | bytes 4194320 | tf_op jit(solution)/shard_map/all_gather | solution.py:194
  272.5 12.7 %fusion.129 = (f32[512,2048]{1,0:T(8,128)}, f32[512,2048]{1,0:T(8,128)}, bf16[512,2048]{1,0:T(8,128)(2,1)}) fusion(f32[512,4096]{1,0:T(8,128)} %fusion.195, bf16[2048,1024]{1,0:T(8,128)(2,1)} %all-gather.14.cloned.1.call-done, bf16[1,512,1024]{2,1,0:T(8,128)(2,1)} %param.17), kind=kOutput, calls=%fused_computation.191 | convolution fusion | flops 2162163712 | bytes 24117248 | tf_op jit(solution)/shard_map/dot_general | solution.py:87
  285.3 10.7 multiply_reduce_fusion.10
  305.6 13.2 %fusion.6 = (f32[2,4,512]{2,1,0:T(4,128)S(1)}, f32[2,1024,512,4]{2,1,3,0:T(8,128)}) fusion(f32[2,4,512,1024]{2,3,1,0:T(8,128)} %get-tuple-element.354, f32[2,4,512]{2,1,0:T(4,128)S(1)} %copy-done.90, bf16[1024,2,64,1]{0,2,3,1:T(8,128)(2,1)S(1)} %bitcast.460, bf16[512,2,4,64]{0,3,2,1:T(8,128)(2,1)} %bitcast.455), kind=kOutput, calls=%fused_computation.18 | convolution fusion | flops 549449728 | bytes 34373632 | tf_op jit(solution)/shard_map/tkgd,ckd->kgtc/dot_general | solution.py:308
  318.7 10.2 fusion.96
  329.0 7.8 fusion.8
  336.7 4.1 fusion.99
  345.1 6.7 convolution_convert_fusion.4
  351.8 6.3 convolution_convert_fusion.3
  358.1 12.0 %convolution_convert_fusion = bf16[1024,4096]{1,0:T(8,128)(2,1)} fusion(f32[512,2048]{1,0:T(8,128)} %get-tuple-element.325, f32[512,2048]{1,0:T(8,128)} %get-tuple-element.324, f32[512,1024]{1,0:T(8,128)} %get-tuple-element.356, f32[1024]{0:T(1024)S(1)} %bitcast.487, f32[512]{0:T(512)S(1)} %fusion.182), kind=kOutput, calls=%fused_computation.43 | convolution fusion | flops 4304928768 | bytes 18880512 | tf_op jit(solution)/shard_map/dot_general | solution.py:93
  370.4 3.4 multiply_reduce_fusion.7
  373.8 5.4 fusion.46
  379.2 3.5 copy.219
  382.8 4.5 fusion.89
  387.3 21.0 %all-gather.1 = bf16[48,64,128]{2,1,0:T(8,128)(2,1)} all-gather(bf16[24,64,128]{2,1,0:T(8,128)(2,1)S(1)} %fusion.89), channel_id=3, replica_groups=mesh['fsdp'=16,'seq'=2] {'seq'}, dimensions={0}, use_global_device_ids=true | all-gather | bytes 1179648 | tf_op jit(solution)/shard_map/all_gather | solution.py:58
  411.6 5.2 fusion.48
  416.9 23.3 %fusion.44 = f32[1,512,24,64]{1,3,2,0:T(8,128)} fusion(f32[24,64,512]{2,1,0:T(8,128)S(1)} %get-tuple-element.359, f32[1,512,24,64]{1,3,2,0:T(8,128)S(1)} %bitcast.437, f32[24,64,512]{2,1,0:T(8,128)S(1)} %bitcast.436, f32[512,24]{0,1:T(8,128)S(1)} %copy-done.64, f32[512,512]{1,0:T(8,128)S(1)} %copy-done.37, f32[512,24]{0,1:T(8,128)S(1)} %copy-done.62, ...), kind=kOutput, calls=%fused_computation.88 | convolution fusion | flops 4860149760 | bytes 14041184 | tf_op jit(solution)/shard_map/transpose(jvp(strh,srhd->sthd))/dot_general | solution.py:143
  440.2 3.6 copy.226
  443.8 37.7 %fusion.10 = (f32[512,24]{0,1:T(8,128)}, f32[512,24]{0,1:T(8,128)}, f32[512,24]{0,1:T(8,128)}, f32[512,512]{1,0:T(8,128)S(1)}) fusion(f32[512,512]{1,0:T(8,128)} %copy-done.36, f32[512,24]{0,1:T(8,128)} %copy.205, f32[512,24]{0,1:T(8,128)} %copy.203, pred[512,512]{1,0:T(8,128)(4,1)S(1)} %copy-done.43, f32[24,64,512]{2,1,0:T(8,128)} %bitcast.434, ...), kind=kOutput, calls=%fused_computation.24 | convolution fusion | flops 4913328128 | bytes 8896512 | tf_op jit(solution)/shard_map/transpose(jvp(strh,srhd->sthd))/dot_general | solution.py:143
  481.5 2.9 convolution_bitcast_fusion.1
  484.4 5.1 fusion.106
  491.7 5.3 fusion.103
  497.1 5.8 multiply_reduce_fusion.5
  503.0 3.1 multiply_multiply_fusion.6
  507.8 2.4 fusion.82
  510.2 4.3 fusion.43
  514.6 2.9 pad_add_fusion
  517.7 2.6 fusion.75
  520.4 10.0 convolution_convert_fusion.1
  530.8 4.1 multiply_reduce_fusion.6
  541.2 5.0 reduce-window.16
  550.1 31.6 %reduce-scatter.20.cloned.1.call-done = bf16[1024,2048]{1,0:T(8,128)(2,1)} async-done(((bf16[1024,4096]{1,0:T(8,128)(2,1)}), bf16[1024,2048]{1,0:T(8,128)(2,1)}) %reduce-scatter.20.cloned.1.call-update) | async-done | bytes 4194320 | tf_op jit(solution)/shard_map/reduce_scatter | solution.py:366
  581.9 101.5 %reduce-scatter.12.cloned.1.call-done = bf16[1024,2048]{1,0:T(8,128)(2,1)} async-done(((bf16[1024,4096]{1,0:T(8,128)(2,1)}), bf16[1024,2048]{1,0:T(8,128)(2,1)}) %reduce-scatter.12.cloned.1.call-update) | async-done | bytes 4194320 | tf_op jit(solution)/shard_map/reduce_scatter | solution.py:360
  686.2 6.1 fusion.81
  692.4 118.5 %all-reduce.22.cloned.1.call-done = f32[1024,24]{0,1:T(8,128)} async-done(((f32[1024,24]{0,1:T(8,128)}), f32[1024,24]{0,1:T(8,128)}) %all-reduce.22.cloned.1.call-update) | async-done | bytes 98320 | tf_op jit(solution)/shard_map/psum | solution.py:387
  812.3 10.7 fusion.65
  822.9 43.1 %all-reduce.19 = (f32[2,1024]{1,0:T(2,128)}, f32[5,1792]{1,0:T(8,128)}, f32[1536]{0:T(1024)}, f32[3,24]{1,0:T(4,128)}) all-reduce(f32[2,1024]{1,0:T(2,128)S(1)} %pad_maximum_fusion.7, f32[5,1792]{1,0:T(8,128)S(1)} %pad_add_fusion.1, f32[1536]{0:T(1024)S(1)} %copy-done.74, ...), channel_id=1, replica_groups=mesh['fsdp'=16,'seq'=2] {'fsdp','seq'}, use_global_device_ids=true, to_apply=%region_35.36 | all-reduce | flops 12616 | bytes 100928 | tf_op jit(solution)/shard_map/psum | solution.py:387
  866.1 3.4 fusion.72
  869.5 8.0 reduce-scatter.18.cloned.1.call-done
  879.2 62.6 %reduce-scatter.26.cloned.1.call-done = bf16[128,512]{1,0:T(8,128)(2,1)} async-done(((bf16[2048,512]{1,0:T(8,128)(2,1)}), bf16[128,512]{1,0:T(8,128)(2,1)}) %reduce-scatter.26.cloned.1.call-update) | async-done | bytes 131088 | tf_op jit(solution)/shard_map/reduce_scatter | solution.py:383
  943.5 74.2 %reduce-scatter.22.cloned.1.call-done = bf16[64,2048]{1,0:T(8,128)(2,1)} async-done(((bf16[1024,2048]{1,0:T(8,128)(2,1)}), bf16[64,2048]{1,0:T(8,128)(2,1)}) %reduce-scatter.22.cloned.1.call-update) | async-done | bytes 262160 | tf_op jit(solution)/shard_map/reduce_scatter | solution.py:380
  1019.5 73.8 %reduce-scatter.14.cloned.1.call-done = bf16[64,2048]{1,0:T(8,128)(2,1)} async-done(((bf16[1024,2048]{1,0:T(8,128)(2,1)}), bf16[64,2048]{1,0:T(8,128)(2,1)}) %reduce-scatter.14.cloned.1.call-update) | async-done | bytes 262160 | tf_op jit(solution)/shard_map/reduce_scatter | solution.py:374
  (370 shorter events, 74.6 us)
Async XLA Ops:
  7.2 33.4 %copy-start.100 = (f32[2,1024]{1,0:T(2,128)S(1)}, f32[2,1024]{1,0:T(2,128)}, u32[]{:S(2)}) copy-start(f32[2,1024]{1,0:T(2,128)} %param.24) | copy-start | bytes 24580
  7.2 34.0 %copy-start.27 = (bf16[1,512,1024]{2,1,0:T(8,128)(2,1)S(1)}, bf16[1,512,1024]{2,1,0:T(8,128)(2,1)}, u32[]{:S(2)}) copy-start(bf16[1,512,1024]{2,1,0:T(8,128)(2,1)} %param.16) | copy-start | bytes 3145732
  7.2 34.3 %copy-start.104 = (f32[3,24]{1,0:T(4,128)S(1)}, f32[3,24]{1,0:T(4,128)}, u32[]{:S(2)}) copy-start(f32[3,24]{1,0:T(4,128)} %param.27) | copy-start | bytes 868
  7.2 34.8 %copy-start.101 = (bf16[64,24]{0,1:T(8,128)(2,1)S(1)}, bf16[64,24]{0,1:T(8,128)(2,1)}, u32[]{:S(2)}) copy-start(bf16[64,24]{0,1:T(8,128)(2,1)} %param.20) | copy-start | bytes 9220
  7.2 87.6 %all-gather.8.cloned.1.call-start = ((), (), s32[]{:S(2)}) async-start(), calls=%async_computation.9 | async-start | bytes 8912896 | tf_op jit(solution)/shard_map/all_gather | solution.py:190
  19.3 198.5 %all-gather.10.cloned.1.call-start = ((), (), s32[]{:S(2)}) async-start(), calls=%async_computation.10 | async-start | bytes 4456448 | tf_op jit(solution)/shard_map/all_gather | solution.py:192
  25.3 41.4 %copy-start.83 = (s32[1,512]{1,0:T(1,128)S(1)}, s32[1,512]{1,0:T(1,128)}, u32[]{:S(2)}) copy-start(s32[1,512]{1,0:T(1,128)} %param.18) | copy-start | bytes 6148
  25.4 42.1 %copy-start.82 = (f32[5,1792]{1,0:T(8,128)S(1)}, f32[5,1792]{1,0:T(8,128)}, u32[]{:S(2)}) copy-start(f32[5,1792]{1,0:T(8,128)} %param.25) | copy-start | bytes 107524
  25.4 199.4 %all-gather.12.cloned.1.call-start = ((), (), s32[]{:S(2)}) async-start(), calls=%async_computation.11 | async-start | bytes 8912896 | tf_op jit(solution)/shard_map/all_gather | solution.py:193
  34.5 238.0 %all-gather.14.cloned.1.call-start = ((), (), s32[]{:S(2)}) async-start(), calls=%async_computation.12 | async-start | bytes 4456448 | tf_op jit(solution)/shard_map/all_gather | solution.py:194
  40.5 479.9 %reduce-scatter.10.cloned.1.call-start = ((), (), s32[]{:S(2)}) async-start(), calls=%async_computation.13 | async-start | bytes 786432 | tf_op jit(solution)/shard_map/reduce_scatter | solution.py:324
  41.2 53.7 %copy-start.91 = (f32[1,1024]{1,0:T(1,128)}, f32[1,1024]{1,0:T(1,128)S(1)}, u32[]{:S(2)}) copy-start(f32[1,1024]{1,0:T(1,128)S(1)} %get-tuple-element.339) | copy-start | bytes 12292
  41.5 23.1 %copy-start.88 = (f32[512]{0:T(512)}, f32[512]{0:T(512)S(1)}, u32[]{:S(2)}) copy-start(f32[512]{0:T(512)S(1)} %fusion.66) | copy-start | bytes 6148
  41.5 53.4 %copy-start.97 = (f32[512]{0:T(512)}, f32[512]{0:T(512)S(1)}, u32[]{:S(2)}) copy-start(f32[512]{0:T(512)S(1)} %fusion.180) | copy-start | bytes 6148
  42.0 25.3 %copy-start.103 = (f32[24]{0:T(128)}, f32[24]{0:T(128)S(1)}, u32[]{:S(2)}) copy-start(f32[24]{0:T(128)S(1)} %get-tuple-element.345) | copy-start | bytes 292
  65.1 29.7 %copy-start.25 = (f32[512,24]{1,0:T(8,128)}, f32[512,24]{1,0:T(8,128)S(1)}, u32[]{:S(2)}) copy-start(f32[512,24]{1,0:T(8,128)S(1)} %get-tuple-element.352) | copy-start | bytes 147460
  67.4 35.8 %copy-start.84 = (f32[1,512]{1,0:T(1,128)}, f32[1,512]{1,0:T(1,128)S(1)}, u32[]{:S(2)}) copy-start(f32[1,512]{1,0:T(1,128)S(1)} %get-tuple-element.347) | copy-start | bytes 6148
  67.4 76.6 %copy-start.66 = (f32[1,1,512]{2,0,1:T(1,128)}, f32[1,1,512]{2,0,1:T(1,128)S(1)}, u32[]{:S(2)}) copy-start(f32[1,1,512]{2,0,1:T(1,128)S(1)} %get-tuple-element.340) | copy-start | bytes 6148
  67.5 76.6 %copy-start.68 = (f32[1,1,512]{2,0,1:T(1,128)}, f32[1,1,512]{2,0,1:T(1,128)S(1)}, u32[]{:S(2)}) copy-start(f32[1,1,512]{2,0,1:T(1,128)S(1)} %get-tuple-element.341) | copy-start | bytes 6148
  67.5 76.6 %copy-start.70 = (f32[1,1,512]{2,0,1:T(1,128)}, f32[1,1,512]{2,0,1:T(1,128)S(1)}, u32[]{:S(2)}) copy-start(f32[1,1,512]{2,0,1:T(1,128)S(1)} %get-tuple-element.342) | copy-start | bytes 6148
  67.5 76.6 %copy-start.72 = (f32[1,1,512]{2,0,1:T(1,128)}, f32[1,1,512]{2,0,1:T(1,128)S(1)}, u32[]{:S(2)}) copy-start(f32[1,1,512]{2,0,1:T(1,128)S(1)} %get-tuple-element.343) | copy-start | bytes 6148
  68.1 76.0 %copy-start.49 = (f32[1792]{0:T(1024)}, f32[1792]{0:T(1024)S(1)}, u32[]{:S(2)}) copy-start(f32[1792]{0:T(1024)S(1)} %get-tuple-element.285) | copy-start | bytes 21508
  68.1 76.0 %copy-start.51 = (f32[1792]{0:T(1024)}, f32[1792]{0:T(1024)S(1)}, u32[]{:S(2)}) copy-start(f32[1792]{0:T(1024)S(1)} %get-tuple-element.286) | copy-start | bytes 21508
  68.1 76.0 %copy-start.53 = (f32[1792]{0:T(1024)}, f32[1792]{0:T(1024)S(1)}, u32[]{:S(2)}) copy-start(f32[1792]{0:T(1024)S(1)} %get-tuple-element.287) | copy-start | bytes 21508
  68.1 76.0 %copy-start.55 = (f32[1792]{0:T(1024)}, f32[1792]{0:T(1024)S(1)}, u32[]{:S(2)}) copy-start(f32[1792]{0:T(1024)S(1)} %get-tuple-element.288) | copy-start | bytes 21508
  69.5 33.6 %copy-start.57 = (f32[512]{0:T(512)}, f32[512]{0:T(512)S(1)}, u32[]{:S(2)}) copy-start(f32[512]{0:T(512)S(1)} %compare_convert_fusion.1) | copy-start | bytes 6148
  69.6 33.5 %copy-start.21 = (f32[1,24,512]{1,2,0:T(8,128)}, f32[1,24,512]{1,2,0:T(8,128)S(1)}, u32[]{:S(2)}) copy-start(f32[1,24,512]{1,2,0:T(8,128)S(1)} %get-tuple-element.321) | copy-start | bytes 147460
  69.7 33.5 %copy-start.95 = (f32[24]{0:T(128)}, f32[24]{0:T(128)S(1)}, u32[]{:S(2)}) copy-start(f32[24]{0:T(128)S(1)} %get-tuple-element.336) | copy-start | bytes 292
  70.0 87.1 %copy-start.40 = (f32[512,24]{0,1:T(8,128)}, f32[512,24]{0,1:T(8,128)S(1)}, u32[]{:S(2)}) copy-start(f32[512,24]{0,1:T(8,128)S(1)} %copy.207) | copy-start | bytes 147460
  106.6 36.4 %collective-permute-start = (bf16[1,3,1792]{2,1,0:T(4,128)(2,1)}, bf16[1,3,1792]{2,1,0:T(4,128)(2,1)}, u32[]{:S(2)}, u32[]{:S(2)}) collective-permute-start(bf16[1,3,1792]{2,1,0:T(4,128)(2,1)} %slice.167), channel_id=1, source_target_pairs={{0,1},{2,3},{4,5},{6,7},{8,9},{10,11},{12,13},{14,15},{16,17},{18,... | collective-permute-start | bytes 32264 | tf_op jit(solution)/shard_map/ppermute | solution.py:27
  120.5 13.9 %copy-start.34 = (bf16[1024,128]{0,1:T(8,128)(2,1)}, bf16[1024,128]{0,1:T(8,128)(2,1)S(1)}, u32[]{:S(2)}) copy-start(bf16[1024,128]{0,1:T(8,128)(2,1)S(1)} %copy.195) | copy-start | bytes 786436
  157.0 17.2 %copy-start.108 = (bf16[2,1,24]{2,1,0:T(2,128)(2,1)S(1)}, bf16[2,1,24]{2,1,0:T(2,128)(2,1)}, u32[]{:S(2)}) copy-start(bf16[2,1,24]{2,1,0:T(2,128)(2,1)} %all_gather.52) | copy-start | bytes 292
  174.7 33.9 %copy-start.5 = (f32[1,24,64,128]{3,2,1,0:T(8,128)}, f32[1,24,64,128]{3,2,1,0:T(8,128)S(1)}, u32[]{:S(2)}) copy-start(f32[1,24,64,128]{3,2,1,0:T(8,128)S(1)} %get-tuple-element.189) | copy-start | bytes 2359300
  178.7 30.0 %copy-start.19 = (f32[512,24,64]{0,2,1:T(8,128)}, f32[512,24,64]{0,2,1:T(8,128)S(1)}, u32[]{:S(2)}) copy-start(f32[512,24,64]{0,2,1:T(8,128)S(1)} %fusion.123) | copy-start | bytes 9437188
  216.3 157.5 %copy-start.59 = (f32[512]{0:T(512)}, f32[512]{0:T(512)S(1)}, u32[]{:S(2)}) copy-start(f32[512]{0:T(512)S(1)} %fusion.181) | copy-start | bytes 6148
  272.5 12.7 %copy-start.31 = (f32[512,1024]{1,0:T(8,128)S(1)}, f32[512,1024]{1,0:T(8,128)}, u32[]{:S(2)}) copy-start(f32[512,1024]{1,0:T(8,128)} %get-tuple-element.356) | copy-start | bytes 6291460
  305.6 23.4 %slice-start.2 = ((s8[16777216]{0:T(1024)(128)(4,1)}), s8[4194304]{0:T(1024)(128)(4,1)S(1)}, s32[]{:S(2)}) async-start(s8[16777216]{0:T(1024)(128)(4,1)} %bitcast.439), calls=%async_computation.25 | async-start | bytes 8388608
  305.6 23.4 %slice-start.3 = ((s8[16777216]{0:T(1024)(128)(4,1)}), s8[4194304]{0:T(1024)(128)(4,1)S(1)}, s32[]{:S(2)}) async-start(s8[16777216]{0:T(1024)(128)(4,1)} %bitcast.439), calls=%async_computation.26 | async-start | bytes 8388608
  305.6 23.4 %slice-start.4 = ((s8[16777216]{0:T(1024)(128)(4,1)}), s8[4194304]{0:T(1024)(128)(4,1)S(1)}, s32[]{:S(2)}) async-start(s8[16777216]{0:T(1024)(128)(4,1)} %bitcast.439), calls=%async_computation.27 | async-start | bytes 8388608
  344.6 204.2 %reduce-scatter.16.cloned.1.call-start = ((), (), s32[]{:S(2)}) async-start(), calls=%async_computation.17 | async-start | bytes 6291456 | tf_op jit(solution)/shard_map/reduce_scatter | solution.py:363
  351.8 197.8 %reduce-scatter.24.cloned.1.call-start = ((), (), s32[]{:S(2)}) async-start(), calls=%async_computation.21 | async-start | bytes 6291456 | tf_op jit(solution)/shard_map/reduce_scatter | solution.py:369
  358.1 223.7 %reduce-scatter.20.cloned.1.call-start = ((), (), s32[]{:S(2)}) async-start(), calls=%async_computation.19 | async-start | bytes 12582912 | tf_op jit(solution)/shard_map/reduce_scatter | solution.py:366
  370.2 313.2 %reduce-scatter.12.cloned.1.call-start = ((), (), s32[]{:S(2)}) async-start(), calls=%async_computation.14 | async-start | bytes 12582912 | tf_op jit(solution)/shard_map/reduce_scatter | solution.py:360
  443.8 40.6 %copy-start.6 = (f32[1,24,64,128]{3,2,1,0:T(8,128)S(1)}, f32[1,24,64,128]{3,2,1,0:T(8,128)}, u32[]{:S(2)}) copy-start(f32[1,24,64,128]{3,2,1,0:T(8,128)} %copy-done.5) | copy-start | bytes 2359300
  443.8 40.6 %copy-start.11 = (f32[512,1536]{0,1:T(8,128)S(1)}, f32[512,1536]{0,1:T(8,128)}, u32[]{:S(2)}) copy-start(f32[512,1536]{0,1:T(8,128)} %copy.219) | copy-start | bytes 9437188
  443.8 53.2 %copy-start.20 = (f32[1,512,1536]{2,1,0:T(8,128)S(1)}, f32[1,512,1536]{2,1,0:T(8,128)}, u32[]{:S(2)}) copy-start(f32[1,512,1536]{2,1,0:T(8,128)} %copy.226) | copy-start | bytes 9437188
  484.4 12.6 %copy-start.17 = (f32[1,512,1792]{2,1,0:T(8,128)S(1)}, f32[1,512,1792]{2,1,0:T(8,128)}, u32[]{:S(2)}) copy-start(f32[1,512,1792]{2,1,0:T(8,128)} %get-tuple-element.323) | copy-start | bytes 11010052
  506.2 11.5 %collective-permute-start.1 = (f32[1,3,1792]{2,1,0:T(4,128)S(1)}, f32[1,3,1792]{2,1,0:T(4,128)S(1)}, u32[]{:S(2)}, u32[]{:S(2)}) collective-permute-start(f32[1,3,1792]{2,1,0:T(4,128)S(1)} %pad_add_fusion.2), channel_id=1, source_target_pairs={{1,0},{3,2},{5,4},{7,6},{9,8},{11,10},{13,12},{15,14},{17,16},{19,... | collective-permute-start | bytes 64520 | tf_op jit(solution)/shard_map/ppermute | solution.py:27
  517.7 12.7 %copy-start.39 = (bf16[512,512]{1,0:T(8,128)(2,1)}, bf16[512,512]{1,0:T(8,128)(2,1)S(1)}, u32[]{:S(2)}) copy-start(bf16[512,512]{1,0:T(8,128)(2,1)S(1)} %copy.227) | copy-start | bytes 1572868
  530.5 280.4 %all-reduce.22.cloned.1.call-start = ((), (), s32[]{:S(2)}) async-start(), calls=%async_computation.16 | async-start | bytes 196608 | tf_op jit(solution)/shard_map/psum | solution.py:387
  548.8 328.8 %reduce-scatter.18.cloned.1.call-start = ((), (), s32[]{:S(2)}) async-start(), calls=%async_computation.18 | async-start | bytes 2228224 | tf_op jit(solution)/shard_map/reduce_scatter | solution.py:377
  549.5 392.3 %reduce-scatter.26.cloned.1.call-start = ((), (), s32[]{:S(2)}) async-start(), calls=%async_computation.22 | async-start | bytes 2228224 | tf_op jit(solution)/shard_map/reduce_scatter | solution.py:383
  550.1 467.6 %reduce-scatter.22.cloned.1.call-start = ((), (), s32[]{:S(2)}) async-start(), calls=%async_computation.20 | async-start | bytes 4456448 | tf_op jit(solution)/shard_map/reduce_scatter | solution.py:380
  581.8 101.6 %copy-start.76 = (f32[1536]{0:T(1024)S(1)}, f32[1536]{0:T(1024)}, u32[]{:S(2)}) copy-start(f32[1536]{0:T(1024)} %get-tuple-element.313) | copy-start | bytes 18436
  581.8 101.8 %copy-start.81 = (f32[1792]{0:T(1024)S(1)}, f32[1792]{0:T(1024)}, u32[]{:S(2)}) copy-start(f32[1792]{0:T(1024)} %get-tuple-element.273) | copy-start | bytes 21508
  581.8 101.8 %copy-start.80 = (f32[1792]{0:T(1024)S(1)}, f32[1792]{0:T(1024)}, u32[]{:S(2)}) copy-start(f32[1792]{0:T(1024)} %get-tuple-element.274) | copy-start | bytes 21508
  581.8 101.8 %copy-start.79 = (f32[1792]{0:T(1024)S(1)}, f32[1792]{0:T(1024)}, u32[]{:S(2)}) copy-start(f32[1792]{0:T(1024)} %get-tuple-element.275) | copy-start | bytes 21508
  581.8 101.9 %copy-start.78 = (f32[1792]{0:T(1024)S(1)}, f32[1792]{0:T(1024)}, u32[]{:S(2)}) copy-start(f32[1792]{0:T(1024)} %get-tuple-element.276) | copy-start | bytes 21508
  581.8 101.9 %copy-start.77 = (f32[1792]{0:T(1024)S(1)}, f32[1792]{0:T(1024)}, u32[]{:S(2)}) copy-start(f32[1792]{0:T(1024)} %get-tuple-element.281) | copy-start | bytes 21508
  581.8 102.7 %copy-start.46 = (bf16[1024,24]{0,1:T(8,128)(2,1)S(1)}, bf16[1024,24]{0,1:T(8,128)(2,1)}, u32[]{:S(2)}) copy-start(bf16[1024,24]{0,1:T(8,128)(2,1)} %copy-done.45) | copy-start | bytes 147460
  581.8 104.4 %copy-start.32 = (f32[512,1024]{1,0:T(8,128)S(1)}, f32[512,1024]{1,0:T(8,128)}, u32[]{:S(2)}) copy-start(f32[512,1024]{1,0:T(8,128)} %get-tuple-element.356) | copy-start | bytes 6291460
  581.9 511.4 %reduce-scatter.14.cloned.1.call-start = ((), (), s32[]{:S(2)}) async-start(), calls=%async_computation.15 | async-start | bytes 4456448 | tf_op jit(solution)/shard_map/reduce_scatter | solution.py:374
  812.2 53.8 %copy-start.89 = (f32[512]{0:T(512)S(1)}, f32[512]{0:T(512)}, u32[]{:S(2)}) copy-start(f32[512]{0:T(512)} %copy-done.88) | copy-start | bytes 6148
  812.2 53.8 %copy-start.24 = (f32[512,1024]{1,0:T(8,128)S(1)}, f32[512,1024]{1,0:T(8,128)}, u32[]{:S(2)}) copy-start(f32[512,1024]{1,0:T(8,128)} %copy-done.23) | copy-start | bytes 6291460
  (67 other events, 410.0 us)
Sparse Core Ops, SparseCore 0:
  19.4 75.3 all-gather.7
  97.0 49.0 all-gather.9
  148.2 73.3 all-gather.11
  223.7 48.8 all-gather.13
  344.7 13.0 reduce-scatter.9
  360.1 62.7 reduce-scatter.15
  425.1 54.3 reduce-scatter.23
  481.9 99.8 reduce-scatter.19
  584.1 99.2 reduce-scatter.11
  690.3 120.5 all-reduce.21
  815.1 62.4 reduce-scatter.17
  881.1 60.6 reduce-scatter.25
  946.2 71.4 reduce-scatter.21
  1021.4 71.7 reduce-scatter.13
where the time goes:
time: 1110 us; the launch traced here: 1100 us
  waiting for transfers between devices  523 us (47%)
  matrix products  282 us (25%)
  blocking collectives  143 us (13%)
  other arithmetic  81.6 us (7%)
  local copies, waits for them, and re-layouts  47.8 us (4%)
  between operations  16.7 us (2%)
    psum x1, waiting for transfers between devices, body(): lax.psum((jnp.stack([d_gain1, d_gain2]), g_conv, g_ssm, g_head_out + g_he...  118 us
    reduce_scatter x1, waiting for transfers between devices, body(): lax.psum_scatter(grad_in.astype(jnp.bfloat16), 'seq', scatter_dimension=1...  101 us
    dot_general x3, matrix products, block_output(): within = jnp.einsum('strh,srhd->sthd', weights, inputs, precision=PRECISE)  90.9 us
    reduce_scatter x1, waiting for transfers between devices, body(): lax.psum_scatter(part_gu.astype(jnp.bfloat16), 'fsdp', scatter_dimension=...  74.2 us
    reduce_scatter x1, waiting for transfers between devices, body(): lax.psum_scatter(part_in.astype(jnp.bfloat16), 'fsdp', scatter_dimension=...  73.8 us
    reduce_scatter x1, waiting for transfers between devices, body(): lax.psum_scatter(part_down.astype(jnp.bfloat16), 'fsdp', scatter_dimensio...  62.6 us
    psum x1, blocking collectives, body(): lax.psum((jnp.stack([d_gain1, d_gain2]), g_conv, g_ssm, g_head_out + g_he...  43.1 us
    dot_general x5, matrix products, times_rows(): lax.dot_general(left, weight, (((1,), (1,)), ((), ())), preferred_element...  38.3 us
  transfers between devices with their start and end apart: 16, of which 9 were waited for; matrix products, arithmetic and copies ran while one was open for 30% of the time, Pallas kernels for 0%

commit v1 on v0

--- a/solution.py
+++ b/solution.py
@@ -1,3 +1,4 @@
+import math
 from functools import partial
 
 import jax
@@ -95,9 +96,40 @@
     )
 
 
-def conv_pieces(extended, conv_params, dt_raw, head_params, valid):
-    length = dt_raw.shape[1]
-    summed = conv_params[CONV] + jnp.zeros((extended.shape[0], length, XBC), jnp.float32)
+def seq_gather(blocks):
+    count, place = lax.axis_size("seq"), lax.axis_index("seq")
+    rows, cols = blocks.shape
+    whole = jnp.zeros((rows, count * cols), blocks.dtype)
+    whole = lax.dynamic_update_slice(whole, blocks, (0, place * cols))
+    for hop in range(1, count):
+        route = [(d, (d + hop) % count) for d in range(count)]
+        came = lax.ppermute(blocks, "seq", route)
+        source = lax.rem(place - hop + count, count)
+        whole = lax.dynamic_update_slice(whole, came, (0, source * cols))
+    return whole
+
+
+def seq_scatter(pick):
+    count, place = lax.axis_size("seq"), lax.axis_index("seq")
+    total = pick(place).astype(jnp.float32)
+    for hop in range(1, count):
+        route = [(d, (d + hop) % count) for d in range(count)]
+        target = lax.rem(place + hop, count)
+        total = total + lax.ppermute(pick(target), "seq", route).astype(jnp.float32)
+    return total
+
+
+def columns(array, place, width):
+    return lax.dynamic_slice_in_dim(array, place * width, width, 1)
+
+
+def per_channel(array):
+    return jnp.repeat(array, SSM_DIM, axis=-1)
+
+
+def conv_pieces(extended, conv_params, dt_raw, head_params, valid, chunk):
+    num, length = dt_raw.shape[:2]
+    summed = conv_params[CONV] + jnp.zeros((num, length, XBC), jnp.float32)
     for lagged in range(CONV):
         offset = CONV - 1 - lagged
         summed = (
@@ -106,21 +138,37 @@
             * extended[:, offset : offset + length, :]
             * valid[lagged][..., None]
         )
-    activated = jax.nn.silu(summed)
-    inputs = activated[..., :D_SSM].reshape(activated.shape[0], length, SSM_HEADS, SSM_DIM)
+    activated = jax.nn.silu(summed).reshape(num, length // chunk, chunk, XBC)
+    inputs = activated[..., :D_SSM]
     b_proj = activated[..., D_SSM : D_SSM + STATE]
     c_proj = activated[..., D_SSM + STATE :]
     step_size = jax.nn.softplus(dt_raw + head_params[1])
-    cumul = jnp.cumsum(-jnp.exp(head_params[0]) * step_size, axis=1)
+    step_size = step_size.reshape(num, length // chunk, chunk, SSM_HEADS)
+    lower = jnp.tril(jnp.ones((chunk, chunk), jnp.float32))
+    cumul = jnp.einsum(
+        "tr,scrh->scth", lower, -jnp.exp(head_params[0]) * step_size, precision=PRECISE
+    )
     return (inputs, b_proj, c_proj, step_size, cumul)
 
 
 def block_summary(inputs, b_proj, step_size, cumul, tail_mask, alive):
-    final = cumul[:, -1, :]
-    decay = jnp.exp(final) * alive[:, None]
-    weights = jnp.exp(final[:, None, :] - cumul) * step_size * tail_mask[..., None]
-    state = jnp.einsum("sph,sphd,spn->shdn", weights, inputs, b_proj, precision=PRECISE)
-    return (decay, state)
+    final = cumul[:, :, -1, :]
+    decay = jnp.exp(final) * alive[..., None]
+    weights = jnp.exp(final[:, :, None, :] - cumul) * step_size * tail_mask[..., None]
+    state = jnp.einsum(
+        "scpe,scpn->scen", per_channel(weights) * inputs, b_proj, preferred_element_type=jnp.float32
+    )
+    num, chunks = state.shape[:2]
+    state = state.reshape(num, chunks, SSM_HEADS, SSM_DIM, STATE)
+    reach = jnp.ones_like(decay[:, 0])
+    carried = jnp.zeros_like(state[:, 0])
+    reaches, carries = [], []
+    for k in range(chunks):
+        reaches.append(reach)
+        carries.append(carried)
+        carried = decay[:, k][:, :, None, None] * carried + state[:, k]
+        reach = reach * decay[:, k]
+    return (reach, carried, jnp.stack(reaches, 1), jnp.stack(carries, 1))
 
 
 def block_output(
@@ -130,21 +178,33 @@
     step_size,
     cumul,
     head_params,
+    reaches,
+    carries,
     entering,
     gate_in,
     ssm_gain,
     inner_mask,
     carry_mask,
 ):
-    gram = jnp.einsum("stn,srn->str", c_proj, b_proj, precision=PRECISE)
-    spread = cumul[:, :, None, :] - cumul[:, None, :, :]
-    decays = jnp.exp(jnp.where(inner_mask[..., None], spread, -1e30))
-    weights = decays * (gram[..., None] * step_size[:, None, :, :])
-    within = jnp.einsum("strh,srhd->sthd", weights, inputs, precision=PRECISE)
+    num, chunks, chunk = inputs.shape[:3]
+    gram = jnp.einsum("sctn,scrn->sctr", c_proj, b_proj, preferred_element_type=jnp.float32)
+    cumul_h = jnp.swapaxes(cumul, 2, 3)
+    step_h = jnp.swapaxes(step_size, 2, 3)
+    spread = cumul_h[..., :, None] - cumul_h[..., None, :]
+    decays = jnp.exp(jnp.where(inner_mask[:, :, None], spread, -1e30))
+    weights = decays * (gram[:, :, None] * step_h[..., None, :])
+    heads = inputs.reshape(num, chunks, chunk, SSM_HEADS, SSM_DIM)
+    within = jnp.einsum(
+        "schtr,scrhd->scthd", weights, heads, preferred_element_type=jnp.float32
+    ).reshape(inputs.shape)
     entry = jnp.exp(cumul) * carry_mask[..., None]
-    incoming = jnp.einsum("sth,shdn,stn->sthd", entry, entering, c_proj, precision=PRECISE)
-    output = within + incoming + head_params[2][:, None] * inputs
-    output = output.reshape(output.shape[0], output.shape[1], D_SSM) * jax.nn.silu(gate_in)
+    states = carries + reaches[..., None, None] * entering[:, None]
+    states = states.reshape(num, chunks, D_SSM, STATE)
+    incoming = per_channel(entry) * jnp.einsum(
+        "scen,sctn->scte", states, c_proj, preferred_element_type=jnp.float32
+    )
+    output = within + incoming + per_channel(head_params[2]) * inputs
+    output = output.reshape(num, chunks * chunk, D_SSM) * jax.nn.silu(gate_in)
     return rms_norm(output, ssm_gain)
 
 
@@ -178,13 +238,14 @@
     head_share = HEADS // KV_HEADS
     att_scale = HEAD_DIM ** (-0.5)
     rim_len = CONV - 1
+    chunk = math.gcd(span_len, 128)
+    chunks = span_len // chunk
     base_col = q_width + 2 * kv_width
-    dt_rows = w_dt.shape[0]
     cols_in, cols_out, cols_gu, cols_down = (
-        lax.all_gather(w_in, "seq", axis=1, tiled=True),
-        lax.all_gather(w_out, "seq", axis=1, tiled=True),
-        lax.all_gather(w_gate_up, "seq", axis=1, tiled=True),
-        lax.all_gather(w_down, "seq", axis=1, tiled=True),
+        seq_gather(w_in),
+        seq_gather(w_out),
+        seq_gather(w_gate_up),
+        seq_gather(w_down),
     )
     full_in, full_dt, full_out, full_gu, full_down = (
         lax.all_gather(cols_in, "fsdp", axis=0, tiled=True),
@@ -243,15 +304,18 @@
         jnp.float32
     )
     pieces, pieces_back = jax.vjp(
-        partial(conv_pieces, valid=valid),
+        partial(conv_pieces, valid=valid, chunk=chunk),
         extended,
         conv_params,
         dt_raw.reshape(num_seqs, span_len, SSM_HEADS),
         head_params,
     )
     inputs, b_proj, c_proj, step_size, cumul = pieces
-    tail_mask = (positions[None, :] >= doc_start[:, -1:]).astype(jnp.float32)
-    alive_mask = (doc_start[:, -1] < block_start).astype(jnp.float32)
+    starts = doc_start.reshape(num_seqs, chunks, chunk)
+    places = positions.reshape(chunks, chunk)
+    chunk_start = places[:, :1]
+    tail_mask = (places >= starts[..., -1:]).astype(jnp.float32)
+    alive_mask = (starts[..., -1] < places[:, 0]).astype(jnp.float32)
     summary, summary_back = jax.vjp(
         partial(block_summary, tail_mask=tail_mask, alive=alive_mask),
         inputs,
@@ -263,10 +327,10 @@
     empty_state = jnp.zeros_like(summary[1])
     prefix = entering_2((summary[0], summary[1]), "seq", join_states, (unit_decay, empty_state))
     entering = prefix[1]
-    inner_mask = (positions[None, None, :] <= positions[None, :, None]) & (
-        positions[None, None, :] >= doc_start[:, :, None]
-    )
-    carry_mask = (doc_start < block_start).astype(jnp.float32)
+    inner_mask = (places[:, None, :] <= places[:, :, None]) & (
+        places[:, None, :] >= starts[..., None]
+    )
+    carry_mask = (starts < chunk_start).astype(jnp.float32)
     mamba_f, output_back = jax.vjp(
         partial(block_output, inner_mask=inner_mask, carry_mask=carry_mask),
         inputs,
@@ -275,6 +339,8 @@
         step_size,
         cumul,
         head_params,
+        summary[2],
+        summary[3],
         entering,
         gate_in,
         ssm_gain,
@@ -293,11 +359,17 @@
     d_activ = times_rows(upstream, full_down)
     d_paired = activ_back(d_activ)[0].astype(jnp.bfloat16)
     grad_gu = outer_total(normed2, d_paired)
+    grad_gu = grad_gu.astype(jnp.bfloat16)
+    grad_gu, grad_down, d_paired = lax.optimization_barrier((grad_gu, grad_down.astype(jnp.bfloat16), d_paired))
+    share_gu = lax.psum_scatter(grad_gu, "fsdp", scatter_dimension=0, tiled=True)
     d_normed2 = times_rows(d_paired, full_gu)
     d_second, d_gain2 = norm2_back(d_normed2)
     d_second = d_second + upstream.astype(jnp.float32)
     d_mixed = d_second.astype(jnp.bfloat16)
     grad_out = outer_total(mixed_in, d_mixed)
+    grad_pair = jnp.concatenate([grad_down, grad_out.astype(jnp.bfloat16)], axis=1)
+    grad_pair, d_mixed = lax.optimization_barrier((grad_pair, d_mixed))
+    share_pair = lax.psum_scatter(grad_pair, "fsdp", scatter_dimension=0, tiled=True)
     d_mixed_in = times_rows(d_mixed, full_out)
     d_attended = (
         d_mixed_in[:, :q_width]
@@ -333,13 +405,16 @@
         scatter_dimension=0,
         tiled=True,
     ).astype(jnp.float32)
-    g_inputs, g_bproj, g_cproj, g_step, g_cumul, g_head_out, g_entering, g_gate, g_ssm = (
+    g_inputs, g_bproj, g_cproj, g_step, g_cumul, g_head_out, g_reaches, g_carries, *g_rest = (
         output_back(d_mamba)
     )
+    g_entering, g_gate, g_ssm = g_rest
     ahead = prefix_2((summary[0], g_entering), "seq", join_grads, (unit_decay, empty_state))
     state_grad = ahead[1]
     d_decay = jnp.sum(state_grad * entering, axis=(2, 3))
-    s_inputs, s_bproj, s_step, s_cumul = summary_back((d_decay, state_grad))
+    s_inputs, s_bproj, s_step, s_cumul = summary_back(
+        (d_decay, state_grad, g_reaches, g_carries)
+    )
     d_extended, g_conv, d_dt_raw, g_head_in = pieces_back(
         (g_inputs + s_inputs, g_bproj + s_bproj, g_cproj, g_step + s_step, g_cumul + s_cumul)
     )
@@ -351,54 +426,44 @@
         [d_queries, d_kv, g_gate.reshape(num_rows, D_SSM), d_conv_in.reshape(num_rows, XBC)], axis=1
     ).astype(jnp.bfloat16)
     d_dt_low = d_dt_raw.reshape(num_rows, SSM_HEADS).astype(jnp.bfloat16)
-    grad_in = outer_total(normed, d_projected)
-    grad_dt = outer_total(normed, d_dt_low)
+    pad = jnp.zeros((num_rows, 128 - SSM_HEADS), jnp.bfloat16)
+    grad_in = outer_total(normed, jnp.concatenate([d_projected, d_dt_low, pad], axis=1))
+    share_in = lax.psum_scatter(
+        grad_in.astype(jnp.bfloat16), "fsdp", scatter_dimension=0, tiled=True
+    )
     d_normed = times_rows(d_projected, full_in) + times_rows(d_dt_low, full_dt)
     d_hidden, d_gain1 = norm1_back(d_normed)
     d_hidden = d_hidden + d_second
-    part_in, part_out, part_gu, part_down = (
-        lax.psum_scatter(
-            grad_in.astype(jnp.bfloat16), "seq", scatter_dimension=1, tiled=True
-        ).astype(jnp.float32),
-        lax.psum_scatter(
-            grad_out.astype(jnp.bfloat16), "seq", scatter_dimension=1, tiled=True
-        ).astype(jnp.float32),
-        lax.psum_scatter(
-            grad_gu.astype(jnp.bfloat16), "seq", scatter_dimension=1, tiled=True
-        ).astype(jnp.float32),
-        lax.psum_scatter(
-            grad_down.astype(jnp.bfloat16), "seq", scatter_dimension=1, tiled=True
-        ).astype(jnp.float32),
-    )
-    shard_in, shard_out, shard_gu, shard_down = (
-        lax.psum_scatter(
-            part_in.astype(jnp.bfloat16), "fsdp", scatter_dimension=0, tiled=True
-        ).astype(jnp.float32),
-        lax.psum_scatter(
-            part_out.astype(jnp.bfloat16), "fsdp", scatter_dimension=0, tiled=True
-        ).astype(jnp.float32),
-        lax.psum_scatter(
-            part_gu.astype(jnp.bfloat16), "fsdp", scatter_dimension=0, tiled=True
-        ).astype(jnp.float32),
-        lax.psum_scatter(
-            part_down.astype(jnp.bfloat16), "fsdp", scatter_dimension=0, tiled=True
-        ).astype(jnp.float32),
+    width = model_width // lax.axis_size("seq")
+    in_width = share_gu.shape[1] // lax.axis_size("seq")
+    total_gu = seq_scatter(lambda k: columns(share_gu, k, in_width))
+    total_pair = seq_scatter(
+        lambda k: jnp.concatenate(
+            [
+                columns(share_pair[:, :model_width], k, width),
+                columns(share_pair[:, model_width:], k, width),
+            ],
+            axis=1,
+        )
+    )
+    in_cols = d_projected.shape[1]
+    total_in = seq_scatter(
+        lambda k: jnp.concatenate(
+            [columns(share_in[:, :in_cols], k, in_width), share_in[:, in_cols:]], axis=1
+        )
     )
     summed_small = lax.psum(
-        (jnp.stack([d_gain1, d_gain2]), g_conv, g_ssm, g_head_out + g_head_in, grad_dt),
+        (jnp.stack([d_gain1, d_gain2]), g_conv, g_ssm, g_head_out + g_head_in),
         ("fsdp", "seq"),
-    )
-    shard_dt = lax.dynamic_slice_in_dim(
-        summed_small[4], lax.axis_index("fsdp") * dt_rows, dt_rows, 0
     )
     return (
         result.reshape(num_seqs, span_len, model_width).astype(jnp.bfloat16),
         d_hidden.reshape(num_seqs, span_len, model_width),
-        shard_in,
-        shard_dt,
-        shard_out,
-        shard_gu,
-        shard_down,
+        total_in[:, :in_width],
+        total_in[:, in_width : in_width + SSM_HEADS],
+        total_pair[:, width:],
+        total_gu,
+        total_pair[:, :width],
         summed_small[0],
         summed_small[1],
         summed_small[2],

time: 1110 us -> 747 us (0.67)
  waiting for transfers between devices: 523 us -> 225 us
  matrix products: 282 us -> 189 us
  local copies, waits for them, and re-layouts: 47.8 us -> 88.1 us
  blocking collectives: 143 us -> 104 us
  other arithmetic: 81.6 us -> 97.2 us
  starting transfers between devices: 6.92 us -> 19.8 us
    reduce_scatter x8 -> x3, waiting for transfers between devices: 352 us -> 125 us  [the longest x1 108 us: body(): lax.psum_scatter(grad_in.astype(jnp.bfloat16), 'fsdp', scatter_dimension=...]
    psum x1 -> x0, waiting for transfers between devices: 118 us -> none  [body(): lax.psum((jnp.stack([d_gain1, d_gain2]), g_conv, g_ssm, g_head_out + g_he...]
    dot_general x12 -> x14, matrix products: 126 us -> 46.5 us  [the longest x3 17.4 us: block_output(): jnp.einsum('schtr,scrhd->scthd', weights, heads, preferred_element_type=j...]
    all_gather x4 -> x0, blocking collectives: 33 us -> none  [the longest x1 12 us: body(): lax.all_gather(w_in, 'seq', axis=1, tiled=True)]
    all_gather x1, waiting for transfers between devices: 0.01 us -> 27.2 us  [body(): lax.all_gather(cols_gu, 'fsdp', axis=0, tiled=True)]
    ppermute x0 -> x7, waiting for transfers between devices: none -> 18.6 us  [the longest x4 12.5 us: seq_gather(): came = lax.ppermute(blocks, 'seq', route)]
    unnamed x231 -> x294, local copies, waits for them, and re-layouts: 7.88 us -> 23.5 us
    ppermute x0 -> x7, starting transfers between devices: none -> 13.8 us  [the longest x4 8.44 us: seq_gather(): came = lax.ppermute(blocks, 'seq', route)]
  transfers between devices with their start and end apart: 16 -> 17, of which waited for: 9 -> 9; matrix products, arithmetic and copies ran while one was open for 30% -> 34% of each run, Pallas kernels for 0% -> 0%
where the time goes in v1:
time: 747 us; the launch traced here: 739 us
  waiting for transfers between devices  225 us (30%)
  matrix products  189 us (25%)
  blocking collectives  104 us (14%)
  other arithmetic  97.2 us (13%)
  local copies, waits for them, and re-layouts  88.1 us (12%)
  starting transfers between devices  19.8 us (3%)
  between operations  16.2 us (2%)
    reduce_scatter x1, waiting for transfers between devices, body(): lax.psum_scatter(grad_in.astype(jnp.bfloat16), 'fsdp', scatter_dimension=...  108 us
    psum x1, blocking collectives, body(): lax.psum((jnp.stack([d_gain1, d_gain2]), g_conv, g_ssm, g_head_out + g_he...  45.2 us
    all_gather x1, waiting for transfers between devices, body(): lax.all_gather(cols_down, 'fsdp', axis=0, tiled=True)  39 us
    dot_general x5, matrix products, times_rows(): lax.dot_general(left, weight, (((1,), (1,)), ((), ())), preferred_element...  34.7 us
    dot_general x4, matrix products, outer_total(): lax.dot_general(left, right, (((0,), (0,)), ((), ())), preferred_element_...  29.4 us
    all_gather x1, waiting for transfers between devices, body(): lax.all_gather(cols_gu, 'fsdp', axis=0, tiled=True)  27.2 us
    unnamed x294, local copies, waits for them, and re-layouts  23.5 us
    all_gather x1, blocking collectives, body(): lax.all_gather(w_dt, 'fsdp', axis=0, tiled=True)  22.2 us
  transfers between devices with their start and end apart: 17, of which 9 were waited for; matrix products, arithmetic and copies ran while one was open for 34% of the time, Pallas kernels for 0%

profile of v1, /device:TPU:0, one launch (start us, length us, event | category | flops | bytes accessed | tf_op | source)
XLA Modules:
  0.0 738.8 jit_solution(13416860517812721330)
XLA Ops:
  7.3 3.0 collective-permute-start
  11.3 5.5 collective-permute-done
  25.7 4.5 collective-permute-done.3
  32.9 22.2 %all-gather = bf16[16,64,24]{1,2,0:T(8,128)(2,1)S(1)} all-gather(bf16[1,64,24]{1,2,0:T(8,128)(2,1)S(1)} %bitcast.525), channel_id=1, replica_groups=mesh['fsdp'=16,'seq'=2] {'fsdp'}, dimensions={0}, use_global_device_ids=true | all-gather | bytes 52224 | tf_op jit(solution)/shard_map/all_gather | solution.py:252
  62.8 4.2 all_gather.35
  69.6 3.6 copy.299
  75.3 3.6 copy.297
  80.5 14.1 %all-gather.6.cloned.1.call-done = bf16[1024,4096]{1,0:T(8,128)(2,1)} async-done(((bf16[64,4096]{1,0:T(8,128)(2,1)}), bf16[1024,4096]{1,0:T(8,128)(2,1)}) %all-gather.6.cloned.1.call-update) | async-done | bytes 8388624 | tf_op jit(solution)/shard_map/all_gather | solution.py:251
  94.7 8.2 %convolution_convert_fusion.2 = bf16[512,4096]{1,0:T(8,128)(2,1)S(1)} fusion(bf16[1024,4096]{1,0:T(8,128)(2,1)} %all-gather.6.cloned.1.call-done, bf16[1,512,1024]{2,1,0:T(8,128)(2,1)S(1)} %copy-done.35, f32[1024]{0:T(1024)S(1)} %bitcast.519, f32[512]{0:T(512)S(1)} %fusion.166), kind=kOutput, calls=%fused_computation.33 | convolution fusion | flops 4299161600 | bytes 13637632 | tf_op jit(solution)/shard_map/dot_general | solution.py:260
  105.0 4.0 collective-permute-start.1
  109.0 9.4 %all_gather.33 = bf16[1024,256]{1,0:T(8,128)(2,1)S(1)} all-gather(bf16[512,256]{1,0:T(8,128)(2,1)S(1)} %slice.223), channel_id=1, replica_groups=mesh['fsdp'=16,'seq'=2] {'seq'}, dimensions={0}, use_global_device_ids=true | all-gather | bytes 786432 | tf_op jit(solution)/shard_map/all_gather | solution.py:263
  120.8 10.7 %fusion.205 = (f32[2,4,512]{2,1,0:T(4,128)}, f32[2,4,512,1024]{2,3,1,0:T(8,128)}) fusion(pred[512,1024]{0,1:T(8,128)(4,1)} %compare_and_fusion, bf16[1024,2,64,1]{0,2,3,1:T(8,128)(2,1)S(1)} %bitcast.487, bf16[512,2,4,64]{0,3,2,1:T(8,128)(2,1)S(1)} %bitcast.478), kind=kOutput, calls=%fused_computation.386 | convolution fusion | flops 553649152 | bytes 18104320 | tf_op jit(solution)/shard_map/sub | solution.py:286
  131.6 7.5 %fusion.91 = bf16[2,64,4,512]{3,1,2,0:T(8,128)(2,1)S(1)} fusion(bf16[1024,2,64,1]{0,2,3,1:T(8,128)(2,1)} %bitcast.493, f32[2,4,512,1024]{2,3,1,0:T(8,128)} %get-tuple-element.423, f32[2,4,512]{2,1,0:T(4,128)} %get-tuple-element.422), kind=kOutput, calls=%fused_computation.167 | convolution fusion | flops 545521664 | bytes 17580032 | tf_op jit(solution)/shard_map/kgtc,ckd->tkgd/dot_general | solution.py:290
  141.2 5.3 fusion.34
  151.3 4.9 fusion.13
  156.2 3.6 copy.300
  159.8 3.6 fusion.43
  165.0 10.9 %all_gather.36 = bf16[2,1,24,64,128]{4,3,2,1,0:T(8,128)(2,1)S(1)} all-gather(bf16[1,1,24,64,128]{4,3,2,1,0:T(8,128)(2,1)S(1)} %get-tuple-element.360), channel_id=1, replica_groups=mesh['fsdp'=16,'seq'=2] {'seq'}, dimensions={0}, use_global_device_ids=true | all-gather | bytes 1179648 | tf_op jit(solution)/shard_map/all_gather | solution.py:34
  176.6 6.3 bitcast_add_fusion
  182.9 3.9 multiply_reduce_fusion.11
  188.5 6.8 multiply_reduce_fusion.14
  195.3 27.2 %all-gather.10.cloned.1.call-done = bf16[1024,4096]{1,0:T(8,128)(2,1)} async-done(((bf16[64,4096]{1,0:T(8,128)(2,1)}), bf16[1024,4096]{1,0:T(8,128)(2,1)}) %all-gather.10.cloned.1.call-update) | async-done | bytes 8388624 | tf_op jit(solution)/shard_map/all_gather | solution.py:254
  222.5 11.8 %fusion.184 = f32[512,4096]{1,0:T(8,128)} fusion(bf16[1024,4096]{1,0:T(8,128)(2,1)} %all-gather.10.cloned.1.call-done, f32[512,1024]{1,0:T(8,128)} %get-tuple-element.425, f32[1024]{0:T(1024)S(1)} %bitcast.501, f32[512]{0:T(512)S(1)} %fusion.168), kind=kOutput, calls=%fused_computation.373 | convolution fusion | flops 4296540160 | bytes 18880512 | tf_op jit(solution)/shard_map/dot_general | solution.py:353
  234.3 39.0 %all-gather.12.cloned.1.call-done = bf16[2048,1024]{1,0:T(8,128)(2,1)} async-done(((bf16[128,1024]{1,0:T(8,128)(2,1)}), bf16[2048,1024]{1,0:T(8,128)(2,1)}) %all-gather.12.cloned.1.call-update) | async-done | bytes 4194320 | tf_op jit(solution)/shard_map/all_gather | solution.py:255
  273.3 11.3 %bitcast_multiply_fusion.2 = (f32[512,2048]{1,0:T(8,128)S(1)}, f32[512,2048]{1,0:T(8,128)}, bf16[512,2048]{1,0:T(8,128)(2,1)}) fusion(f32[512,4096]{1,0:T(8,128)} %fusion.184, bf16[2048,1024]{1,0:T(8,128)(2,1)} %all-gather.12.cloned.1.call-done, bf16[1,512,1024]{2,1,0:T(8,128)(2,1)} %param.17), kind=kOutput, calls=%fused_computation.51 | convolution fusion | flops 2162163712 | bytes 24117248 | tf_op jit(solution)/shard_map/dot_general | solution.py:88
  284.7 2.9 add_convert_fusion
  289.6 7.2 convolution_convert_fusion.1
  296.7 6.5 convolution_convert_fusion.4
  303.2 8.3 %multiply_reduce_fusion.12 = (f32[1024]{0:T(1024)}, f32[512]{0:T(512)S(1)}, f32[512,1024]{1,0:T(8,128)S(1)}) fusion(f32[512,1024]{1,0:T(8,128)S(1)} %copy-done.24, f32[512]{0:T(512)S(1)} %fusion.168, f32[1024]{0:T(1024)S(1)} %bitcast.503, bf16[512,4096]{1,0:T(8,128)(2,1)S(1)} %copy-done.34, bf16[1024,4096]{1,0:T(8,128)(2,1)} %all-gather.10.cloned.1.call-done), kind=kOutput, calls=%fused_computation.139 | convolution fusion | flops 4298111488 | bytes 16789504 | tf_op jit(solution)/shard_map/dot_general | solution.py:88
  314.1 4.3 convolution_convert_fusion.3
  318.4 8.2 %pad_maximum_fusion = bf16[2048,2048]{1,0:T(8,128)(2,1)} fusion(bf16[2048,1024]{1,0:T(8,128)(2,1)} %convolution_convert_fusion.3, bf16[2048,1024]{1,0:T(8,128)(2,1)} %convolution_convert_fusion.4), kind=kLoop, calls=%fused_computation.17 | loop fusion | flops 16777216 | bytes 16777216 | tf_op jit(solution)/shard_map/concatenate | solution.py:370
  326.6 4.9 fusion.206
  336.4 9.4 %fusion.98 = bf16[2,64,1024]{2,1,0:T(8,128)(2,1)} fusion(bf16[512,2,4,64]{0,3,2,1:T(8,128)(2,1)} %bitcast.490, f32[2,4,512,1024]{2,3,1,0:T(8,128)} %get-tuple-element.423, f32[2,4,512]{2,1,0:T(4,128)S(1)} %copy-done.116), kind=kOutput, calls=%fused_computation.171 | convolution fusion | flops 545390592 | bytes 17580032 | tf_op jit(solution)/shard_map/kgtc,tkgd->ckd/dot_general | solution.py:393
  345.8 10.5 %fusion.2 = (f32[2,4,512]{2,1,0:T(4,128)S(1)}, f32[2,1024,512,4]{2,1,3,0:T(8,128)}) fusion(f32[2,4,512,1024]{2,3,1,0:T(8,128)} %get-tuple-element.423, f32[2,4,512]{2,1,0:T(4,128)S(1)} %copy-done.116, bf16[1024,2,64,1]{0,2,3,1:T(8,128)(2,1)S(1)} %bitcast.494, bf16[512,2,4,64]{0,3,2,1:T(8,128)(2,1)S(1)} %bitcast.491), kind=kOutput, calls=%fused_computation.8 | convolution fusion | flops 549449728 | bytes 34373632 | tf_op jit(solution)/shard_map/tkgd,ckd->kgtc/dot_general | solution.py:380
  358.1 11.6 %fusion.4 = bf16[2,4,512,1024]{2,3,1,0:T(8,128)(2,1)S(1)} fusion(f32[2,1024,512,4]{2,1,3,0:T(8,128)} %get-tuple-element.429, f32[2,4,512]{2,1,0:T(4,128)S(1)} %get-tuple-element.428, f32[2,4,512,1024]{2,3,1,0:T(8,128)} %get-tuple-element.423, f32[2,4,512]{2,1,0:T(4,128)S(1)} %copy-done.116), kind=kLoop, calls=%fused_computation.10 | loop fusion | flops 16777216 | bytes 41975808 | tf_op jit(solution)/shard_map/convert_element_type | solution.py:384
  369.7 2.6 fusion.101
  376.5 2.8 multiply_reduce_fusion.7
  379.5 5.0 multiply_reduce_fusion.6
  386.2 3.5 reshape.1275
  389.7 5.6 multiply_reduce_fusion.8
  395.3 12.1 %all_gather.40 = bf16[2,1,24,64,128]{4,3,2,1,0:T(8,128)(2,1)} all-gather(bf16[1,1,24,64,128]{4,3,2,1,0:T(8,128)(2,1)S(1)} %bitcast.485), channel_id=1, replica_groups=mesh['fsdp'=16,'seq'=2] {'seq'}, dimensions={0}, use_global_device_ids=true | all-gather | bytes 1179648 | tf_op jit(solution)/shard_map/all_gather | solution.py:59
  411.8 5.2 fusion.12
  417.0 3.5 copy.316
  420.5 3.7 fusion.115
  428.5 5.9 multiply_add_fusion.1
  434.5 3.6 copy.320
  440.4 4.3 bitcast_multiply_fusion.15
  444.7 3.5 copy.321
  448.2 3.0 reduce_sum.344
  452.5 7.3 fusion.30
  461.7 4.2 fusion.69
  471.6 5.3 multiply_reduce_fusion.5
  482.4 5.7 pad_add_fusion
  488.1 2.7 fusion.90
  491.1 4.0 fusion.40
  500.3 6.9 concatenate.59
  507.2 11.5 %convolution_convert_fusion = bf16[1024,4224]{1,0:T(8,128)(2,1)} fusion(bf16[512,4224]{1,0:T(8,128)(2,1)} %concatenate.59, bf16[1,512,1024]{2,1,0:T(8,128)(2,1)} %param.16, f32[1024]{0:T(1024)S(1)} %bitcast.520, f32[512]{0:T(512)S(1)} %copy-done.118), kind=kOutput, calls=%fused_computation.14 | convolution fusion | flops 4435607552 | bytes 14030848 | tf_op jit(solution)/shard_map/dot_general | solution.py:94
  521.0 6.9 fusion.89
  527.9 9.7 %fusion.63 = (f32[1024]{0:T(1024)S(1)}, f32[512]{0:T(512)S(1)}, f32[512,1024]{1,0:T(8,128)}) fusion(bf16[1,512,1024]{2,1,0:T(8,128)(2,1)S(1)} %copy-done.36, f32[512]{0:T(512)S(1)} %copy-done.118, f32[1024]{0:T(1024)S(1)} %bitcast.521, f32[512,1024]{1,0:T(8,128)S(1)} %fusion.207, bf16[1024,4096]{1,0:T(8,128)(2,1)} %all-gather.6.cloned.1.call-done, ...), kind=kOutput, calls=%fused_computation.132 | convolution fusion | flops 4315937280 | bytes 17838080 | tf_op jit(solution)/shard_map/dot_general | solution.py:88
  537.7 45.2 %all-reduce.31 = (f32[2,1024]{1,0:T(2,128)}, f32[5,1792]{1,0:T(8,128)}, f32[1536]{0:T(1024)}, f32[3,24]{1,0:T(4,128)}) all-reduce(f32[2,1024]{1,0:T(2,128)S(1)} %pad_maximum_fusion.8, f32[5,1792]{1,0:T(8,128)S(1)} %pad_add_fusion.3, f32[1536]{0:T(1024)S(1)} %get-tuple-element.300, ...), channel_id=1, replica_groups=mesh['fsdp'=16,'seq'=2] {'fsdp','seq'}, use_global_device_ids=true, to_apply=%region_34.35 | all-reduce | flops 12616 | bytes 100928 | tf_op jit(solution)/shard_map/psum | solution.py:455
  582.9 4.9 fusion.66
  591.2 16.9 %reduce-scatter.9.cloned.1.call-done = bf16[128,2048]{1,0:T(8,128)(2,1)} async-done(((bf16[2048,2048]{1,0:T(8,128)(2,1)}), bf16[128,2048]{1,0:T(8,128)(2,1)}) %reduce-scatter.9.cloned.1.call-update) | async-done | bytes 524304 | tf_op jit(solution)/shard_map/reduce_scatter | solution.py:372
  611.7 108.1 %reduce-scatter.7.cloned.1.call-done = bf16[64,4224]{1,0:T(8,128)(2,1)} async-done(((bf16[1024,4224]{1,0:T(8,128)(2,1)}), bf16[64,4224]{1,0:T(8,128)(2,1)}) %reduce-scatter.7.cloned.1.call-update) | async-done | bytes 540688 | tf_op jit(solution)/shard_map/reduce_scatter | solution.py:431
  724.1 6.1 collective-permute-done.6
  (461 shorter events, 106.9 us)
Async XLA Ops:
  7.2 16.6 %copy-start.59 = (bf16[64,2048]{1,0:T(8,128)(2,1)S(1)}, bf16[64,2048]{1,0:T(8,128)(2,1)}, u32[]{:S(2)}) copy-start(bf16[64,2048]{1,0:T(8,128)(2,1)} %param.22) | copy-start | bytes 786436
  7.2 23.9 %copy-start.67 = (bf16[128,512]{1,0:T(8,128)(2,1)S(1)}, bf16[128,512]{1,0:T(8,128)(2,1)}, u32[]{:S(2)}) copy-start(bf16[128,512]{1,0:T(8,128)(2,1)} %param.23) | copy-start | bytes 393220
  7.2 25.7 %copy-start.122 = (bf16[64,24]{0,1:T(8,128)(2,1)S(1)}, bf16[64,24]{0,1:T(8,128)(2,1)}, u32[]{:S(2)}) copy-start(bf16[64,24]{0,1:T(8,128)(2,1)} %param.20) | copy-start | bytes 9220
  7.2 48.0 %copy-start.35 = (bf16[1,512,1024]{2,1,0:T(8,128)(2,1)S(1)}, bf16[1,512,1024]{2,1,0:T(8,128)(2,1)}, u32[]{:S(2)}) copy-start(bf16[1,512,1024]{2,1,0:T(8,128)(2,1)} %param.16) | copy-start | bytes 3145732
  7.2 87.4 %all-gather.6.cloned.1.call-start = ((), (), s32[]{:S(2)}) async-start(), calls=%async_computation.4 | async-start | bytes 8912896 | tf_op jit(solution)/shard_map/all_gather | solution.py:251
  7.3 9.6 %collective-permute-start = (bf16[64,2048]{1,0:T(8,128)(2,1)}, bf16[64,2048]{1,0:T(8,128)(2,1)S(1)}, u32[]{:S(2)}, u32[]{:S(2)}) collective-permute-start(bf16[64,2048]{1,0:T(8,128)(2,1)} %param.19), channel_id=1, source_target_pairs={{0,1},{1,0},{2,3},{3,2},{4,5},{5,4},{6,7},{7,6},{8,9},{9,8},{10,11... | collective-permute-start | bytes 786440 | tf_op jit(solution)/shard_map/ppermute | solution.py:106
  10.3 45.2 %copy-start.141 = (f32[3,24]{1,0:T(4,128)S(1)}, f32[3,24]{1,0:T(4,128)}, u32[]{:S(2)}) copy-start(f32[3,24]{1,0:T(4,128)} %param.27) | copy-start | bytes 868
  10.3 45.2 %copy-start.119 = (f32[2,1024]{1,0:T(2,128)S(1)}, f32[2,1024]{1,0:T(2,128)}, u32[]{:S(2)}) copy-start(f32[2,1024]{1,0:T(2,128)} %param.24) | copy-start | bytes 24580
  17.7 170.8 %all-gather.8.cloned.1.call-start = ((), (), s32[]{:S(2)}) async-start(), calls=%async_computation.5 | async-start | bytes 4456448 | tf_op jit(solution)/shard_map/all_gather | solution.py:253
  17.7 5.2 collective-permute-start.2
  23.7 198.8 %all-gather.10.cloned.1.call-start = ((), (), s32[]{:S(2)}) async-start(), calls=%async_computation.6 | async-start | bytes 8912896 | tf_op jit(solution)/shard_map/all_gather | solution.py:254
  23.8 6.4 collective-permute-start.3
  25.6 31.9 %copy-start.78 = (s32[1,512]{1,0:T(1,128)S(1)}, s32[1,512]{1,0:T(1,128)}, u32[]{:S(2)}) copy-start(s32[1,512]{1,0:T(1,128)} %param.18) | copy-start | bytes 6148
  31.0 242.3 %all-gather.12.cloned.1.call-start = ((), (), s32[]{:S(2)}) async-start(), calls=%async_computation.7 | async-start | bytes 4456448 | tf_op jit(solution)/shard_map/all_gather | solution.py:255
  31.1 48.6 %collective-permute-start.4 = (bf16[128,512]{1,0:T(8,128)(2,1)S(1)}, bf16[128,512]{1,0:T(8,128)(2,1)S(1)}, u32[]{:S(2)}, u32[]{:S(2)}) collective-permute-start(bf16[128,512]{1,0:T(8,128)(2,1)S(1)} %copy-done.67), channel_id=1, source_target_pairs={{0,1},{1,0},{2,3},{3,2},{4,5},{5,4},{6,7},{7,6},{8,9},{9,8},{10,11... | collective-permute-start | bytes 393224 | tf_op jit(solution)/shard_map/ppermute | solution.py:106
  55.2 11.8 %copy-start.64 = (bf16[1024,24]{0,1:T(8,128)(2,1)}, bf16[1024,24]{0,1:T(8,128)(2,1)S(1)}, u32[]{:S(2)}) copy-start(bf16[1024,24]{0,1:T(8,128)(2,1)S(1)} %reshape.1298) | copy-start | bytes 147460
  55.6 14.1 %copy-start.123 = (f32[24]{0:T(128)}, f32[24]{0:T(128)S(1)}, u32[]{:S(2)}) copy-start(f32[24]{0:T(128)S(1)} %get-tuple-element.403) | copy-start | bytes 292
  55.6 39.1 %copy-start.117 = (f32[512]{0:T(512)}, f32[512]{0:T(512)S(1)}, u32[]{:S(2)}) copy-start(f32[512]{0:T(512)S(1)} %fusion.166) | copy-start | bytes 6148
  55.6 39.1 %copy-start.114 = (f32[1,1024]{1,0:T(1,128)}, f32[1,1024]{1,0:T(1,128)S(1)}, u32[]{:S(2)}) copy-start(f32[1,1024]{1,0:T(1,128)S(1)} %get-tuple-element.395) | copy-start | bytes 12292
  55.6 255.9 %copy-start.81 = (f32[1,1024]{1,0:T(1,128)}, f32[1,1024]{1,0:T(1,128)S(1)}, u32[]{:S(2)}) copy-start(f32[1,1024]{1,0:T(1,128)S(1)} %get-tuple-element.394) | copy-start | bytes 12292
  57.5 9.5 %copy-start.51 = (f32[1,4,128,24]{2,3,1,0:T(8,128)}, f32[1,4,128,24]{2,3,1,0:T(8,128)S(1)}, u32[]{:S(2)}) copy-start(f32[1,4,128,24]{2,3,1,0:T(8,128)S(1)} %copy.296) | copy-start | bytes 147460
  58.1 15.2 %copy-start.125 = (f32[4]{0:T(128)}, f32[4]{0:T(128)S(1)}, u32[]{:S(2)}) copy-start(f32[4]{0:T(128)S(1)} %convert_reduce_fusion) | copy-start | bytes 52
  58.4 92.8 %copy-start.44 = (f32[4,24,128]{2,1,0:T(8,128)}, f32[4,24,128]{2,1,0:T(8,128)S(1)}, u32[]{:S(2)}) copy-start(f32[4,24,128]{2,1,0:T(8,128)S(1)} %fusion.122) | copy-start | bytes 147460
  59.3 13.9 %copy-start.127 = (f32[1,1,24]{2,1,0:T(1,128)}, f32[1,1,24]{2,1,0:T(1,128)S(1)}, u32[]{:S(2)}) copy-start(f32[1,1,24]{2,1,0:T(1,128)S(1)} %get-tuple-element.409) | copy-start | bytes 292
  59.3 13.9 %copy-start.129 = (f32[1,1,24]{2,1,0:T(1,128)}, f32[1,1,24]{2,1,0:T(1,128)S(1)}, u32[]{:S(2)}) copy-start(f32[1,1,24]{2,1,0:T(1,128)S(1)} %get-tuple-element.410) | copy-start | bytes 292
  59.3 104.0 %copy-start.120 = (f32[24]{0:T(128)}, f32[24]{0:T(128)S(1)}, u32[]{:S(2)}) copy-start(f32[24]{0:T(128)S(1)} %get-tuple-element.412) | copy-start | bytes 292
  59.5 81.6 %copy-start.85 = (f32[1,1,512]{2,0,1:T(1,128)}, f32[1,1,512]{2,0,1:T(1,128)S(1)}, u32[]{:S(2)}) copy-start(f32[1,1,512]{2,0,1:T(1,128)S(1)} %get-tuple-element.396) | copy-start | bytes 6148
  59.5 81.6 %copy-start.87 = (f32[1,1,512]{2,0,1:T(1,128)}, f32[1,1,512]{2,0,1:T(1,128)S(1)}, u32[]{:S(2)}) copy-start(f32[1,1,512]{2,0,1:T(1,128)S(1)} %get-tuple-element.397) | copy-start | bytes 6148
  59.5 81.6 %copy-start.89 = (f32[1,1,512]{2,0,1:T(1,128)}, f32[1,1,512]{2,0,1:T(1,128)S(1)}, u32[]{:S(2)}) copy-start(f32[1,1,512]{2,0,1:T(1,128)S(1)} %get-tuple-element.398) | copy-start | bytes 6148
  59.5 81.6 %copy-start.91 = (f32[1,1,512]{2,0,1:T(1,128)}, f32[1,1,512]{2,0,1:T(1,128)S(1)}, u32[]{:S(2)}) copy-start(f32[1,1,512]{2,0,1:T(1,128)S(1)} %get-tuple-element.399) | copy-start | bytes 6148
  73.4 103.0 %copy-start.76 = (f32[1536]{0:T(1024)}, f32[1536]{0:T(1024)S(1)}, u32[]{:S(2)}) copy-start(f32[1536]{0:T(1024)S(1)} %mul.1061) | copy-start | bytes 18436
  79.7 61.5 %copy-start.68 = (f32[1792]{0:T(1024)}, f32[1792]{0:T(1024)S(1)}, u32[]{:S(2)}) copy-start(f32[1792]{0:T(1024)S(1)} %get-tuple-element.319) | copy-start | bytes 21508
  79.7 61.5 %copy-start.70 = (f32[1792]{0:T(1024)}, f32[1792]{0:T(1024)S(1)}, u32[]{:S(2)}) copy-start(f32[1792]{0:T(1024)S(1)} %get-tuple-element.320) | copy-start | bytes 21508
  79.7 61.5 %copy-start.72 = (f32[1792]{0:T(1024)}, f32[1792]{0:T(1024)S(1)}, u32[]{:S(2)}) copy-start(f32[1792]{0:T(1024)S(1)} %get-tuple-element.321) | copy-start | bytes 21508
  79.7 61.5 %copy-start.74 = (f32[1792]{0:T(1024)}, f32[1792]{0:T(1024)S(1)}, u32[]{:S(2)}) copy-start(f32[1792]{0:T(1024)S(1)} %get-tuple-element.322) | copy-start | bytes 21508
  80.5 419.1 %reduce-scatter.5.cloned.1.call-start = ((), (), s32[]{:S(2)}) async-start(), calls=%async_computation.8 | async-start | bytes 786432 | tf_op jit(solution)/shard_map/reduce_scatter | solution.py:396
  102.9 15.5 %copy-start.20 = (bf16[512,4096]{1,0:T(8,128)(2,1)}, bf16[512,4096]{1,0:T(8,128)(2,1)S(1)}, u32[]{:S(2)}) copy-start(bf16[512,4096]{1,0:T(8,128)(2,1)S(1)} %convolution_convert_fusion.2) | copy-start | bytes 12582916
  105.0 35.0 %collective-permute-start.1 = (bf16[1,3,1792]{2,1,0:T(4,128)(2,1)}, bf16[1,3,1792]{2,1,0:T(4,128)(2,1)}, u32[]{:S(2)}, u32[]{:S(2)}) collective-permute-start(bf16[1,3,1792]{2,1,0:T(4,128)(2,1)} %slice.228), channel_id=1, source_target_pairs={{0,1},{2,3},{4,5},{6,7},{8,9},{10,11},{12,13},{14,15},{16,17},{18,... | collective-permute-start | bytes 32264 | tf_op jit(solution)/shard_map/ppermute | solution.py:28
  119.5 12.1 %copy-start.46 = (bf16[1024,128]{0,1:T(8,128)(2,1)}, bf16[1024,128]{0,1:T(8,128)(2,1)S(1)}, u32[]{:S(2)}) copy-start(bf16[1024,128]{0,1:T(8,128)(2,1)S(1)} %copy.287) | copy-start | bytes 786436
  120.8 10.7 %copy-start.38 = (bf16[512,512]{0,1:T(8,128)(2,1)}, bf16[512,512]{0,1:T(8,128)(2,1)S(1)}, u32[]{:S(2)}) copy-start(bf16[512,512]{0,1:T(8,128)(2,1)S(1)} %copy.288) | copy-start | bytes 1572868
  163.3 12.6 %copy-start.15 = (f32[4,1536,128]{2,1,0:T(8,128)}, f32[4,1536,128]{2,1,0:T(8,128)S(1)}, u32[]{:S(2)}) copy-start(f32[4,1536,128]{2,1,0:T(8,128)S(1)} %fusion.43) | copy-start | bytes 9437188
  163.4 12.5 %copy-start.143 = (bf16[2,1,24]{2,1,0:T(2,128)(2,1)S(1)}, bf16[2,1,24]{2,1,0:T(2,128)(2,1)}, u32[]{:S(2)}) copy-start(bf16[2,1,24]{2,1,0:T(2,128)(2,1)} %all_gather.35) | copy-start | bytes 292
  165.0 11.4 %copy-start.29 = (f32[1,1,24,64,128]{4,3,2,1,0:T(8,128)}, f32[1,1,24,64,128]{4,3,2,1,0:T(8,128)S(1)}, u32[]{:S(2)}) copy-start(f32[1,1,24,64,128]{4,3,2,1,0:T(8,128)S(1)} %get-tuple-element.361) | copy-start | bytes 2359300
  165.0 11.4 %copy-start.30 = (f32[1,1,24,64,128]{4,3,2,1,0:T(8,128)}, f32[1,1,24,64,128]{4,3,2,1,0:T(8,128)S(1)}, u32[]{:S(2)}) copy-start(f32[1,1,24,64,128]{4,3,2,1,0:T(8,128)S(1)} %get-tuple-element.362) | copy-start | bytes 2359300
  186.7 189.8 %copy-start.2 = (f32[512,1536]{1,0:T(8,128)}, f32[512,1536]{1,0:T(8,128)S(1)}, u32[]{:S(2)}) copy-start(f32[512,1536]{1,0:T(8,128)S(1)} %get-tuple-element.359) | copy-start | bytes 9437188
  195.3 116.3 %copy-start.104 = (f32[512]{0:T(512)}, f32[512]{0:T(512)S(1)}, u32[]{:S(2)}) copy-start(f32[512]{0:T(512)S(1)} %fusion.168) | copy-start | bytes 6148
  326.6 9.8 %copy-start.116 = (f32[2,4,512]{2,1,0:T(4,128)S(1)}, f32[2,4,512]{2,1,0:T(4,128)}, u32[]{:S(2)}) copy-start(f32[2,4,512]{2,1,0:T(4,128)} %get-tuple-element.422) | copy-start | bytes 49156
  336.4 9.4 %copy-start.55 = (bf16[512,512]{0,1:T(8,128)(2,1)S(1)}, bf16[512,512]{0,1:T(8,128)(2,1)}, u32[]{:S(2)}) copy-start(bf16[512,512]{0,1:T(8,128)(2,1)} %copy.304) | copy-start | bytes 1572868
  336.4 9.4 %copy-start.61 = (bf16[1024,128]{0,1:T(8,128)(2,1)S(1)}, bf16[1024,128]{0,1:T(8,128)(2,1)}, u32[]{:S(2)}) copy-start(bf16[1024,128]{0,1:T(8,128)(2,1)} %copy.286) | copy-start | bytes 786436
  358.1 11.6 %copy-start.39 = (bf16[512,512]{0,1:T(8,128)(2,1)S(1)}, bf16[512,512]{0,1:T(8,128)(2,1)}, u32[]{:S(2)}) copy-start(bf16[512,512]{0,1:T(8,128)(2,1)} %copy-done.38) | copy-start | bytes 1572868
  375.7 212.1 %reduce-scatter.11.cloned.1.call-start = ((), (), s32[]{:S(2)}) async-start(), calls=%async_computation.11 | async-start | bytes 8912896 | tf_op jit(solution)/shard_map/reduce_scatter | solution.py:364
  376.3 231.9 %reduce-scatter.9.cloned.1.call-start = ((), (), s32[]{:S(2)}) async-start(), calls=%async_computation.10 | async-start | bytes 8912896 | tf_op jit(solution)/shard_map/reduce_scatter | solution.py:372
  410.8 309.0 %reduce-scatter.7.cloned.1.call-start = ((), (), s32[]{:S(2)}) async-start(), calls=%async_computation.9 | async-start | bytes 9191424 | tf_op jit(solution)/shard_map/reduce_scatter | solution.py:431
  452.5 9.2 %copy-start.139 = (f32[4]{0:T(128)S(1)}, f32[4]{0:T(128)}, u32[]{:S(2)}) copy-start(f32[4]{0:T(128)} %pad.149.clone) | copy-start | bytes 52
  480.8 16.3 %collective-permute-start.5 = (f32[1,3,1792]{2,1,0:T(4,128)}, f32[1,3,1792]{2,1,0:T(4,128)}, u32[]{:S(2)}, u32[]{:S(2)}) collective-permute-start(f32[1,3,1792]{2,1,0:T(4,128)} %pad_add_fusion.4), channel_id=1, source_target_pairs={{1,0},{3,2},{5,4},{7,6},{9,8},{11,10},{13,12},{15,14},{17,16},{19,... | collective-permute-start | bytes 64520 | tf_op jit(solution)/shard_map/ppermute | solution.py:28
  527.9 9.8 %copy-start.137 = (f32[1024]{0:T(1024)S(1)}, f32[1024]{0:T(1024)}, u32[]{:S(2)}) copy-start(f32[1024]{0:T(1024)} %get-tuple-element.306) | copy-start | bytes 12292
  527.9 55.0 %copy-start.109 = (f32[512]{0:T(512)S(1)}, f32[512]{0:T(512)}, u32[]{:S(2)}) copy-start(f32[512]{0:T(512)} %copy-done.108) | copy-start | bytes 6148
  527.9 55.0 %copy-start.82 = (f32[1,1024]{1,0:T(1,128)S(1)}, f32[1,1024]{1,0:T(1,128)}, u32[]{:S(2)}) copy-start(f32[1,1024]{1,0:T(1,128)} %copy-done.81) | copy-start | bytes 12292
  527.9 55.0 %copy-start.103 = (f32[512]{0:T(512)S(1)}, f32[512]{0:T(512)}, u32[]{:S(2)}) copy-start(f32[512]{0:T(512)} %copy-done.102) | copy-start | bytes 6148
  527.9 55.0 %copy-start.105 = (f32[512]{0:T(512)S(1)}, f32[512]{0:T(512)}, u32[]{:S(2)}) copy-start(f32[512]{0:T(512)} %copy-done.104) | copy-start | bytes 6148
  587.8 23.0 %copy-start.53 = (bf16[64,4096]{1,0:T(8,128)(2,1)S(1)}, bf16[64,4096]{1,0:T(8,128)(2,1)}, u32[]{:S(2)}) copy-start(bf16[64,4096]{1,0:T(8,128)(2,1)} %reduce-scatter.11.cloned.1.call-done) | copy-start | bytes 1572868
  588.9 22.0 %collective-permute-start.8 = (bf16[64,2048]{1,0:T(8,128)(2,1)S(1)}, bf16[64,2048]{1,0:T(8,128)(2,1)S(1)}, u32[]{:S(2)}, u32[]{:S(2)}) collective-permute-start(bf16[64,2048]{1,0:T(8,128)(2,1)S(1)} %constant_dynamic-slice_fusion), channel_id=1, source_target_pairs={{0,1},{1,0},{2,3},{3,2},{4,5},{5,4},{6,7},{7,6},{8,9},{9,8},{10,11... | collective-permute-start | bytes 786440 | tf_op jit(solution)/shard_map/ppermute | solution.py:118
  609.3 113.9 %collective-permute-start.7 = (bf16[128,1024]{1,0:T(8,128)(2,1)S(1)}, bf16[128,1024]{1,0:T(8,128)(2,1)S(1)}, u32[]{:S(2)}, u32[]{:S(2)}) collective-permute-start(bf16[128,1024]{1,0:T(8,128)(2,1)S(1)} %pad_maximum_fusion.7), channel_id=1, source_target_pairs={{0,1},{1,0},{2,3},{3,2},{4,5},{5,4},{6,7},{7,6},{8,9},{9,8},{10,11... | collective-permute-start | bytes 786440 | tf_op jit(solution)/shard_map/ppermute | solution.py:118
  721.7 8.5 %collective-permute-start.6 = (bf16[64,2176]{1,0:T(8,128)(2,1)S(1)}, bf16[64,2176]{1,0:T(8,128)(2,1)S(1)}, u32[]{:S(2)}, u32[]{:S(2)}) collective-permute-start(bf16[64,2176]{1,0:T(8,128)(2,1)S(1)} %pad_maximum_fusion.5), channel_id=1, source_target_pairs={{0,1},{1,0},{2,3},{3,2},{4,5},{5,4},{6,7},{7,6},{8,9},{9,8},{10,11... | collective-permute-start | bytes 835592 | tf_op jit(solution)/shard_map/ppermute | solution.py:118
  (99 other events, 375.0 us)
Sparse Core Ops, SparseCore 0:
  17.8 76.8 all-gather.5
  97.4 48.8 all-gather.7
  149.1 73.3 all-gather.9
  224.5 48.7 all-gather.11
  375.8 13.0 reduce-scatter.4
  393.4 104.6 reduce-scatter.10
  502.7 105.4 reduce-scatter.8
  612.8 106.9 reduce-scatter.6

commit v2 on v1

--- a/solution.py
+++ b/solution.py
@@ -28,52 +28,64 @@
     return lax.ppermute(block, axis, route)
 
 
-def entering_2(array, axis, combine, identity):
-    devices, index = (lax.axis_size(axis), lax.axis_index(axis))
-    everything = jax.tree.map(
-        lambda part, kind: lax.all_gather(part.astype(kind), axis),
-        array,
-        (jnp.bfloat16, jnp.bfloat16),
-    )
-    start = jax.tree.map(
-        lambda part, zero: jnp.broadcast_to(jnp.asarray(zero, part.dtype), part.shape),
-        array,
-        identity,
-    )
-
-    def lap(k, before):
-        reached = k < index
-        new = combine(
-            before, jax.tree.map(lambda part, own: part[k].astype(own.dtype), everything, array)
-        )
-        return jax.tree.map(lambda a, b: jnp.where(reached, a, b), new, before)
-
-    return lax.fori_loop(0, devices, lap, start)
-
-
-def prefix_2(array, axis, join, neutral):
-    count = lax.axis_size(axis)
-    place = lax.axis_index(axis)
-    ahead = count - 1 - place
-    gathered = jax.tree.map(
-        lambda a, kind: lax.all_gather(a.astype(kind), axis),
-        array,
-        jax.tree.map(lambda a: jnp.bfloat16 if a.dtype == jnp.float32 else a.dtype, array),
-    )
-    state = jax.tree.map(lambda a, e: jnp.zeros_like(a) + jnp.asarray(e, a.dtype), array, neutral)
-
-    def one(lap, state):
-        source = count - 1 - lap
-        return join(
-            state,
-            jax.tree.map(
-                lambda a, own: lax.dynamic_index_in_dim(a, source, 0, False).astype(own.dtype),
-                gathered,
-                array,
-            ),
-        )
-
-    return lax.fori_loop(0, ahead, one, state)
+def entering_states(decay, state, direction):
+    count = lax.axis_size("seq")
+    rank = lax.axis_index("seq")
+    if direction < 0:
+        rank = count - 1 - rank
+    decay = jnp.where(rank == 0, 1.0, passed_along(decay, "seq", direction))
+    state = passed_along(state.astype(jnp.bfloat16), "seq", direction).astype(jnp.float32)
+    reach = 1
+    while reach < count - 1:
+        earlier = passed_along(decay, "seq", direction * reach)
+        lower = passed_along(state.astype(jnp.bfloat16), "seq", direction * reach)
+        joined = decay[:, :, None, None] * lower.astype(jnp.float32) + state
+        state = jnp.where(rank >= reach, joined, state)
+        decay = jnp.where(rank >= reach, decay * earlier, decay)
+        reach *= 2
+    return state
+
+
+def other_core(block):
+    route = [(d, d + 1 - 2 * (d % 2)) for d in range(lax.axis_size("fsdp"))]
+    return lax.ppermute(block, "fsdp", route)
+
+
+def same_core():
+    count = lax.axis_size("fsdp")
+    return [list(range(0, count, 2)), list(range(1, count, 2))]
+
+
+def chip_gather(block):
+    rows, cols = block.shape
+    chips = lax.axis_size("fsdp") // 2
+    own = lax.all_gather(block, "fsdp", axis=0, tiled=True, axis_index_groups=same_core())
+    other = other_core(own)
+    first = lax.axis_index("fsdp") % 2 == 0
+    even = jnp.where(first, own, other).reshape(chips, 1, rows, cols)
+    odd = jnp.where(first, other, own).reshape(chips, 1, rows, cols)
+    return jnp.concatenate([even, odd], axis=1).reshape(2 * chips * rows, cols)
+
+
+def core_sums(grad):
+    chips = lax.axis_size("fsdp") // 2
+    rows = grad.shape[0] // (2 * chips)
+    split = grad.reshape(chips, 2, rows, grad.shape[1])
+    core = lax.axis_index("fsdp") % 2
+    mine = lax.dynamic_index_in_dim(split, core, 1, False)
+    came = other_core(lax.dynamic_index_in_dim(split, 1 - core, 1, False))
+    return (mine.astype(jnp.float32) + came.astype(jnp.float32)).astype(jnp.bfloat16)
+
+
+def chip_scatter(sums):
+    chips, rows, cols = sums.shape
+    return lax.psum_scatter(
+        sums.reshape(chips * rows, cols),
+        "fsdp",
+        scatter_dimension=0,
+        axis_index_groups=same_core(),
+        tiled=True,
+    )
 
 
 def rms_norm(values, gain):
@@ -96,16 +108,18 @@
     )
 
 
-def seq_gather(blocks):
+def seq_gather(block, axis):
     count, place = lax.axis_size("seq"), lax.axis_index("seq")
-    rows, cols = blocks.shape
-    whole = jnp.zeros((rows, count * cols), blocks.dtype)
-    whole = lax.dynamic_update_slice(whole, blocks, (0, place * cols))
+    size = block.shape[axis]
+    shape = list(block.shape)
+    shape[axis] *= count
+    whole = jnp.zeros(shape, block.dtype)
+    whole = lax.dynamic_update_slice_in_dim(whole, block, place * size, axis)
     for hop in range(1, count):
         route = [(d, (d + hop) % count) for d in range(count)]
-        came = lax.ppermute(blocks, "seq", route)
+        came = lax.ppermute(block, "seq", route)
         source = lax.rem(place - hop + count, count)
-        whole = lax.dynamic_update_slice(whole, came, (0, source * cols))
+        whole = lax.dynamic_update_slice_in_dim(whole, came, source * size, axis)
     return whole
 
 
@@ -208,14 +222,6 @@
     return rms_norm(output, ssm_gain)
 
 
-def join_states(earlier, later):
-    return (earlier[0] * later[0], later[0][:, :, None, None] * earlier[1] + later[1])
-
-
-def join_grads(earlier, later):
-    return (later[0] * earlier[0], later[1] + later[0][:, :, None, None] * earlier[1])
-
-
 def body(
     tokens,
     cotangent,
@@ -242,17 +248,17 @@
     chunks = span_len // chunk
     base_col = q_width + 2 * kv_width
     cols_in, cols_out, cols_gu, cols_down = (
-        seq_gather(w_in),
-        seq_gather(w_out),
-        seq_gather(w_gate_up),
-        seq_gather(w_down),
+        seq_gather(w_in, 1),
+        seq_gather(w_out, 1),
+        seq_gather(w_gate_up, 1),
+        seq_gather(w_down, 1),
     )
     full_in, full_dt, full_out, full_gu, full_down = (
-        lax.all_gather(cols_in, "fsdp", axis=0, tiled=True),
+        chip_gather(cols_in),
         lax.all_gather(w_dt, "fsdp", axis=0, tiled=True),
-        lax.all_gather(cols_out, "fsdp", axis=0, tiled=True),
-        lax.all_gather(cols_gu, "fsdp", axis=0, tiled=True),
-        lax.all_gather(cols_down, "fsdp", axis=0, tiled=True),
+        chip_gather(cols_out),
+        chip_gather(cols_gu),
+        chip_gather(cols_down),
     )
     hidden = tokens.reshape(num_rows, model_width).astype(jnp.float32)
     normed_f, norm1_back = jax.vjp(rms_norm, hidden, norm_gains[0])
@@ -260,7 +266,7 @@
     projected = jnp.dot(normed, full_in, preferred_element_type=jnp.float32).astype(jnp.bfloat16)
     dt_raw = jnp.dot(normed, full_dt, preferred_element_type=jnp.float32)
     queries = projected[:, :q_width].reshape(num_rows, KV_HEADS, head_share, HEAD_DIM)
-    kv_all = lax.all_gather(projected[:, q_width:base_col], "seq", axis=0, tiled=True)
+    kv_all = seq_gather(projected[:, q_width:base_col], 0)
     total_keys = kv_all.shape[0]
     keys_all = kv_all[:, :kv_width].reshape(total_keys, KV_HEADS, HEAD_DIM)
     values_all = kv_all[:, kv_width:].reshape(total_keys, KV_HEADS, HEAD_DIM)
@@ -323,10 +329,7 @@
         step_size,
         cumul,
     )
-    unit_decay = jnp.ones_like(summary[0])
-    empty_state = jnp.zeros_like(summary[1])
-    prefix = entering_2((summary[0], summary[1]), "seq", join_states, (unit_decay, empty_state))
-    entering = prefix[1]
+    entering = entering_states(summary[0], summary[1], 1)
     inner_mask = (places[:, None, :] <= places[:, :, None]) & (
         places[:, None, :] >= starts[..., None]
     )
@@ -359,17 +362,19 @@
     d_activ = times_rows(upstream, full_down)
     d_paired = activ_back(d_activ)[0].astype(jnp.bfloat16)
     grad_gu = outer_total(normed2, d_paired)
-    grad_gu = grad_gu.astype(jnp.bfloat16)
-    grad_gu, grad_down, d_paired = lax.optimization_barrier((grad_gu, grad_down.astype(jnp.bfloat16), d_paired))
-    share_gu = lax.psum_scatter(grad_gu, "fsdp", scatter_dimension=0, tiled=True)
+    grad_gu, grad_down, d_paired = lax.optimization_barrier(
+        (grad_gu.astype(jnp.bfloat16), grad_down.astype(jnp.bfloat16), d_paired)
+    )
+    share_gu = chip_scatter(core_sums(grad_gu))
     d_normed2 = times_rows(d_paired, full_gu)
     d_second, d_gain2 = norm2_back(d_normed2)
     d_second = d_second + upstream.astype(jnp.float32)
     d_mixed = d_second.astype(jnp.bfloat16)
     grad_out = outer_total(mixed_in, d_mixed)
-    grad_pair = jnp.concatenate([grad_down, grad_out.astype(jnp.bfloat16)], axis=1)
-    grad_pair, d_mixed = lax.optimization_barrier((grad_pair, d_mixed))
-    share_pair = lax.psum_scatter(grad_pair, "fsdp", scatter_dimension=0, tiled=True)
+    grad_out, d_mixed = lax.optimization_barrier((grad_out.astype(jnp.bfloat16), d_mixed))
+    share_pair = chip_scatter(
+        jnp.concatenate([core_sums(grad_down), core_sums(grad_out)], axis=1)
+    )
     d_mixed_in = times_rows(d_mixed, full_out)
     d_attended = (
         d_mixed_in[:, :q_width]
@@ -393,24 +398,15 @@
     d_values = jnp.einsum(
         "kgtc,tkgd->ckd", probs_low, d_attended, preferred_element_type=jnp.float32
     )
-    d_kv = lax.psum_scatter(
-        jnp.concatenate(
-            [
-                d_keys.reshape(num_rows * lax.axis_size("seq"), kv_width),
-                d_values.reshape(num_rows * lax.axis_size("seq"), kv_width),
-            ],
-            axis=1,
-        ).astype(jnp.bfloat16),
-        "seq",
-        scatter_dimension=0,
-        tiled=True,
-    ).astype(jnp.float32)
+    d_kv_all = jnp.concatenate(
+        [d_keys.reshape(total_keys, kv_width), d_values.reshape(total_keys, kv_width)], axis=1
+    ).astype(jnp.bfloat16)
+    d_kv = seq_scatter(lambda k: lax.dynamic_slice_in_dim(d_kv_all, k * num_rows, num_rows, 0))
     g_inputs, g_bproj, g_cproj, g_step, g_cumul, g_head_out, g_reaches, g_carries, *g_rest = (
         output_back(d_mamba)
     )
     g_entering, g_gate, g_ssm = g_rest
-    ahead = prefix_2((summary[0], g_entering), "seq", join_grads, (unit_decay, empty_state))
-    state_grad = ahead[1]
+    state_grad = entering_states(summary[0], g_entering, -1)
     d_decay = jnp.sum(state_grad * entering, axis=(2, 3))
     s_inputs, s_bproj, s_step, s_cumul = summary_back(
         (d_decay, state_grad, g_reaches, g_carries)
@@ -428,24 +424,15 @@
     d_dt_low = d_dt_raw.reshape(num_rows, SSM_HEADS).astype(jnp.bfloat16)
     pad = jnp.zeros((num_rows, 128 - SSM_HEADS), jnp.bfloat16)
     grad_in = outer_total(normed, jnp.concatenate([d_projected, d_dt_low, pad], axis=1))
-    share_in = lax.psum_scatter(
-        grad_in.astype(jnp.bfloat16), "fsdp", scatter_dimension=0, tiled=True
-    )
+    share_in = chip_scatter(core_sums(grad_in.astype(jnp.bfloat16)))
     d_normed = times_rows(d_projected, full_in) + times_rows(d_dt_low, full_dt)
     d_hidden, d_gain1 = norm1_back(d_normed)
     d_hidden = d_hidden + d_second
     width = model_width // lax.axis_size("seq")
     in_width = share_gu.shape[1] // lax.axis_size("seq")
     total_gu = seq_scatter(lambda k: columns(share_gu, k, in_width))
-    total_pair = seq_scatter(
-        lambda k: jnp.concatenate(
-            [
-                columns(share_pair[:, :model_width], k, width),
-                columns(share_pair[:, model_width:], k, width),
-            ],
-            axis=1,
-        )
-    )
+    total_pair = seq_scatter(lambda k: columns(share_pair, k, width))
+    pair_rows = total_pair.shape[0] // 2
     in_cols = d_projected.shape[1]
     total_in = seq_scatter(
         lambda k: jnp.concatenate(
@@ -461,9 +448,9 @@
         d_hidden.reshape(num_seqs, span_len, model_width),
         total_in[:, :in_width],
         total_in[:, in_width : in_width + SSM_HEADS],
-        total_pair[:, width:],
+        total_pair[pair_rows:],
         total_gu,
-        total_pair[:, :width],
+        total_pair[:pair_rows],
         summed_small[0],
         summed_small[1],
         summed_small[2],

time: 747 us -> 840 us (1.12)
  waiting for transfers between devices: 225 us -> 295 us
  other arithmetic: 97.2 us -> 153 us
  blocking collectives: 104 us -> 65.3 us
  matrix products: 189 us -> 170 us
  local copies, waits for them, and re-layouts: 88.1 us -> 103 us
    all_gather x4, waiting for transfers between devices: 80.4 us -> 183 us  [chip_gather(): lax.all_gather(block, 'fsdp', axis=0, tiled=True, axis_index_groups=same_...]
    reduce_scatter x4 -> x3, waiting for transfers between devices: 125 us -> 84.4 us  [chip_scatter(): lax.psum_scatter(sums.reshape(chips * rows, cols), 'fsdp', scatter_dimens...]
    all_gather x4 -> x0, blocking collectives: 36.6 us -> none  [the longest x2 15.1 us: entering_2(): lax.all_gather(part.astype(kind), axis)]
    select_n x2 -> x4, other arithmetic: 0.38 us -> 19.7 us  [chip_gather(): even = jnp.where(first, own, other).reshape(chips, 1, rows, cols)]
    concatenate x3 -> x6, other arithmetic: 10.1 us -> 26.6 us  [the longest x4 22.5 us: chip_gather(): return jnp.concatenate([even, odd], axis=1).reshape(2 * chips * rows, cols)]
    convert_element_type x4 -> x5, other arithmetic: 1.57 us -> 15.8 us  [the longest x4 14.1 us: core_sums(): (mine.astype(jnp.float32) + came.astype(jnp.float32)).astype(jnp.bfloat16)]
    dot_general x5, matrix products: 34.7 us -> 24.6 us  [times_rows(): lax.dot_general(left, weight, (((1,), (1,)), ((), ())), preferred_element...]
    ppermute x4 -> x13, waiting for transfers between devices: 12.5 us -> 22 us  [the longest x5 15 us: seq_gather(): came = lax.ppermute(block, 'seq', route)]
  transfers between devices with their start and end apart: 17 -> 28, of which waited for: 9 -> 12; matrix products, arithmetic and copies ran while one was open for 34% -> 35% of each run, Pallas kernels for 0% -> 0%
where the time goes in v2:
time: 840 us; the launch traced here: 830 us
  waiting for transfers between devices  295 us (35%)
  matrix products  170 us (20%)
  other arithmetic  153 us (18%)
  local copies, waits for them, and re-layouts  103 us (12%)
  blocking collectives  65.3 us (8%)
  starting transfers between devices  26.6 us (3%)
  between operations  16.5 us (2%)
    all_gather x4, waiting for transfers between devices, chip_gather(): lax.all_gather(block, 'fsdp', axis=0, tiled=True, axis_index_groups=same_...  183 us
    reduce_scatter x3, waiting for transfers between devices, chip_scatter(): lax.psum_scatter(sums.reshape(chips * rows, cols), 'fsdp', scatter_dimens...  84.4 us
    psum x1, blocking collectives, body(): lax.psum((jnp.stack([d_gain1, d_gain2]), g_conv, g_ssm, g_head_out + g_he...  42.8 us
    dot_general x4, matrix products, outer_total(): lax.dot_general(left, right, (((0,), (0,)), ((), ())), preferred_element_...  25.7 us
    dot_general x5, matrix products, times_rows(): lax.dot_general(left, weight, (((1,), (1,)), ((), ())), preferred_element...  24.6 us
    all_gather x1, blocking collectives, body(): lax.all_gather(w_dt, 'fsdp', axis=0, tiled=True)  22.5 us
    concatenate x4, other arithmetic, chip_gather(): return jnp.concatenate([even, odd], axis=1).reshape(2 * chips * rows, cols)  22.5 us
    unnamed x322, local copies, waits for them, and re-layouts  21.5 us
  transfers between devices with their start and end apart: 28, of which 12 were waited for; matrix products, arithmetic and copies ran while one was open for 35% of the time, Pallas kernels for 0%

profile of v2, /device:TPU:0, one launch (start us, length us, event | category | flops | bytes accessed | tf_op | source)
XLA Modules:
  0.0 829.8 jit_solution(7428012947021108900)
XLA Ops:
  7.3 3.0 collective-permute-start
  11.3 5.5 collective-permute-done
  31.7 4.6 collective-permute-done.7
  37.1 22.5 %all-gather = bf16[16,64,24]{1,2,0:T(8,128)(2,1)S(1)} all-gather(bf16[1,64,24]{1,2,0:T(8,128)(2,1)S(1)} %bitcast.606), channel_id=1, replica_groups=mesh['fsdp'=16,'seq'=2] {'fsdp'}, dimensions={0}, use_global_device_ids=true | all-gather | bytes 52224 | tf_op jit(solution)/shard_map/all_gather | solution.py:258
  62.3 30.7 %all-gather.6.cloned.1.call-done = bf16[512,4096]{1,0:T(8,128)(2,1)} async-done(((bf16[64,4096]{1,0:T(8,128)(2,1)}), bf16[512,4096]{1,0:T(8,128)(2,1)}) %all-gather.6.cloned.1.call-update) | async-done | bytes 4194320 | tf_op jit(solution)/shard_map/all_gather | solution.py:62
  93.8 49.5 %all-gather.8.cloned.1.call-done = bf16[1024,1024]{1,0:T(8,128)(2,1)} async-done(((bf16[128,1024]{1,0:T(8,128)(2,1)}), bf16[1024,1024]{1,0:T(8,128)(2,1)}) %all-gather.8.cloned.1.call-update) | async-done | bytes 2097168 | tf_op jit(solution)/shard_map/all_gather | solution.py:62
  143.6 50.2 %all-gather.12.cloned.1.call-done = bf16[1024,1024]{1,0:T(8,128)(2,1)} async-done(((bf16[128,1024]{1,0:T(8,128)(2,1)}), bf16[1024,1024]{1,0:T(8,128)(2,1)}) %all-gather.12.cloned.1.call-update) | async-done | bytes 2097168 | tf_op jit(solution)/shard_map/all_gather | solution.py:62
  207.3 4.6 broadcast_select_fusion.7
  212.0 4.1 broadcast_select_fusion.5
  216.1 52.2 %all-gather.10.cloned.1.call-done = bf16[512,4096]{1,0:T(8,128)(2,1)} async-done(((bf16[64,4096]{1,0:T(8,128)(2,1)}), bf16[512,4096]{1,0:T(8,128)(2,1)}) %all-gather.10.cloned.1.call-update) | async-done | bytes 4194320 | tf_op jit(solution)/shard_map/all_gather | solution.py:62
  268.3 4.8 pad_maximum_fusion.2
  276.8 5.2 broadcast_select_fusion.3
  282.0 7.6 pad_maximum_fusion
  289.6 8.3 convolution_convert_fusion.2
  309.4 5.8 broadcast_select_fusion.1
  315.2 7.6 pad_maximum_fusion.1
  330.2 5.3 fusion.37
  340.8 4.8 fusion.14
  345.6 3.5 copy.304
  360.1 10.5 %fusion.227 = (f32[2,4,512]{2,1,0:T(4,128)}, f32[2,4,512,1024]{2,3,1,0:T(8,128)}) fusion(pred[512,1024]{0,1:T(8,128)(4,1)S(1)} %copy-done.73, bf16[1024,2,64,1]{0,2,3,1:T(8,128)(2,1)S(1)} %bitcast.569, bf16[512,2,4,64]{0,3,2,1:T(8,128)(2,1)S(1)} %bitcast.559), kind=kOutput, calls=%fused_computation.419 | convolution fusion | flops 553649152 | bytes 18104320 | tf_op jit(solution)/shard_map/sub | solution.py:292
  370.6 8.3 fusion.101
  381.1 6.0 bitcast_add_fusion
  387.1 3.9 multiply_reduce_fusion.11
  396.7 4.6 fusion.211
  401.3 6.5 bitcast_multiply_fusion.2
  407.8 6.0 add_convert_fusion
  413.8 9.4 %convolution_convert_fusion.1 = bf16[1024,4096]{1,0:T(8,128)(2,1)} fusion(bf16[512,4096]{1,0:T(8,128)(2,1)} %add_convert_fusion, f32[512,1024]{1,0:T(8,128)S(1)} %get-tuple-element.208, f32[1024]{0:T(1024)S(1)} %bitcast.583, f32[512]{0:T(512)S(1)} %fusion.195), kind=kOutput, calls=%fused_computation.23 | convolution fusion | flops 4300734464 | bytes 14686208 | tf_op jit(solution)/shard_map/dot_general | solution.py:106
  423.2 4.5 convolution_convert_fusion.4
  427.7 5.4 multiply_reduce_fusion.12
  435.8 4.4 convolution_convert_fusion.3
  445.1 10.5 %fusion.1 = (f32[2,4,512]{2,1,0:T(4,128)S(1)}, f32[2,1024,512,4]{2,1,3,0:T(8,128)}) fusion(f32[2,4,512,1024]{2,3,1,0:T(8,128)} %get-tuple-element.206, f32[2,4,512]{2,1,0:T(4,128)S(1)} %copy-done.132, bf16[1024,2,64,1]{0,2,3,1:T(8,128)(2,1)S(1)} %bitcast.576, bf16[512,2,4,64]{0,3,2,1:T(8,128)(2,1)S(1)} %bitcast.571), kind=kOutput, calls=%fused_computation.3 | convolution fusion | flops 549449728 | bytes 34373632 | tf_op jit(solution)/shard_map/tkgd,ckd->kgtc/dot_general | solution.py:385
  455.6 9.1 %fusion.108 = bf16[2,64,1024]{2,1,0:T(8,128)(2,1)} fusion(bf16[512,2,4,64]{0,3,2,1:T(8,128)(2,1)S(1)} %bitcast.572, f32[2,4,512,1024]{2,3,1,0:T(8,128)} %get-tuple-element.206, f32[2,4,512]{2,1,0:T(4,128)S(1)} %copy-done.132), kind=kOutput, calls=%fused_computation.198 | convolution fusion | flops 545390592 | bytes 17580032 | tf_op jit(solution)/shard_map/kgtc,tkgd->ckd/dot_general | solution.py:398
  464.8 11.6 %fusion.3 = bf16[2,4,512,1024]{2,3,1,0:T(8,128)(2,1)S(1)} fusion(f32[2,1024,512,4]{2,1,3,0:T(8,128)} %get-tuple-element.212, f32[2,4,512]{2,1,0:T(4,128)S(1)} %get-tuple-element.211, f32[2,4,512,1024]{2,3,1,0:T(8,128)} %get-tuple-element.206, f32[2,4,512]{2,1,0:T(4,128)S(1)} %copy-done.132), kind=kLoop, calls=%fused_computation.5 | loop fusion | flops 16777216 | bytes 41975808 | tf_op jit(solution)/shard_map/convert_element_type | solution.py:389
  476.4 3.3 fusion.111
  482.9 3.9 multiply_reduce_fusion.6
  488.5 3.5 reshape.1319
  492.0 6.5 multiply_reduce_fusion.8
  499.9 7.2 fusion.33
  520.5 3.4 collective-permute-start.11
  523.8 4.9 dynamic-slice_bitcast_fusion.1
  528.7 4.9 fusion.43
  533.6 2.8 fusion.25
  540.5 4.8 fusion.118
  545.3 4.1 fusion.13
  549.4 3.6 copy.319
  553.0 3.6 copy.324
  556.6 3.0 reduce_sum.344
  567.2 3.9 multiply_reduce_fusion.17
  574.9 6.0 multiply_add_fusion.1
  580.9 3.6 copy.323
  596.3 3.2 fusion.121
  602.2 5.1 multiply_reduce_fusion.5
  610.2 2.9 pad_add_fusion
  613.1 7.2 fusion.6
  625.4 6.7 concatenate.68
  632.1 7.5 convolution_convert_fusion
  640.4 7.0 collective-permute-done.14
  647.3 3.1 fusion.5
  652.2 6.5 fusion.99
  660.8 10.0 %fusion.71 = (f32[1024]{0:T(1024)S(1)}, f32[512]{0:T(512)S(1)}, f32[512,1024]{1,0:T(8,128)}) fusion(bf16[1,512,1024]{2,1,0:T(8,128)(2,1)S(1)} %copy-done.42, f32[512]{0:T(512)S(1)} %copy-done.136, f32[1024]{0:T(1024)S(1)} %bitcast.602, f32[512,1024]{1,0:T(8,128)S(1)} %fusion.229, bf16[1024,4096]{1,0:T(8,128)(2,1)} %bitcast.528, ...), kind=kOutput, calls=%fused_computation.147 | convolution fusion | flops 4315937280 | bytes 17838080 | tf_op jit(solution)/shard_map/dot_general | solution.py:100
  670.8 42.8 %all-reduce.31 = (f32[2,1024]{1,0:T(2,128)}, f32[5,1792]{1,0:T(8,128)}, f32[1536]{0:T(1024)}, f32[3,24]{1,0:T(4,128)}) all-reduce(f32[2,1024]{1,0:T(2,128)S(1)} %pad_maximum_fusion.10, f32[5,1792]{1,0:T(8,128)S(1)} %copy-done.82, f32[1536]{0:T(1024)S(1)} %copy-done.114, ...), channel_id=1, replica_groups=mesh['fsdp'=16,'seq'=2] {'fsdp','seq'}, use_global_device_ids=true, to_apply=%region_29.30 | all-reduce | flops 12616 | bytes 100928 | tf_op jit(solution)/shard_map/psum | solution.py:442
  717.0 5.0 fusion.78
  726.2 84.3 %reduce-scatter.4.cloned.1.call-done = bf16[64,4224]{1,0:T(8,128)(2,1)} async-done(((bf16[512,4224]{1,0:T(8,128)(2,1)}), bf16[64,4224]{1,0:T(8,128)(2,1)}) %reduce-scatter.4.cloned.1.call-update) | async-done | bytes 540688 | tf_op jit(solution)/shard_map/reduce_scatter | solution.py:82
  815.8 5.2 collective-permute-done.15
  (516 shorter events, 163.3 us)
Async XLA Ops:
  7.2 52.6 %copy-start.96 = (s32[1,512]{1,0:T(1,128)S(1)}, s32[1,512]{1,0:T(1,128)}, u32[]{:S(2)}) copy-start(s32[1,512]{1,0:T(1,128)} %param.14) | copy-start | bytes 6148
  7.2 53.0 %copy-start.39 = (bf16[1,512,1024]{2,1,0:T(8,128)(2,1)S(1)}, bf16[1,512,1024]{2,1,0:T(8,128)(2,1)}, u32[]{:S(2)}) copy-start(bf16[1,512,1024]{2,1,0:T(8,128)(2,1)} %param.12) | copy-start | bytes 3145732
  7.2 85.8 %all-gather.6.cloned.1.call-start = ((), (), s32[]{:S(2)}) async-start(), calls=%async_computation.3 | async-start | bytes 4718592 | tf_op jit(solution)/shard_map/all_gather | solution.py:62
  7.3 9.6 %collective-permute-start = (bf16[64,2048]{1,0:T(8,128)(2,1)}, bf16[64,2048]{1,0:T(8,128)(2,1)S(1)}, u32[]{:S(2)}, u32[]{:S(2)}) collective-permute-start(bf16[64,2048]{1,0:T(8,128)(2,1)} %param.15), channel_id=1, source_target_pairs={{0,1},{1,0},{2,3},{3,2},{4,5},{5,4},{6,7},{7,6},{8,9},{9,8},{10,11... | collective-permute-start | bytes 786440 | tf_op jit(solution)/shard_map/ppermute | solution.py:120
  10.3 50.2 %copy-start.155 = (f32[3,24]{1,0:T(4,128)S(1)}, f32[3,24]{1,0:T(4,128)}, u32[]{:S(2)}) copy-start(f32[3,24]{1,0:T(4,128)} %param.23) | copy-start | bytes 868
  10.4 50.2 %copy-start.138 = (f32[2,1024]{1,0:T(2,128)S(1)}, f32[2,1024]{1,0:T(2,128)}, u32[]{:S(2)}) copy-start(f32[2,1024]{1,0:T(2,128)} %param.20) | copy-start | bytes 24580
  17.7 125.6 %all-gather.8.cloned.1.call-start = ((), (), s32[]{:S(2)}) async-start(), calls=%async_computation.4 | async-start | bytes 2359296 | tf_op jit(solution)/shard_map/all_gather | solution.py:62
  17.7 5.2 collective-permute-start.5
  23.7 170.1 %all-gather.12.cloned.1.call-start = ((), (), s32[]{:S(2)}) async-start(), calls=%async_computation.6 | async-start | bytes 2359296 | tf_op jit(solution)/shard_map/all_gather | solution.py:62
  23.8 5.2 collective-permute-start.9
  29.7 238.5 %all-gather.10.cloned.1.call-start = ((), (), s32[]{:S(2)}) async-start(), calls=%async_computation.5 | async-start | bytes 4718592 | tf_op jit(solution)/shard_map/all_gather | solution.py:62
  29.8 6.4 collective-permute-start.7
  37.1 676.6 %reduce-scatter.6.cloned.1.call-start = ((), (), s32[]{:S(2)}) async-start(), calls=%async_computation.8 | async-start | bytes 4718592 | tf_op jit(solution)/shard_map/reduce_scatter | solution.py:82
  59.8 135.3 %copy-start.83 = (bf16[1024,24]{0,1:T(8,128)(2,1)}, bf16[1024,24]{0,1:T(8,128)(2,1)S(1)}, u32[]{:S(2)}) copy-start(bf16[1024,24]{0,1:T(8,128)(2,1)S(1)} %reshape.1349) | copy-start | bytes 147460
  60.2 135.1 %copy-start.145 = (f32[4]{0:T(128)}, f32[4]{0:T(128)S(1)}, u32[]{:S(2)}) copy-start(f32[4]{0:T(128)S(1)} %convert_reduce_fusion) | copy-start | bytes 52
  60.5 134.8 %copy-start.144 = (f32[24]{0:T(128)}, f32[24]{0:T(128)S(1)}, u32[]{:S(2)}) copy-start(f32[24]{0:T(128)S(1)} %get-tuple-element.189) | copy-start | bytes 292
  60.6 229.0 %copy-start.135 = (f32[512]{0:T(512)}, f32[512]{0:T(512)S(1)}, u32[]{:S(2)}) copy-start(f32[512]{0:T(512)S(1)} %fusion.193) | copy-start | bytes 6148
  60.6 229.0 %copy-start.129 = (f32[1,1024]{1,0:T(1,128)}, f32[1,1024]{1,0:T(1,128)S(1)}, u32[]{:S(2)}) copy-start(f32[1,1024]{1,0:T(1,128)S(1)} %get-tuple-element.181) | copy-start | bytes 12292
  60.6 372.5 %copy-start.102 = (f32[1,1024]{1,0:T(1,128)}, f32[1,1024]{1,0:T(1,128)S(1)}, u32[]{:S(2)}) copy-start(f32[1,1024]{1,0:T(1,128)S(1)} %get-tuple-element.180) | copy-start | bytes 12292
  93.0 182.6 %collective-permute-start.1 = (bf16[512,4096]{1,0:T(8,128)(2,1)}, bf16[512,4096]{1,0:T(8,128)(2,1)}, u32[]{:S(2)}, u32[]{:S(2)}) collective-permute-start(bf16[512,4096]{1,0:T(8,128)(2,1)} %all-gather.6.cloned.1.call-done), channel_id=1, source_target_pairs={{0,2},{2,0},{4,6},{6,4},{8,10},{10,8},{12,14},{14,12},{16,18},{18,... | collective-permute-start | bytes 12582920 | tf_op jit(solution)/shard_map/ppermute | solution.py:51
  93.5 247.3 %copy-start.60 = (f32[4,24,128]{2,1,0:T(8,128)}, f32[4,24,128]{2,1,0:T(8,128)S(1)}, u32[]{:S(2)}) copy-start(f32[4,24,128]{2,1,0:T(8,128)S(1)} %fusion.149) | copy-start | bytes 147460
  93.7 104.1 %copy-start.113 = (f32[4,24]{1,0:T(4,128)}, f32[4,24]{1,0:T(4,128)S(1)}, u32[]{:S(2)}) copy-start(f32[4,24]{1,0:T(4,128)S(1)} %get-tuple-element.128) | copy-start | bytes 1156
  93.7 104.1 %copy-start.128 = (f32[4,24]{1,0:T(4,128)}, f32[4,24]{1,0:T(4,128)S(1)}, u32[]{:S(2)}) copy-start(f32[4,24]{1,0:T(4,128)S(1)} %get-tuple-element.127) | copy-start | bytes 1156
  93.8 104.0 %copy-start.104 = (f32[4,128]{1,0:T(4,128)}, f32[4,128]{1,0:T(4,128)S(1)}, u32[]{:S(2)}) copy-start(f32[4,128]{1,0:T(4,128)S(1)} %get-tuple-element.218) | copy-start | bytes 6148
  93.8 104.0 %copy-start.124 = (f32[4,128]{1,0:T(4,128)}, f32[4,128]{1,0:T(4,128)S(1)}, u32[]{:S(2)}) copy-start(f32[4,128]{1,0:T(4,128)S(1)} %get-tuple-element.219) | copy-start | bytes 6148
  143.3 64.0 %collective-permute-start.6 = (bf16[1024,1024]{1,0:T(8,128)(2,1)}, bf16[1024,1024]{1,0:T(8,128)(2,1)}, u32[]{:S(2)}, u32[]{:S(2)}) collective-permute-start(bf16[1024,1024]{1,0:T(8,128)(2,1)} %all-gather.8.cloned.1.call-done), channel_id=1, source_target_pairs={{0,2},{2,0},{4,6},{6,4},{8,10},{10,8},{12,14},{14,12},{16,18},{18,... | collective-permute-start | bytes 6291464 | tf_op jit(solution)/shard_map/ppermute | solution.py:51
  143.3 54.4 %copy-start.127 = (f32[1,4,24]{2,1,0:T(4,128)}, f32[1,4,24]{2,1,0:T(4,128)S(1)}, u32[]{:S(2)}) copy-start(f32[1,4,24]{2,1,0:T(4,128)S(1)} %bitcast_multiply_fusion.10) | copy-start | bytes 1156
  143.4 51.7 %copy-start.70 = (f32[1,4,128,24]{2,3,1,0:T(8,128)}, f32[1,4,128,24]{2,3,1,0:T(8,128)S(1)}, u32[]{:S(2)}) copy-start(f32[1,4,128,24]{2,3,1,0:T(8,128)S(1)} %copy.300) | copy-start | bytes 147460
  193.8 18.2 %collective-permute-start.10 = (bf16[1024,1024]{1,0:T(8,128)(2,1)}, bf16[1024,1024]{1,0:T(8,128)(2,1)}, u32[]{:S(2)}, u32[]{:S(2)}) collective-permute-start(bf16[1024,1024]{1,0:T(8,128)(2,1)} %all-gather.12.cloned.1.call-done), channel_id=1, source_target_pairs={{0,2},{2,0},{4,6},{6,4},{8,10},{10,8},{12,14},{14,12},{16,18},{18,... | collective-permute-start | bytes 6291464 | tf_op jit(solution)/shard_map/ppermute | solution.py:51
  194.4 160.5 %copy-start.133 = (f32[24]{0:T(128)}, f32[24]{0:T(128)S(1)}, u32[]{:S(2)}) copy-start(f32[24]{0:T(128)S(1)} %get-tuple-element.195) | copy-start | bytes 292
  197.9 183.1 %copy-start.94 = (f32[1536]{0:T(1024)}, f32[1536]{0:T(1024)S(1)}, u32[]{:S(2)}) copy-start(f32[1536]{0:T(1024)S(1)} %mul.1040) | copy-start | bytes 18436
  202.2 146.9 %copy-start.7 = (f32[1,4,128,1536]{3,2,1,0:T(8,128)}, f32[1,4,128,1536]{3,2,1,0:T(8,128)S(1)}, u32[]{:S(2)}) copy-start(f32[1,4,128,1536]{3,2,1,0:T(8,128)S(1)} %copy.301) | copy-start | bytes 9437188
  204.1 126.1 %copy-start.86 = (f32[1792]{0:T(1024)}, f32[1792]{0:T(1024)S(1)}, u32[]{:S(2)}) copy-start(f32[1792]{0:T(1024)S(1)} %get-tuple-element.123) | copy-start | bytes 21508
  204.1 126.1 %copy-start.88 = (f32[1792]{0:T(1024)}, f32[1792]{0:T(1024)S(1)}, u32[]{:S(2)}) copy-start(f32[1792]{0:T(1024)S(1)} %get-tuple-element.124) | copy-start | bytes 21508
  204.1 126.1 %copy-start.90 = (f32[1792]{0:T(1024)}, f32[1792]{0:T(1024)S(1)}, u32[]{:S(2)}) copy-start(f32[1792]{0:T(1024)S(1)} %get-tuple-element.125) | copy-start | bytes 21508
  204.1 126.1 %copy-start.92 = (f32[1792]{0:T(1024)}, f32[1792]{0:T(1024)S(1)}, u32[]{:S(2)}) copy-start(f32[1792]{0:T(1024)S(1)} %get-tuple-element.126) | copy-start | bytes 21508
  204.1 126.1 %copy-start.105 = (f32[1,1,512]{2,0,1:T(1,128)}, f32[1,1,512]{2,0,1:T(1,128)S(1)}, u32[]{:S(2)}) copy-start(f32[1,1,512]{2,0,1:T(1,128)S(1)} %get-tuple-element.182) | copy-start | bytes 6148
  204.2 126.1 %copy-start.107 = (f32[1,1,512]{2,0,1:T(1,128)}, f32[1,1,512]{2,0,1:T(1,128)S(1)}, u32[]{:S(2)}) copy-start(f32[1,1,512]{2,0,1:T(1,128)S(1)} %get-tuple-element.183) | copy-start | bytes 6148
  204.2 126.1 %copy-start.109 = (f32[1,1,512]{2,0,1:T(1,128)}, f32[1,1,512]{2,0,1:T(1,128)S(1)}, u32[]{:S(2)}) copy-start(f32[1,1,512]{2,0,1:T(1,128)S(1)} %get-tuple-element.184) | copy-start | bytes 6148
  204.2 126.1 %copy-start.111 = (f32[1,1,512]{2,0,1:T(1,128)}, f32[1,1,512]{2,0,1:T(1,128)S(1)}, u32[]{:S(2)}) copy-start(f32[1,1,512]{2,0,1:T(1,128)S(1)} %get-tuple-element.185) | copy-start | bytes 6148
  268.3 41.1 %collective-permute-start.8 = (bf16[512,4096]{1,0:T(8,128)(2,1)}, bf16[512,4096]{1,0:T(8,128)(2,1)}, u32[]{:S(2)}, u32[]{:S(2)}) collective-permute-start(bf16[512,4096]{1,0:T(8,128)(2,1)} %all-gather.10.cloned.1.call-done), channel_id=1, source_target_pairs={{0,2},{2,0},{4,6},{6,4},{8,10},{10,8},{12,14},{14,12},{16,18},{18,... | collective-permute-start | bytes 12582920 | tf_op jit(solution)/shard_map/ppermute | solution.py:51
  301.7 54.8 %collective-permute-start.2 = (bf16[512,256]{1,0:T(8,128)(2,1)}, bf16[512,256]{1,0:T(8,128)(2,1)}, u32[]{:S(2)}, u32[]{:S(2)}) collective-permute-start(bf16[512,256]{1,0:T(8,128)(2,1)} %slice.213), channel_id=1, source_target_pairs={{0,1},{1,0},{2,3},{3,2},{4,5},{5,4},{6,7},{7,6},{8,9},{9,8},{10,11... | collective-permute-start | bytes 786440 | tf_op jit(solution)/shard_map/ppermute | solution.py:120
  306.7 21.6 %collective-permute-start.3 = (bf16[1,3,1792]{2,1,0:T(4,128)(2,1)}, bf16[1,3,1792]{2,1,0:T(4,128)(2,1)S(1)}, u32[]{:S(2)}, u32[]{:S(2)}) collective-permute-start(bf16[1,3,1792]{2,1,0:T(4,128)(2,1)} %slice.218), channel_id=1, source_target_pairs={{0,1},{2,3},{4,5},{6,7},{8,9},{10,11},{12,13},{14,15},{16,17},{18,... | collective-permute-start | bytes 32264 | tf_op jit(solution)/shard_map/ppermute | solution.py:28
  353.5 27.5 %collective-permute-start.4 = (bf16[1,24,64,128]{3,2,1,0:T(8,128)(2,1)}, bf16[1,24,64,128]{3,2,1,0:T(8,128)(2,1)S(1)}, u32[]{:S(2)}, u32[]{:S(2)}) collective-permute-start(bf16[1,24,64,128]{3,2,1,0:T(8,128)(2,1)} %get-tuple-element.145), channel_id=1, source_target_pairs={{0,1},{2,3},{4,5},{6,7},{8,9},{10,11},{12,13},{14,15},{16,17},{18,... | collective-permute-start | bytes 1179656 | tf_op jit(solution)/shard_map/ppermute | solution.py:28
  391.0 51.5 %copy-start.2 = (f32[512,1536]{1,0:T(8,128)}, f32[512,1536]{1,0:T(8,128)S(1)}, u32[]{:S(2)}) copy-start(f32[512,1536]{1,0:T(8,128)S(1)} %get-tuple-element.142) | copy-start | bytes 9437188
  396.1 37.0 %copy-start.23 = (f32[512,1024]{1,0:T(8,128)}, f32[512,1024]{1,0:T(8,128)S(1)}, u32[]{:S(2)}) copy-start(f32[512,1024]{1,0:T(8,128)S(1)} %get-tuple-element.208) | copy-start | bytes 6291460
  498.5 67.6 %collective-permute-start.12 = (bf16[1,24,64,128]{3,2,1,0:T(8,128)(2,1)}, bf16[1,24,64,128]{3,2,1,0:T(8,128)(2,1)}, u32[]{:S(2)}, u32[]{:S(2)}) collective-permute-start(bf16[1,24,64,128]{3,2,1,0:T(8,128)(2,1)} %bitcast.103), channel_id=1, source_target_pairs={{1,0},{3,2},{5,4},{7,6},{9,8},{11,10},{13,12},{15,14},{17,16},{19,... | collective-permute-start | bytes 1179656 | tf_op jit(solution)/shard_map/ppermute | solution.py:28
  512.0 21.6 %collective-permute-start.17 = (bf16[8,128,1024]{2,1,0:T(8,128)(2,1)}, bf16[8,128,1024]{2,1,0:T(8,128)(2,1)}, u32[]{:S(2)}, u32[]{:S(2)}) collective-permute-start(bf16[8,128,1024]{2,1,0:T(8,128)(2,1)} %dynamic-slice_bitcast_fusion.2), channel_id=1, source_target_pairs={{0,2},{2,0},{4,6},{6,4},{8,10},{10,8},{12,14},{14,12},{16,18},{18,... | collective-permute-start | bytes 6291464 | tf_op jit(solution)/shard_map/ppermute | solution.py:51
  516.5 19.9 %collective-permute-start.16 = (bf16[8,128,1024]{2,1,0:T(8,128)(2,1)}, bf16[8,128,1024]{2,1,0:T(8,128)(2,1)S(1)}, u32[]{:S(2)}, u32[]{:S(2)}) collective-permute-start(bf16[8,128,1024]{2,1,0:T(8,128)(2,1)} %dynamic-slice_bitcast_fusion.3), channel_id=1, source_target_pairs={{0,2},{2,0},{4,6},{6,4},{8,10},{10,8},{12,14},{14,12},{16,18},{18,... | collective-permute-start | bytes 6291464 | tf_op jit(solution)/shard_map/ppermute | solution.py:51
  520.5 43.9 %collective-permute-start.11 = (bf16[512,256]{1,0:T(8,128)(2,1)}, bf16[512,256]{1,0:T(8,128)(2,1)}, u32[]{:S(2)}, u32[]{:S(2)}) collective-permute-start(bf16[512,256]{1,0:T(8,128)(2,1)} %fusion.140), channel_id=1, source_target_pairs={{0,1},{1,0},{2,3},{3,2},{4,5},{5,4},{6,7},{7,6},{8,9},{9,8},{10,11... | collective-permute-start | bytes 786440 | tf_op jit(solution)/shard_map/ppermute | solution.py:132
  539.9 183.7 %reduce-scatter.8.cloned.1.call-start = ((), (), s32[]{:S(2)}) async-start(), calls=%async_computation.9 | async-start | bytes 4718592 | tf_op jit(solution)/shard_map/reduce_scatter | solution.py:82
  562.4 50.8 %collective-permute-start.19 = (bf16[8,64,4096]{2,1,0:T(8,128)(2,1)}, bf16[8,64,4096]{2,1,0:T(8,128)(2,1)}, u32[]{:S(2)}, u32[]{:S(2)}) collective-permute-start(bf16[8,64,4096]{2,1,0:T(8,128)(2,1)} %dynamic-slice_bitcast_fusion.1), channel_id=1, source_target_pairs={{0,2},{2,0},{4,6},{6,4},{8,10},{10,8},{12,14},{14,12},{16,18},{18,... | collective-permute-start | bytes 12582920 | tf_op jit(solution)/shard_map/ppermute | solution.py:51
  608.9 13.3 %collective-permute-start.13 = (f32[1,3,1792]{2,1,0:T(4,128)S(1)}, f32[1,3,1792]{2,1,0:T(4,128)}, u32[]{:S(2)}, u32[]{:S(2)}) collective-permute-start(f32[1,3,1792]{2,1,0:T(4,128)S(1)} %pad_add_fusion.4), channel_id=1, source_target_pairs={{1,0},{3,2},{5,4},{7,6},{9,8},{11,10},{13,12},{15,14},{17,16},{19,... | collective-permute-start | bytes 64520 | tf_op jit(solution)/shard_map/ppermute | solution.py:28
  620.4 190.1 %reduce-scatter.4.cloned.1.call-start = ((), (), s32[]{:S(2)}) async-start(), calls=%async_computation.7 | async-start | bytes 4866048 | tf_op jit(solution)/shard_map/reduce_scatter | solution.py:82
  639.9 7.4 collective-permute-start.14
  660.7 52.9 %copy-start.126 = (f32[512]{0:T(512)S(1)}, f32[512]{0:T(512)}, u32[]{:S(2)}) copy-start(f32[512]{0:T(512)} %copy-done.125) | copy-start | bytes 6148
  660.7 56.2 %copy-start.103 = (f32[1,1024]{1,0:T(1,128)S(1)}, f32[1,1024]{1,0:T(1,128)}, u32[]{:S(2)}) copy-start(f32[1,1024]{1,0:T(1,128)} %copy-done.102) | copy-start | bytes 12292
  660.7 56.2 %copy-start.121 = (f32[512]{0:T(512)S(1)}, f32[512]{0:T(512)}, u32[]{:S(2)}) copy-start(f32[512]{0:T(512)} %copy-done.120) | copy-start | bytes 6148
  660.7 56.2 %copy-start.123 = (f32[512]{0:T(512)S(1)}, f32[512]{0:T(512)}, u32[]{:S(2)}) copy-start(f32[512]{0:T(512)} %copy-done.122) | copy-start | bytes 6148
  660.7 56.2 %copy-start.131 = (f32[1,1024]{1,0:T(1,128)S(1)}, f32[1,1024]{1,0:T(1,128)}, u32[]{:S(2)}) copy-start(f32[1,1024]{1,0:T(1,128)} %copy-done.129) | copy-start | bytes 12292
  660.7 56.2 %copy-start.137 = (f32[512]{0:T(512)S(1)}, f32[512]{0:T(512)}, u32[]{:S(2)}) copy-start(f32[512]{0:T(512)} %copy-done.135) | copy-start | bytes 6148
  714.6 8.1 collective-permute-start.18
  724.6 89.4 %collective-permute-start.20 = (bf16[64,2048]{1,0:T(8,128)(2,1)S(1)}, bf16[64,2048]{1,0:T(8,128)(2,1)S(1)}, u32[]{:S(2)}, u32[]{:S(2)}) collective-permute-start(bf16[64,2048]{1,0:T(8,128)(2,1)S(1)} %constant_dynamic-slice_fusion), channel_id=1, source_target_pairs={{0,1},{1,0},{2,3},{3,2},{4,5},{5,4},{6,7},{7,6},{8,9},{9,8},{10,11... | collective-permute-start | bytes 786440 | tf_op jit(solution)/shard_map/ppermute | solution.py:132
  812.4 8.5 %collective-permute-start.15 = (bf16[64,2176]{1,0:T(8,128)(2,1)S(1)}, bf16[64,2176]{1,0:T(8,128)(2,1)S(1)}, u32[]{:S(2)}, u32[]{:S(2)}) collective-permute-start(bf16[64,2176]{1,0:T(8,128)(2,1)S(1)} %pad_maximum_fusion.8), channel_id=1, source_target_pairs={{0,1},{1,0},{2,3},{3,2},{4,5},{5,4},{6,7},{7,6},{8,9},{9,8},{10,11... | collective-permute-start | bytes 835592 | tf_op jit(solution)/shard_map/ppermute | solution.py:132
  (124 other events, 749.3 us)
Sparse Core Ops, SparseCore 0:
  17.8 75.1 all-gather.5
  95.7 47.5 all-gather.7
  146.0 47.7 all-gather.11
  196.3 71.8 all-gather.9
  540.0 85.2 reduce-scatter.5
  629.2 88.2 reduce-scatter.7
  721.1 89.3 reduce-scatter.3

commit v3 on v2

--- a/solution.py
+++ b/solution.py
@@ -46,46 +46,8 @@
     return state
 
 
-def other_core(block):
-    route = [(d, d + 1 - 2 * (d % 2)) for d in range(lax.axis_size("fsdp"))]
-    return lax.ppermute(block, "fsdp", route)
-
-
-def same_core():
-    count = lax.axis_size("fsdp")
-    return [list(range(0, count, 2)), list(range(1, count, 2))]
-
-
-def chip_gather(block):
-    rows, cols = block.shape
-    chips = lax.axis_size("fsdp") // 2
-    own = lax.all_gather(block, "fsdp", axis=0, tiled=True, axis_index_groups=same_core())
-    other = other_core(own)
-    first = lax.axis_index("fsdp") % 2 == 0
-    even = jnp.where(first, own, other).reshape(chips, 1, rows, cols)
-    odd = jnp.where(first, other, own).reshape(chips, 1, rows, cols)
-    return jnp.concatenate([even, odd], axis=1).reshape(2 * chips * rows, cols)
-
-
-def core_sums(grad):
-    chips = lax.axis_size("fsdp") // 2
-    rows = grad.shape[0] // (2 * chips)
-    split = grad.reshape(chips, 2, rows, grad.shape[1])
-    core = lax.axis_index("fsdp") % 2
-    mine = lax.dynamic_index_in_dim(split, core, 1, False)
-    came = other_core(lax.dynamic_index_in_dim(split, 1 - core, 1, False))
-    return (mine.astype(jnp.float32) + came.astype(jnp.float32)).astype(jnp.bfloat16)
-
-
-def chip_scatter(sums):
-    chips, rows, cols = sums.shape
-    return lax.psum_scatter(
-        sums.reshape(chips * rows, cols),
-        "fsdp",
-        scatter_dimension=0,
-        axis_index_groups=same_core(),
-        tiled=True,
-    )
+def row_scatter(grad):
+    return lax.psum_scatter(grad, "fsdp", scatter_dimension=0, tiled=True)
 
 
 def rms_norm(values, gain):
@@ -254,11 +216,11 @@
         seq_gather(w_down, 1),
     )
     full_in, full_dt, full_out, full_gu, full_down = (
-        chip_gather(cols_in),
+        lax.all_gather(cols_in, "fsdp", axis=0, tiled=True),
         lax.all_gather(w_dt, "fsdp", axis=0, tiled=True),
-        chip_gather(cols_out),
-        chip_gather(cols_gu),
-        chip_gather(cols_down),
+        lax.all_gather(cols_out, "fsdp", axis=0, tiled=True),
+        lax.all_gather(cols_gu, "fsdp", axis=0, tiled=True),
+        lax.all_gather(cols_down, "fsdp", axis=0, tiled=True),
     )
     hidden = tokens.reshape(num_rows, model_width).astype(jnp.float32)
     normed_f, norm1_back = jax.vjp(rms_norm, hidden, norm_gains[0])
@@ -365,16 +327,15 @@
     grad_gu, grad_down, d_paired = lax.optimization_barrier(
         (grad_gu.astype(jnp.bfloat16), grad_down.astype(jnp.bfloat16), d_paired)
     )
-    share_gu = chip_scatter(core_sums(grad_gu))
+    share_gu = row_scatter(grad_gu)
     d_normed2 = times_rows(d_paired, full_gu)
     d_second, d_gain2 = norm2_back(d_normed2)
     d_second = d_second + upstream.astype(jnp.float32)
     d_mixed = d_second.astype(jnp.bfloat16)
     grad_out = outer_total(mixed_in, d_mixed)
-    grad_out, d_mixed = lax.optimization_barrier((grad_out.astype(jnp.bfloat16), d_mixed))
-    share_pair = chip_scatter(
-        jnp.concatenate([core_sums(grad_down), core_sums(grad_out)], axis=1)
-    )
+    grad_pair = jnp.concatenate([grad_down, grad_out.astype(jnp.bfloat16)], axis=1)
+    grad_pair, d_mixed = lax.optimization_barrier((grad_pair, d_mixed))
+    share_pair = row_scatter(grad_pair)
     d_mixed_in = times_rows(d_mixed, full_out)
     d_attended = (
         d_mixed_in[:, :q_width]
@@ -424,15 +385,22 @@
     d_dt_low = d_dt_raw.reshape(num_rows, SSM_HEADS).astype(jnp.bfloat16)
     pad = jnp.zeros((num_rows, 128 - SSM_HEADS), jnp.bfloat16)
     grad_in = outer_total(normed, jnp.concatenate([d_projected, d_dt_low, pad], axis=1))
-    share_in = chip_scatter(core_sums(grad_in.astype(jnp.bfloat16)))
+    share_in = row_scatter(grad_in.astype(jnp.bfloat16))
     d_normed = times_rows(d_projected, full_in) + times_rows(d_dt_low, full_dt)
     d_hidden, d_gain1 = norm1_back(d_normed)
     d_hidden = d_hidden + d_second
     width = model_width // lax.axis_size("seq")
     in_width = share_gu.shape[1] // lax.axis_size("seq")
     total_gu = seq_scatter(lambda k: columns(share_gu, k, in_width))
-    total_pair = seq_scatter(lambda k: columns(share_pair, k, width))
-    pair_rows = total_pair.shape[0] // 2
+    total_pair = seq_scatter(
+        lambda k: jnp.concatenate(
+            [
+                columns(share_pair[:, :model_width], k, width),
+                columns(share_pair[:, model_width:], k, width),
+            ],
+            axis=1,
+        )
+    )
     in_cols = d_projected.shape[1]
     total_in = seq_scatter(
         lambda k: jnp.concatenate(
@@ -448,9 +416,9 @@
         d_hidden.reshape(num_seqs, span_len, model_width),
         total_in[:, :in_width],
         total_in[:, in_width : in_width + SSM_HEADS],
-        total_pair[pair_rows:],
+        total_pair[:, width:],
         total_gu,
-        total_pair[:pair_rows],
+        total_pair[:, :width],
         summed_small[0],
         summed_small[1],
         summed_small[2],

time: 840 us -> 658 us (0.78)
  waiting for transfers between devices: 295 us -> 140 us
  other arithmetic: 153 us -> 92.9 us
  matrix products: 170 us -> 206 us
    all_gather x4, waiting for transfers between devices: 183 us -> 88.7 us  [the longest x1 39 us: body(): lax.all_gather(cols_down, 'fsdp', axis=0, tiled=True)]
    reduce_scatter x3, waiting for transfers between devices: 84.4 us -> 24.2 us  [row_scatter(): return lax.psum_scatter(grad, 'fsdp', scatter_dimension=0, tiled=True)]
    select_n x4 -> x0, other arithmetic: 19.7 us -> none  [chip_gather(): even = jnp.where(first, own, other).reshape(chips, 1, rows, cols)]
    concatenate x5 -> x2, other arithmetic: 25 us -> 8.75 us  [the longest x1 8.73 us: body(): jnp.concatenate([grad_down, grad_out.astype(jnp.bfloat16)], axis=1)]
    convert_element_type x4 -> x0, other arithmetic: 14.1 us -> none  [core_sums(): (mine.astype(jnp.float32) + came.astype(jnp.float32)).astype(jnp.bfloat16)]
    dot_general x5, matrix products: 24.6 us -> 38.2 us  [times_rows(): lax.dot_general(left, weight, (((1,), (1,)), ((), ())), preferred_element...]
    unnamed x322 -> x286, local copies, waits for them, and re-layouts: 21.5 us -> 21.8 us
  transfers between devices with their start and end apart: 28 -> 20, of which waited for: 12 -> 10; matrix products, arithmetic and copies ran while one was open for 35% -> 54% of each run, Pallas kernels for 0% -> 0%
where the time goes in v3:
time: 658 us; the launch traced here: 650 us
  matrix products  206 us (31%)
  waiting for transfers between devices  140 us (21%)
  local copies, waits for them, and re-layouts  103 us (16%)
  other arithmetic  92.9 us (14%)
  blocking collectives  67.4 us (10%)
  starting transfers between devices  24.3 us (4%)
  between operations  16 us (2%)
    psum x1, blocking collectives, body(): lax.psum((jnp.stack([d_gain1, d_gain2]), g_conv, g_ssm, g_head_out + g_he...  45.2 us
    all_gather x1, waiting for transfers between devices, body(): lax.all_gather(cols_down, 'fsdp', axis=0, tiled=True)  39 us
    dot_general x5, matrix products, times_rows(): lax.dot_general(left, weight, (((1,), (1,)), ((), ())), preferred_element...  38.2 us
    all_gather x1, waiting for transfers between devices, body(): lax.all_gather(cols_gu, 'fsdp', axis=0, tiled=True)  32.2 us
    dot_general x4, matrix products, outer_total(): lax.dot_general(left, right, (((0,), (0,)), ((), ())), preferred_element_...  27.3 us
    reduce_scatter x3, waiting for transfers between devices, row_scatter(): return lax.psum_scatter(grad, 'fsdp', scatter_dimension=0, tiled=True)  24.2 us
    all_gather x1, blocking collectives, body(): lax.all_gather(w_dt, 'fsdp', axis=0, tiled=True)  22.2 us
    unnamed x286, local copies, waits for them, and re-layouts  21.8 us
  transfers between devices with their start and end apart: 20, of which 10 were waited for; matrix products, arithmetic and copies ran while one was open for 54% of the time, Pallas kernels for 0%

profile of v3, /device:TPU:0, one launch (start us, length us, event | category | flops | bytes accessed | tf_op | source)
XLA Modules:
  0.0 649.6 jit_solution(7559946930827699024)
XLA Ops:
  7.3 3.0 collective-permute-start
  11.3 5.5 collective-permute-done
  20.5 2.5 collective-permute-done.4
  25.6 4.5 collective-permute-done.5
  32.9 22.2 %all-gather = bf16[16,64,24]{1,2,0:T(8,128)(2,1)S(1)} all-gather(bf16[1,64,24]{1,2,0:T(8,128)(2,1)S(1)} %bitcast.512), channel_id=1, replica_groups=mesh['fsdp'=16,'seq'=2] {'fsdp'}, dimensions={0}, use_global_device_ids=true | all-gather | bytes 52224 | tf_op jit(solution)/shard_map/all_gather | solution.py:220
  66.5 2.4 copy.297
  77.2 17.5 %all-gather.6.cloned.1.call-done = bf16[1024,4096]{1,0:T(8,128)(2,1)} async-done(((bf16[64,4096]{1,0:T(8,128)(2,1)}), bf16[1024,4096]{1,0:T(8,128)(2,1)}) %all-gather.6.cloned.1.call-update) | async-done | bytes 8388624 | tf_op jit(solution)/shard_map/all_gather | solution.py:219
  94.7 8.3 %convolution_convert_fusion.2 = bf16[512,4096]{1,0:T(8,128)(2,1)S(1)} fusion(bf16[1024,4096]{1,0:T(8,128)(2,1)} %all-gather.6.cloned.1.call-done, bf16[1,512,1024]{2,1,0:T(8,128)(2,1)} %param.12, f32[1024]{0:T(1024)S(1)} %bitcast.506, f32[512]{0:T(512)S(1)} %copy-done.116), kind=kOutput, calls=%fused_computation.28 | convolution fusion | flops 4299161600 | bytes 13637632 | tf_op jit(solution)/shard_map/dot_general | solution.py:228
  110.3 2.6 collective-permute-start.2
  120.4 5.3 fusion.33
  128.3 2.7 copy.288
  131.0 4.9 fusion.12
  135.9 3.6 copy.298
  139.6 2.6 fusion.42
  150.6 10.1 %fusion.214 = (f32[2,4,512]{2,1,0:T(4,128)}, f32[2,4,512,1024]{2,3,1,0:T(8,128)}) fusion(pred[512,1024]{0,1:T(8,128)(4,1)S(1)} %copy-done.56, bf16[1024,2,64,1]{0,2,3,1:T(8,128)(2,1)S(1)} %bitcast.475, bf16[512,2,4,64]{0,3,2,1:T(8,128)(2,1)S(1)} %bitcast.466), kind=kOutput, calls=%fused_computation.393 | convolution fusion | flops 553649152 | bytes 18104320 | tf_op jit(solution)/shard_map/sub | solution.py:254
  160.7 8.4 %fusion.90 = bf16[2,64,4,512]{3,1,2,0:T(8,128)(2,1)} fusion(bf16[1024,2,64,1]{0,2,3,1:T(8,128)(2,1)} %bitcast.481, f32[2,4,512,1024]{2,3,1,0:T(8,128)} %get-tuple-element.204, f32[2,4,512]{2,1,0:T(4,128)} %get-tuple-element.203), kind=kOutput, calls=%fused_computation.166 | convolution fusion | flops 545521664 | bytes 17580032 | tf_op jit(solution)/shard_map/kgtc,ckd->tkgd/dot_general | solution.py:258
  171.2 6.4 bitcast_add_fusion
  177.6 3.9 multiply_reduce_fusion.11
  183.2 6.7 %multiply_reduce_fusion.14 = (f32[512]{0:T(512)S(1)}, f32[512,1024]{1,0:T(8,128)}) fusion(bf16[2048,1024]{1,0:T(8,128)(2,1)} %all-gather.8.cloned.1.call-done, bf16[512,1536]{1,0:T(8,128)(2,1)} %multiply_convert_fusion.1, bf16[512,512]{1,0:T(8,128)(2,1)} %copy.299, bf16[1,512,1024]{2,1,0:T(8,128)(2,1)} %param.12), kind=kOutput, calls=%fused_computation.138 | convolution fusion | flops 2153774592 | bytes 9439232 | tf_op jit(solution)/shard_map/dot_general | solution.py:315
  190.0 32.2 %all-gather.10.cloned.1.call-done = bf16[1024,4096]{1,0:T(8,128)(2,1)} async-done(((bf16[64,4096]{1,0:T(8,128)(2,1)}), bf16[1024,4096]{1,0:T(8,128)(2,1)}) %all-gather.10.cloned.1.call-update) | async-done | bytes 8388624 | tf_op jit(solution)/shard_map/all_gather | solution.py:222
  222.2 11.8 %fusion.194 = f32[512,4096]{1,0:T(8,128)} fusion(bf16[1024,4096]{1,0:T(8,128)(2,1)} %all-gather.10.cloned.1.call-done, f32[512,1024]{1,0:T(8,128)} %get-tuple-element.206, f32[1024]{0:T(1024)S(1)} %bitcast.488, f32[512]{0:T(512)S(1)} %fusion.178), kind=kOutput, calls=%fused_computation.380 | convolution fusion | flops 4296540160 | bytes 18880512 | tf_op jit(solution)/shard_map/dot_general | solution.py:318
  234.0 39.0 %all-gather.12.cloned.1.call-done = bf16[2048,1024]{1,0:T(8,128)(2,1)} async-done(((bf16[128,1024]{1,0:T(8,128)(2,1)}), bf16[2048,1024]{1,0:T(8,128)(2,1)}) %all-gather.12.cloned.1.call-update) | async-done | bytes 4194320 | tf_op jit(solution)/shard_map/all_gather | solution.py:223
  273.0 11.3 %bitcast_multiply_fusion.2 = (f32[512,2048]{1,0:T(8,128)S(1)}, f32[512,2048]{1,0:T(8,128)}, bf16[512,2048]{1,0:T(8,128)(2,1)}) fusion(f32[512,4096]{1,0:T(8,128)} %fusion.194, bf16[2048,1024]{1,0:T(8,128)(2,1)} %all-gather.12.cloned.1.call-done, bf16[1,512,1024]{2,1,0:T(8,128)(2,1)} %param.13), kind=kOutput, calls=%fused_computation.46 | convolution fusion | flops 2162163712 | bytes 24117248 | tf_op jit(solution)/shard_map/dot_general | solution.py:62
  284.4 2.9 add_convert_fusion
  289.3 7.2 %convolution_convert_fusion.1 = bf16[1024,4096]{1,0:T(8,128)(2,1)} fusion(bf16[512,4096]{1,0:T(8,128)(2,1)S(1)} %add_convert_fusion, f32[512,1024]{1,0:T(8,128)S(1)} %copy-done.23, f32[1024]{0:T(1024)S(1)} %bitcast.489, f32[512]{0:T(512)S(1)} %fusion.178), kind=kOutput, calls=%fused_computation.18 | convolution fusion | flops 4300734464 | bytes 14686208 | tf_op jit(solution)/shard_map/dot_general | solution.py:68
  296.5 6.3 convolution_convert_fusion.4
  302.9 11.1 %multiply_reduce_fusion.12 = (f32[1024]{0:T(1024)}, f32[512]{0:T(512)S(1)}, f32[512,1024]{1,0:T(8,128)S(1)}) fusion(f32[512,1024]{1,0:T(8,128)} %get-tuple-element.206, f32[512]{0:T(512)S(1)} %fusion.178, f32[1024]{0:T(1024)S(1)} %bitcast.490, bf16[512,4096]{1,0:T(8,128)(2,1)} %copy-done.29, bf16[1024,4096]{1,0:T(8,128)(2,1)} %all-gather.10.cloned.1.call-done), kind=kOutput, calls=%fused_computation.134 | convolution fusion | flops 4298111488 | bytes 16789504 | tf_op jit(solution)/shard_map/dot_general | solution.py:62
  316.8 4.3 convolution_convert_fusion.3
  321.1 8.7 %pad_maximum_fusion = bf16[2048,2048]{1,0:T(8,128)(2,1)} fusion(bf16[2048,1024]{1,0:T(8,128)(2,1)} %convolution_convert_fusion.3, bf16[2048,1024]{1,0:T(8,128)(2,1)} %convolution_convert_fusion.4), kind=kLoop, calls=%fused_computation.12 | loop fusion | flops 16777216 | bytes 16777216 | tf_op jit(solution)/shard_map/concatenate | solution.py:336
  329.8 4.9 fusion.215
  338.4 4.6 multiply_reduce_fusion.6
  344.6 3.6 reshape.1228
  348.2 6.5 multiply_reduce_fusion.8
  358.1 13.5 %fusion.1 = (f32[2,4,512]{2,1,0:T(4,128)S(1)}, f32[2,1024,512,4]{2,1,3,0:T(8,128)}) fusion(f32[2,4,512,1024]{2,3,1,0:T(8,128)} %get-tuple-element.204, f32[2,4,512]{2,1,0:T(4,128)S(1)} %copy-done.112, bf16[1024,2,64,1]{0,2,3,1:T(8,128)(2,1)S(1)} %bitcast.482, bf16[512,2,4,64]{0,3,2,1:T(8,128)(2,1)} %bitcast.477), kind=kOutput, calls=%fused_computation.3 | convolution fusion | flops 549449728 | bytes 34373632 | tf_op jit(solution)/shard_map/tkgd,ckd->kgtc/dot_general | solution.py:346
  375.1 7.8 %fusion.3 = bf16[2,4,512,1024]{2,3,1,0:T(8,128)(2,1)S(1)} fusion(f32[2,1024,512,4]{2,1,3,0:T(8,128)} %get-tuple-element.210, f32[2,4,512]{2,1,0:T(4,128)S(1)} %get-tuple-element.209, f32[2,4,512,1024]{2,3,1,0:T(8,128)S(1)} %bitcast.444, f32[2,4,512]{2,1,0:T(4,128)S(1)} %copy-done.112), kind=kLoop, calls=%fused_computation.5 | loop fusion | flops 16777216 | bytes 41975808 | tf_op jit(solution)/shard_map/convert_element_type | solution.py:350
  383.0 4.8 fusion.100
  388.9 9.4 %fusion.97 = bf16[2,64,1024]{2,1,0:T(8,128)(2,1)} fusion(bf16[512,2,4,64]{0,3,2,1:T(8,128)(2,1)} %bitcast.478, f32[2,4,512,1024]{2,3,1,0:T(8,128)} %get-tuple-element.204, f32[2,4,512]{2,1,0:T(4,128)S(1)} %copy-done.112), kind=kOutput, calls=%fused_computation.170 | convolution fusion | flops 545390592 | bytes 17580032 | tf_op jit(solution)/shard_map/kgtc,tkgd->ckd/dot_general | solution.py:359
  400.1 8.0 %fusion.29 = (f32[4,24,128]{2,1,0:T(8,128)}, f32[4,24,128]{2,1,0:T(8,128)}, f32[4,24,128]{2,1,0:T(8,128)}, bf16[4,128,128]{2,1,0:T(8,128)(2,1)}) fusion(f32[4,24,128]{2,1,0:T(8,128)} %copy.292, f32[4,128,128]{2,1,0:T(8,128)} %copy-done.59, f32[4,24,128]{2,1,0:T(8,128)S(1)} %copy-done.43, pred[4,128,128]{2,1,0:T(8,128)(4,1)} %compare_and_fusion.1, ...), kind=kOutput, calls=%fused_computation.63 | convolution fusion | flops 221671424 | bytes 3850240 | tf_op jit(solution)/shard_map/transpose(jvp(schtr,scrhd->scthd))/dot_general | solution.py:173
  409.8 3.2 collective-permute-start.7
  414.3 5.1 fusion.107
  419.4 6.7 %fusion.89 = bf16[2,64,4,512]{3,1,2,0:T(8,128)(2,1)} fusion(bf16[1024,2,64,1]{0,2,3,1:T(8,128)(2,1)S(1)} %bitcast.476, bf16[2,4,512,1024]{2,3,1,0:T(8,128)(2,1)} %copy-done.6), kind=kOutput, calls=%fused_computation.165 | convolution fusion | flops 537395200 | bytes 9175040 | tf_op jit(solution)/shard_map/kgtc,ckd->tkgd/dot_general | solution.py:352
  430.7 4.7 fusion.39
  435.5 3.9 fusion.11
  439.4 3.6 copy.314
  442.9 3.5 copy.319
  446.5 2.9 reduce_sum.344
  457.2 3.7 multiply_reduce_fusion.17
  464.7 6.0 multiply_add_fusion.1
  470.7 3.6 copy.318
  474.3 2.5 reduce_sum.342
  481.9 2.5 multiply_reduce_fusion.18
  486.1 3.2 fusion.110
  491.9 5.1 multiply_reduce_fusion.5
  502.0 2.6 collective-permute-done.9
  506.1 8.0 %concatenate.59 = bf16[512,4224]{1,0:T(8,128)(2,1)} concatenate(bf16[512,512]{1,0:T(8,128)(2,1)} %copy.317, bf16[512,256]{1,0:T(8,128)(2,1)S(1)} %copy-done.46, bf16[512,1536]{1,0:T(8,128)(2,1)} %fusion.39, bf16[512,1792]{1,0:T(8,128)(2,1)} %fusion.72, bf16[512,24]{1,0:T(8,128)(2,1)S(1)} %get-tuple-element.136, bf16[512,104]{1,0:T(8,128)(2,1)S(1)} %broadcast_in_dim.194), dimensions={1} | concatenate | bytes 8650752 | tf_op jit(solution)/shard_map/concatenate | solution.py:387
  514.1 9.5 %convolution_convert_fusion = bf16[1024,4224]{1,0:T(8,128)(2,1)} fusion(bf16[512,4224]{1,0:T(8,128)(2,1)} %concatenate.59, bf16[1,512,1024]{2,1,0:T(8,128)(2,1)S(1)} %copy-done.31, f32[1024]{0:T(1024)S(1)} %bitcast.507, f32[512]{0:T(512)S(1)} %copy-done.117), kind=kOutput, calls=%fused_computation.9 | convolution fusion | flops 4435607552 | bytes 14030848 | tf_op jit(solution)/shard_map/dot_general | solution.py:68
  525.4 6.6 %fusion.88 = bf16[1,512,1024]{2,1,0:T(8,128)(2,1)} fusion(f32[512,1024]{1,0:T(8,128)S(1)} %copy-done.25, bf16[512,2048]{1,0:T(8,128)(2,1)} %get-tuple-element.154, bf16[2048,1024]{1,0:T(8,128)(2,1)} %all-gather.12.cloned.1.call-done), kind=kOutput, calls=%fused_computation.163 | convolution fusion | flops 2148532224 | bytes 9437184 | tf_op jit(solution)/shard_map/dot_general | solution.py:321
  534.0 10.5 %fusion.62 = (f32[1024]{0:T(1024)S(1)}, f32[512]{0:T(512)S(1)}, f32[512,1024]{1,0:T(8,128)}) fusion(bf16[1,512,1024]{2,1,0:T(8,128)(2,1)S(1)} %copy-done.31, f32[512]{0:T(512)S(1)} %copy-done.118, f32[1024]{0:T(1024)S(1)} %bitcast.508, f32[512,1024]{1,0:T(8,128)S(1)} %fusion.216, bf16[1024,4096]{1,0:T(8,128)(2,1)} %all-gather.6.cloned.1.call-done, ...), kind=kOutput, calls=%fused_computation.127 | convolution fusion | flops 4315937280 | bytes 17838080 | tf_op jit(solution)/shard_map/dot_general | solution.py:62
  544.6 45.2 %all-reduce.31 = (f32[2,1024]{1,0:T(2,128)}, f32[5,1792]{1,0:T(8,128)}, f32[1536]{0:T(1024)}, f32[3,24]{1,0:T(4,128)}) all-reduce(f32[2,1024]{1,0:T(2,128)S(1)} %pad_maximum_fusion.7, f32[5,1792]{1,0:T(8,128)S(1)} %copy-done.64, f32[1536]{0:T(1024)S(1)} %copy-done.94, ...), channel_id=1, replica_groups=mesh['fsdp'=16,'seq'=2] {'fsdp','seq'}, use_global_device_ids=true, to_apply=%region_29.30 | all-reduce | flops 12616 | bytes 100928 | tf_op jit(solution)/shard_map/psum | solution.py:410
  589.8 4.9 fusion.65
  595.8 2.4 collective-permute-start.12
  599.5 5.9 collective-permute-done.12
  606.3 24.2 %reduce-scatter.4.cloned.1.call-done = bf16[64,4224]{1,0:T(8,128)(2,1)} async-done(((bf16[1024,4224]{1,0:T(8,128)(2,1)}), bf16[64,4224]{1,0:T(8,128)(2,1)}) %reduce-scatter.4.cloned.1.call-update) | async-done | bytes 540688 | tf_op jit(solution)/shard_map/reduce_scatter | solution.py:50
  634.9 6.1 collective-permute-done.10
  (451 shorter events, 126.1 us)
Async XLA Ops:
  7.2 16.6 %copy-start.61 = (bf16[64,2048]{1,0:T(8,128)(2,1)S(1)}, bf16[64,2048]{1,0:T(8,128)(2,1)}, u32[]{:S(2)}) copy-start(bf16[64,2048]{1,0:T(8,128)(2,1)} %param.18) | copy-start | bytes 786436
  7.2 25.7 %copy-start.125 = (bf16[64,24]{0,1:T(8,128)(2,1)S(1)}, bf16[64,24]{0,1:T(8,128)(2,1)}, u32[]{:S(2)}) copy-start(bf16[64,24]{0,1:T(8,128)(2,1)} %param.16) | copy-start | bytes 9220
  7.2 48.0 %copy-start.30 = (bf16[1,512,1024]{2,1,0:T(8,128)(2,1)S(1)}, bf16[1,512,1024]{2,1,0:T(8,128)(2,1)}, u32[]{:S(2)}) copy-start(bf16[1,512,1024]{2,1,0:T(8,128)(2,1)} %param.12) | copy-start | bytes 3145732
  7.2 87.4 %all-gather.6.cloned.1.call-start = ((), (), s32[]{:S(2)}) async-start(), calls=%async_computation.3 | async-start | bytes 8912896 | tf_op jit(solution)/shard_map/all_gather | solution.py:219
  7.3 9.6 %collective-permute-start = (bf16[64,2048]{1,0:T(8,128)(2,1)}, bf16[64,2048]{1,0:T(8,128)(2,1)S(1)}, u32[]{:S(2)}, u32[]{:S(2)}) collective-permute-start(bf16[64,2048]{1,0:T(8,128)(2,1)} %param.15), channel_id=1, source_target_pairs={{0,1},{1,0},{2,3},{3,2},{4,5},{5,4},{6,7},{7,6},{8,9},{9,8},{10,11... | collective-permute-start | bytes 786440 | tf_op jit(solution)/shard_map/ppermute | solution.py:82
  10.3 45.2 %copy-start.136 = (f32[3,24]{1,0:T(4,128)S(1)}, f32[3,24]{1,0:T(4,128)}, u32[]{:S(2)}) copy-start(f32[3,24]{1,0:T(4,128)} %param.23) | copy-start | bytes 868
  10.3 45.7 %copy-start.120 = (f32[2,1024]{1,0:T(2,128)S(1)}, f32[2,1024]{1,0:T(2,128)}, u32[]{:S(2)}) copy-start(f32[2,1024]{1,0:T(2,128)} %param.20) | copy-start | bytes 24580
  17.7 165.6 %all-gather.8.cloned.1.call-start = ((), (), s32[]{:S(2)}) async-start(), calls=%async_computation.4 | async-start | bytes 4456448 | tf_op jit(solution)/shard_map/all_gather | solution.py:221
  17.7 5.2 collective-permute-start.4
  23.7 198.5 %all-gather.10.cloned.1.call-start = ((), (), s32[]{:S(2)}) async-start(), calls=%async_computation.5 | async-start | bytes 8912896 | tf_op jit(solution)/shard_map/all_gather | solution.py:222
  23.8 6.4 collective-permute-start.5
  25.6 32.5 %copy-start.78 = (s32[1,512]{1,0:T(1,128)S(1)}, s32[1,512]{1,0:T(1,128)}, u32[]{:S(2)}) copy-start(s32[1,512]{1,0:T(1,128)} %param.14) | copy-start | bytes 6148
  31.0 242.0 %all-gather.12.cloned.1.call-start = ((), (), s32[]{:S(2)}) async-start(), calls=%async_computation.6 | async-start | bytes 4456448 | tf_op jit(solution)/shard_map/all_gather | solution.py:223
  31.1 44.4 %collective-permute-start.6 = (bf16[128,512]{1,0:T(8,128)(2,1)}, bf16[128,512]{1,0:T(8,128)(2,1)}, u32[]{:S(2)}, u32[]{:S(2)}) collective-permute-start(bf16[128,512]{1,0:T(8,128)(2,1)} %param.19), channel_id=1, source_target_pairs={{0,1},{1,0},{2,3},{3,2},{4,5},{5,4},{6,7},{7,6},{8,9},{9,8},{10,11... | collective-permute-start | bytes 393224 | tf_op jit(solution)/shard_map/ppermute | solution.py:82
  55.2 10.9 %copy-start.65 = (bf16[1024,24]{0,1:T(8,128)(2,1)}, bf16[1024,24]{0,1:T(8,128)(2,1)S(1)}, u32[]{:S(2)}) copy-start(bf16[1024,24]{0,1:T(8,128)(2,1)S(1)} %reshape.1247) | copy-start | bytes 147460
  56.0 10.1 %copy-start.126 = (f32[24]{0:T(128)}, f32[24]{0:T(128)S(1)}, u32[]{:S(2)}) copy-start(f32[24]{0:T(128)S(1)} %get-tuple-element.187) | copy-start | bytes 292
  56.1 10.1 %copy-start.115 = (f32[512]{0:T(512)}, f32[512]{0:T(512)S(1)}, u32[]{:S(2)}) copy-start(f32[512]{0:T(512)S(1)} %fusion.176) | copy-start | bytes 6148
  59.0 72.0 %copy-start.42 = (f32[4,24,128]{2,1,0:T(8,128)}, f32[4,24,128]{2,1,0:T(8,128)S(1)}, u32[]{:S(2)}) copy-start(f32[4,24,128]{2,1,0:T(8,128)S(1)} %fusion.132) | copy-start | bytes 147460
  69.0 102.1 %copy-start.76 = (f32[1536]{0:T(1024)}, f32[1536]{0:T(1024)S(1)}, u32[]{:S(2)}) copy-start(f32[1536]{0:T(1024)S(1)} %mul.1028) | copy-start | bytes 18436
  70.9 23.8 %copy-start.110 = (f32[1,1024]{1,0:T(1,128)S(1)}, f32[1,1024]{1,0:T(1,128)}, u32[]{:S(2)}) copy-start(f32[1,1024]{1,0:T(1,128)} %copy-done.109) | copy-start | bytes 12292
  70.9 23.8 %copy-start.116 = (f32[512]{0:T(512)S(1)}, f32[512]{0:T(512)}, u32[]{:S(2)}) copy-start(f32[512]{0:T(512)} %copy-done.115) | copy-start | bytes 6148
  73.3 66.3 %copy-start.7 = (f32[1,4,128,1536]{3,2,1,0:T(8,128)}, f32[1,4,128,1536]{3,2,1,0:T(8,128)S(1)}, u32[]{:S(2)}) copy-start(f32[1,4,128,1536]{3,2,1,0:T(8,128)S(1)} %copy.295) | copy-start | bytes 9437188
  75.4 44.9 %copy-start.68 = (f32[1792]{0:T(1024)}, f32[1792]{0:T(1024)S(1)}, u32[]{:S(2)}) copy-start(f32[1792]{0:T(1024)S(1)} %get-tuple-element.123) | copy-start | bytes 21508
  75.4 44.9 %copy-start.70 = (f32[1792]{0:T(1024)}, f32[1792]{0:T(1024)S(1)}, u32[]{:S(2)}) copy-start(f32[1792]{0:T(1024)S(1)} %get-tuple-element.124) | copy-start | bytes 21508
  75.4 44.9 %copy-start.72 = (f32[1792]{0:T(1024)}, f32[1792]{0:T(1024)S(1)}, u32[]{:S(2)}) copy-start(f32[1792]{0:T(1024)S(1)} %get-tuple-element.125) | copy-start | bytes 21508
  75.5 44.9 %copy-start.74 = (f32[1792]{0:T(1024)}, f32[1792]{0:T(1024)S(1)}, u32[]{:S(2)}) copy-start(f32[1792]{0:T(1024)S(1)} %get-tuple-element.126) | copy-start | bytes 21508
  77.1 517.7 %reduce-scatter.8.cloned.1.call-start = ((), (), s32[]{:S(2)}) async-start(), calls=%async_computation.9 | async-start | bytes 8912896 | tf_op jit(solution)/shard_map/reduce_scatter | solution.py:50
  107.4 39.6 %collective-permute-start.1 = (bf16[512,256]{1,0:T(8,128)(2,1)}, bf16[512,256]{1,0:T(8,128)(2,1)}, u32[]{:S(2)}, u32[]{:S(2)}) collective-permute-start(bf16[512,256]{1,0:T(8,128)(2,1)} %slice.223), channel_id=1, source_target_pairs={{0,1},{1,0},{2,3},{3,2},{4,5},{5,4},{6,7},{7,6},{8,9},{9,8},{10,11... | collective-permute-start | bytes 786440 | tf_op jit(solution)/shard_map/ppermute | solution.py:82
  110.3 8.2 %collective-permute-start.2 = (bf16[1,3,1792]{2,1,0:T(4,128)(2,1)}, bf16[1,3,1792]{2,1,0:T(4,128)(2,1)S(1)}, u32[]{:S(2)}, u32[]{:S(2)}) collective-permute-start(bf16[1,3,1792]{2,1,0:T(4,128)(2,1)} %slice.228), channel_id=1, source_target_pairs={{0,1},{2,3},{4,5},{6,7},{8,9},{10,11},{12,13},{14,15},{16,17},{18,... | collective-permute-start | bytes 32264 | tf_op jit(solution)/shard_map/ppermute | solution.py:28
  143.9 27.2 %collective-permute-start.3 = (bf16[1,24,64,128]{3,2,1,0:T(8,128)(2,1)}, bf16[1,24,64,128]{3,2,1,0:T(8,128)(2,1)S(1)}, u32[]{:S(2)}, u32[]{:S(2)}) collective-permute-start(bf16[1,24,64,128]{3,2,1,0:T(8,128)(2,1)} %get-tuple-element.145), channel_id=1, source_target_pairs={{0,1},{2,3},{4,5},{6,7},{8,9},{10,11},{12,13},{14,15},{16,17},{18,... | collective-permute-start | bytes 1179656 | tf_op jit(solution)/shard_map/ppermute | solution.py:28
  150.6 10.1 %copy-start.47 = (bf16[1024,128]{0,1:T(8,128)(2,1)}, bf16[1024,128]{0,1:T(8,128)(2,1)S(1)}, u32[]{:S(2)}) copy-start(bf16[1024,128]{0,1:T(8,128)(2,1)S(1)} %get-tuple-element.168) | copy-start | bytes 786436
  160.7 10.5 %copy-start.10 = (f32[4,128,1536]{2,1,0:T(8,128)S(1)}, f32[4,128,1536]{2,1,0:T(8,128)}, u32[]{:S(2)}) copy-start(f32[4,128,1536]{2,1,0:T(8,128)} %copy.297) | copy-start | bytes 9437188
  181.5 154.2 %copy-start.2 = (f32[512,1536]{1,0:T(8,128)}, f32[512,1536]{1,0:T(8,128)S(1)}, u32[]{:S(2)}) copy-start(f32[512,1536]{1,0:T(8,128)S(1)} %get-tuple-element.142) | copy-start | bytes 9437188
  183.2 38.9 %copy-start.82 = (f32[1,1024]{1,0:T(1,128)S(1)}, f32[1,1024]{1,0:T(1,128)}, u32[]{:S(2)}) copy-start(f32[1,1024]{1,0:T(1,128)} %get-tuple-element.178) | copy-start | bytes 12292
  190.0 124.0 %copy-start.102 = (f32[512]{0:T(512)}, f32[512]{0:T(512)S(1)}, u32[]{:S(2)}) copy-start(f32[512]{0:T(512)S(1)} %fusion.178) | copy-start | bytes 6148
  302.8 295.5 %reduce-scatter.6.cloned.1.call-start = ((), (), s32[]{:S(2)}) async-start(), calls=%async_computation.8 | async-start | bytes 8912896 | tf_op jit(solution)/shard_map/reduce_scatter | solution.py:50
  302.8 11.1 %copy-start.24 = (f32[512,1024]{1,0:T(8,128)S(1)}, f32[512,1024]{1,0:T(8,128)}, u32[]{:S(2)}) copy-start(f32[512,1024]{1,0:T(8,128)} %get-tuple-element.206) | copy-start | bytes 6291460
  302.9 11.1 %copy-start.32 = (bf16[1,512,1024]{2,1,0:T(8,128)(2,1)S(1)}, bf16[1,512,1024]{2,1,0:T(8,128)(2,1)}, u32[]{:S(2)}) copy-start(bf16[1,512,1024]{2,1,0:T(8,128)(2,1)} %param.13) | copy-start | bytes 3145732
  354.7 101.4 %collective-permute-start.8 = (bf16[1,24,64,128]{3,2,1,0:T(8,128)(2,1)}, bf16[1,24,64,128]{3,2,1,0:T(8,128)(2,1)}, u32[]{:S(2)}, u32[]{:S(2)}) collective-permute-start(bf16[1,24,64,128]{3,2,1,0:T(8,128)(2,1)} %bitcast.91), channel_id=1, source_target_pairs={{1,0},{3,2},{5,4},{7,6},{9,8},{11,10},{13,12},{15,14},{17,16},{19,... | collective-permute-start | bytes 1179656 | tf_op jit(solution)/shard_map/ppermute | solution.py:28
  358.0 13.6 %slice-start = ((s8[16777216]{0:T(1024)(128)(4,1)}), s8[4194304]{0:T(1024)(128)(4,1)S(1)}, s32[]{:S(2)}) async-start(s8[16777216]{0:T(1024)(128)(4,1)} %bitcast.443), calls=%async_computation.10 | async-start | bytes 8388608
  358.0 14.7 %slice-start.1 = ((s8[16777216]{0:T(1024)(128)(4,1)}), s8[4194304]{0:T(1024)(128)(4,1)S(1)}, s32[]{:S(2)}) async-start(s8[16777216]{0:T(1024)(128)(4,1)} %bitcast.443), calls=%async_computation.11 | async-start | bytes 8388608
  358.0 15.9 %slice-start.2 = ((s8[16777216]{0:T(1024)(128)(4,1)}), s8[4194304]{0:T(1024)(128)(4,1)S(1)}, s32[]{:S(2)}) async-start(s8[16777216]{0:T(1024)(128)(4,1)} %bitcast.443), calls=%async_computation.12 | async-start | bytes 8388608
  358.1 17.1 %slice-start.3 = ((s8[16777216]{0:T(1024)(128)(4,1)}), s8[4194304]{0:T(1024)(128)(4,1)S(1)}, s32[]{:S(2)}) async-start(s8[16777216]{0:T(1024)(128)(4,1)} %bitcast.443), calls=%async_computation.13 | async-start | bytes 8388608
  388.9 11.2 %copy-start.43 = (f32[4,24,128]{2,1,0:T(8,128)S(1)}, f32[4,24,128]{2,1,0:T(8,128)}, u32[]{:S(2)}) copy-start(f32[4,24,128]{2,1,0:T(8,128)} %copy-done.42) | copy-start | bytes 147460
  408.2 222.4 %reduce-scatter.4.cloned.1.call-start = ((), (), s32[]{:S(2)}) async-start(), calls=%async_computation.7 | async-start | bytes 9191424 | tf_op jit(solution)/shard_map/reduce_scatter | solution.py:50
  409.8 44.5 %collective-permute-start.7 = (bf16[512,256]{1,0:T(8,128)(2,1)}, bf16[512,256]{1,0:T(8,128)(2,1)}, u32[]{:S(2)}, u32[]{:S(2)}) collective-permute-start(bf16[512,256]{1,0:T(8,128)(2,1)} %fusion.123), channel_id=1, source_target_pairs={{0,1},{1,0},{2,3},{3,2},{4,5},{5,4},{6,7},{7,6},{8,9},{9,8},{10,11... | collective-permute-start | bytes 786440 | tf_op jit(solution)/shard_map/ppermute | solution.py:94
  446.5 10.7 %copy-start.114 = (f32[24]{0:T(128)S(1)}, f32[24]{0:T(128)}, u32[]{:S(2)}) copy-start(f32[24]{0:T(128)} %get-tuple-element.193) | copy-start | bytes 292
  446.5 10.7 %copy-start.122 = (f32[24]{0:T(128)S(1)}, f32[24]{0:T(128)}, u32[]{:S(2)}) copy-start(f32[24]{0:T(128)} %get-tuple-element.190) | copy-start | bytes 292
  446.5 10.7 %copy-start.124 = (f32[24]{0:T(128)S(1)}, f32[24]{0:T(128)}, u32[]{:S(2)}) copy-start(f32[24]{0:T(128)} %get-tuple-element.192) | copy-start | bytes 292
  446.5 10.7 %copy-start.131 = (f32[24]{0:T(128)S(1)}, f32[24]{0:T(128)}, u32[]{:S(2)}) copy-start(f32[24]{0:T(128)} %get-tuple-element.191) | copy-start | bytes 292
  474.3 11.8 %copy-start.9 = (f32[1,4,128,1536]{3,2,1,0:T(8,128)S(1)}, f32[1,4,128,1536]{3,2,1,0:T(8,128)}, u32[]{:S(2)}) copy-start(f32[1,4,128,1536]{3,2,1,0:T(8,128)} %copy-done.7) | copy-start | bytes 9437188
  474.3 11.8 %copy-start.45 = (f32[1,4,128,128]{3,2,1,0:T(8,128)S(1)}, f32[1,4,128,128]{3,2,1,0:T(8,128)}, u32[]{:S(2)}) copy-start(f32[1,4,128,128]{3,2,1,0:T(8,128)} %convolution_bitcast_fusion.2) | copy-start | bytes 786436
  498.6 5.9 collective-permute-start.9
  533.9 10.6 %copy-start.132 = (f32[1024]{0:T(1024)S(1)}, f32[1024]{0:T(1024)}, u32[]{:S(2)}) copy-start(f32[1024]{0:T(1024)} %get-tuple-element.108) | copy-start | bytes 12292
  533.9 10.6 %copy-start.64 = (f32[5,1792]{1,0:T(8,128)S(1)}, f32[5,1792]{1,0:T(8,128)}, u32[]{:S(2)}) copy-start(f32[5,1792]{1,0:T(8,128)} %pad_add_fusion.3) | copy-start | bytes 107524
  534.0 10.6 %copy-start.94 = (f32[1536]{0:T(1024)S(1)}, f32[1536]{0:T(1024)}, u32[]{:S(2)}) copy-start(f32[1536]{0:T(1024)} %get-tuple-element.102) | copy-start | bytes 18436
  534.0 55.8 %copy-start.106 = (f32[512]{0:T(512)S(1)}, f32[512]{0:T(512)}, u32[]{:S(2)}) copy-start(f32[512]{0:T(512)} %copy-done.105) | copy-start | bytes 6148
  534.0 55.8 %copy-start.83 = (f32[1,1024]{1,0:T(1,128)S(1)}, f32[1,1024]{1,0:T(1,128)}, u32[]{:S(2)}) copy-start(f32[1,1024]{1,0:T(1,128)} %get-tuple-element.178) | copy-start | bytes 12292
  534.0 55.8 %copy-start.101 = (f32[512]{0:T(512)S(1)}, f32[512]{0:T(512)}, u32[]{:S(2)}) copy-start(f32[512]{0:T(512)} %copy-done.100) | copy-start | bytes 6148
  534.0 55.8 %copy-start.103 = (f32[512]{0:T(512)S(1)}, f32[512]{0:T(512)}, u32[]{:S(2)}) copy-start(f32[512]{0:T(512)} %copy-done.102) | copy-start | bytes 6148
  594.8 10.7 %copy-start.55 = (bf16[64,4096]{1,0:T(8,128)(2,1)S(1)}, bf16[64,4096]{1,0:T(8,128)(2,1)}, u32[]{:S(2)}) copy-start(bf16[64,4096]{1,0:T(8,128)(2,1)} %reduce-scatter.8.cloned.1.call-done) | copy-start | bytes 1572868
  595.8 9.6 %collective-permute-start.12 = (bf16[64,2048]{1,0:T(8,128)(2,1)S(1)}, bf16[64,2048]{1,0:T(8,128)(2,1)S(1)}, u32[]{:S(2)}, u32[]{:S(2)}) collective-permute-start(bf16[64,2048]{1,0:T(8,128)(2,1)S(1)} %constant_dynamic-slice_fusion), channel_id=1, source_target_pairs={{0,1},{1,0},{2,3},{3,2},{4,5},{5,4},{6,7},{7,6},{8,9},{9,8},{10,11... | collective-permute-start | bytes 786440 | tf_op jit(solution)/shard_map/ppermute | solution.py:94
  599.4 34.5 %collective-permute-start.11 = (bf16[128,1024]{1,0:T(8,128)(2,1)S(1)}, bf16[128,1024]{1,0:T(8,128)(2,1)S(1)}, u32[]{:S(2)}, u32[]{:S(2)}) collective-permute-start(bf16[128,1024]{1,0:T(8,128)(2,1)S(1)} %pad_maximum_fusion.6), channel_id=1, source_target_pairs={{0,1},{1,0},{2,3},{3,2},{4,5},{5,4},{6,7},{7,6},{8,9},{9,8},{10,11... | collective-permute-start | bytes 786440 | tf_op jit(solution)/shard_map/ppermute | solution.py:94
  632.4 8.5 %collective-permute-start.10 = (bf16[64,2176]{1,0:T(8,128)(2,1)S(1)}, bf16[64,2176]{1,0:T(8,128)(2,1)S(1)}, u32[]{:S(2)}, u32[]{:S(2)}) collective-permute-start(bf16[64,2176]{1,0:T(8,128)(2,1)S(1)} %pad_maximum_fusion.4), channel_id=1, source_target_pairs={{0,1},{1,0},{2,3},{3,2},{4,5},{5,4},{6,7},{7,6},{8,9},{9,8},{10,11... | collective-permute-start | bytes 835592 | tf_op jit(solution)/shard_map/ppermute | solution.py:94
  (98 other events, 466.2 us)
Sparse Core Ops, SparseCore 0:
  17.8 76.8 all-gather.5
  97.4 49.1 all-gather.7
  148.8 73.3 all-gather.9
  224.2 48.7 all-gather.11
  302.9 103.0 reduce-scatter.7
  410.0 104.3 reduce-scatter.5
  523.8 106.7 reduce-scatter.3
